TPU v7x, 32 devices: a whole 2x2x4 slice. The times are simulated.
32 devices in a mesh: row: 4 (over x, core), col: 8 (over z, y).
Axes of the slice: x: 2, y: 2, z: 4, core: 2. Of those that a mesh axis runs over, the one named last changes fastest.
Arguments:
- features: bfloat16 [8192, 256], P(('row', 'col')), may hold values from -6 to 6
- node_order: int32 [8192], P(('row', 'col')), may hold values from 0 to 8191, as said below
- tile_vals: bfloat16 [4, 8, 192, 128, 128], P('row', 'col'), may hold values from -0.109375 to 0.109375
- tile_coord: int32 [4, 8, 192], P('row', 'col'), may hold values from 0 to 127
- tile_count: int32 [4, 8], P('row', 'col'), may hold values from 12 to 192, as said below
- weight: bfloat16 [256, 256], replicated, may hold values from -0.375 to 0.375
- cotangent: bfloat16 [8192, 256], P(('row', 'col')), may hold values from -6 to 6
Outputs:
- activations: bfloat16 [8192, 256], P(('row', 'col'))
- weight_grad: float32 [256, 256], replicated
- feature_grad: bfloat16 [8192, 256], P(('row', 'col'))
Inputs may be any that keep to these rules, and one draw needn't show every extreme that they name: `node_order`: each aligned block of 256 entries is a permutation of that block's own indices. `tile_count`: some device holds exactly 192 used slots.
All inputs are finite; a program needn't handle non-finite values.
Results may differ from a plain program's by a relative error of at most 0.015.
Values may be sent and summed in bfloat16 or wider, within the bound.
No kernel may reach another device: no remote copies, remote signals or barrier semaphores. Data moves between devices by JAX's collectives and lax.ppermute only.
A program may use at most 128 MiB of HBM per device.

v0:
```python
import functools

import jax
import jax.numpy as jnp
from jax import lax
from jax.experimental import pallas as pl
from jax.experimental.pallas import tpu as pltpu
from jax.sharding import PartitionSpec as P

CORES = 2
GROUP = 4
UNROLL = 4
LANES = 128
PACK_BITS = 8
PACK = 1 << PACK_BITS
VMEM_BYTES = 16 * 1024 * 1024
LOAD_BYTES = 45 * 1024 * 1024
LOADS = 4
F32 = jnp.float32
BF16 = jnp.bfloat16


def elu_value(pre_act):
    return jnp.where(pre_act > 0, pre_act, jnp.expm1(jnp.minimum(pre_act, 0.0)))


def elu_slope(pre_act):
    return jnp.where(pre_act > 0, 1.0, jnp.exp(jnp.minimum(pre_act, 0.0)))


def permuter(node_order, nodes_here):
    local_pos = node_order % nodes_here
    return (local_pos[:, None] == jnp.arange(nodes_here, dtype=jnp.int32)[None, :]).astype(BF16)


def reorder(onehot, values):
    return jnp.dot(onehot, values, preferred_element_type=F32).astype(BF16)


def restore(onehot, values):
    moved = lax.dot_general(onehot, values, (((0,), (0,)), ((), ())), preferred_element_type=F32)
    return moved.astype(BF16)


def bits_of(size):
    return size.bit_length() - 1


def block_places(coord, here_ref, chips, cols, piece):
    block_cols = chips * CORES * piece
    row_of, col_of = coord >> bits_of(block_cols), coord & (block_cols - 1)
    row_dev, col_dev = col_of >> bits_of(piece), row_of >> bits_of(piece)
    far = ((row_dev >> bits_of(CORES)) - here_ref[cols]) & (chips - 1)
    swap = ((row_dev & (CORES - 1)) - here_ref[cols + 1]) & (CORES - 1)
    ahead = jnp.zeros_like(coord)
    for c in range(cols):
        ahead = jnp.where(col_dev == c, here_ref[c], ahead)
    return swap * chips + far, col_of & (piece - 1), ahead, row_of & (piece - 1)


def exact_dot(left, right, contract):
    return lax.dot_general(
        left.astype(F32).astype(BF16),
        right.astype(F32).astype(BF16),
        (contract, ((), ())),
        preferred_element_type=F32,
    )


def table_width(slot_total, bin_total):
    group_total = slot_total // GROUP + bin_total + 1
    return -(-max(group_total * GROUP, bin_total + 1) // LANES) * LANES


def write_table(out_ref, bins, bin_total, sources, slots, tile_total, empty):
    lanes = slots.shape[1]
    width = out_ref.shape[1]
    bin_rows = -(-bin_total // 8) * 8
    live = slots < tile_total
    of_bin = lax.broadcasted_iota(jnp.int32, (bin_rows, lanes), 0)
    mine = ((of_bin == bins) & live).astype(jnp.int32)
    earlier = lax.broadcasted_iota(jnp.int32, (lanes, lanes), 0) < lax.broadcasted_iota(
        jnp.int32, (lanes, lanes), 1
    )
    before = exact_dot(mine, earlier.astype(jnp.int32), ((1,), (0,)))
    counts = jnp.sum(mine.astype(F32), axis=1, keepdims=True)
    groups = (counts.astype(jnp.int32) + GROUP - 1) >> bits_of(GROUP)
    bin_at = lax.broadcasted_iota(jnp.int32, (bin_rows, width), 0)
    lane_at = lax.broadcasted_iota(jnp.int32, (bin_rows, width), 1)
    firsts = jnp.sum(jnp.where(bin_at < lane_at, groups, 0).astype(F32), axis=0, keepdims=True)
    here = lax.broadcasted_iota(jnp.int32, (bin_rows, bin_rows), 0)
    other = lax.broadcasted_iota(jnp.int32, (bin_rows, bin_rows), 1)
    firsts_of = exact_dot((other < here).astype(jnp.int32), groups, ((1,), (0,))).astype(jnp.int32)
    group_bin = jnp.sum((firsts_of + groups <= lane_at).astype(F32), axis=0, keepdims=True)
    place = jnp.sum(
        mine.astype(F32) * (before + (firsts_of * GROUP).astype(F32)), axis=0, keepdims=True
    ).astype(jnp.int32)
    place = jnp.where(live, place, -1)
    hit = (lax.broadcasted_iota(jnp.int32, (width, lanes), 0) == place).astype(jnp.int32)
    row = lax.broadcasted_iota(jnp.int32, (8, lanes), 0)
    facts = jnp.where(row == 0, slots, jnp.where(row == 1, sources, 1))
    found = exact_dot(facts, hit, ((1,), (1,))).astype(jnp.int32)
    members = jnp.where(found[2:3] > 0, found[0:1] * PACK + found[1:2], empty)
    rows = lax.broadcasted_iota(jnp.int32, (8, width), 0)
    out_ref[...] = jnp.where(
        rows == 0,
        members,
        jnp.where(rows == 1, group_bin.astype(jnp.int32), firsts.astype(jnp.int32)),
    )


def load_kernel(sizes, count_ref, here_ref, coord_ref, tiles_ref, out_ref, ahead_ref, back_ref, sems):
    chips, cols, piece = sizes
    slot_total = tiles_ref.shape[0]
    share = slot_total // LOADS
    copies = [
        pltpu.make_async_copy(
            tiles_ref.at[pl.ds(k * share, share)], out_ref.at[pl.ds(k * share, share)], sems.at[k]
        )
        for k in range(LOADS)
    ]
    for copy in copies:
        copy.start()
    coord = coord_ref[...]
    slots = lax.broadcasted_iota(jnp.int32, coord.shape, 1)
    tile_total = count_ref[0]
    row_place, col_piece, ahead, row_piece = block_places(coord, here_ref, chips, cols, piece)
    block_rows, block_cols = cols * piece, chips * CORES * piece

    order = [k for group in scatter_order(cols) for k in group]
    bins = jnp.zeros_like(coord)
    for place, k in enumerate(order):
        bins = jnp.where(ahead == k, place, bins)
    bins = bins * piece + row_piece
    write_table(
        ahead_ref, bins, block_rows, row_place * piece + col_piece, slots, tile_total, block_cols
    )

    arrivals = arrival_order(cols)
    part_of, block_at = jnp.zeros_like(coord), jnp.zeros_like(coord)
    for part, group in enumerate(arrivals):
        for at, k in enumerate(group):
            part_of = jnp.where(ahead == k, part, part_of)
            block_at = jnp.where(ahead == k, at, block_at)
    bins = part_of * block_cols + row_place * piece + col_piece
    write_table(
        back_ref,
        bins,
        len(arrivals) * block_cols,
        block_at * piece + row_piece,
        slots,
        tile_total,
        max(len(group) for group in arrivals) * piece,
    )
    for copy in copies:
        copy.wait()


def load_tiles(tiles, coord, count, here, sizes):
    chips, cols, piece = sizes
    slot_total = tiles.shape[0]
    lanes = -(-slot_total // LANES) * LANES
    bins_back = len(arrival_order(cols)) * chips * CORES * piece
    coord = jnp.pad(coord, (0, lanes - slot_total))[None, :]
    smem = pl.BlockSpec(memory_space=pltpu.SMEM)
    vmem = pl.BlockSpec(memory_space=pltpu.VMEM)
    return pl.pallas_call(
        functools.partial(load_kernel, sizes),
        out_shape=[
            jax.ShapeDtypeStruct(tiles.shape, tiles.dtype),
            jax.ShapeDtypeStruct((8, table_width(slot_total, cols * piece)), jnp.int32),
            jax.ShapeDtypeStruct((8, table_width(slot_total, bins_back)), jnp.int32),
        ],
        in_specs=[smem, smem, vmem, pl.BlockSpec(memory_space=pl.ANY)],
        out_specs=[vmem] * 3,
        scratch_shapes=[pltpu.SemaphoreType.DMA((LOADS,))],
        compiler_params=pltpu.CompilerParams(vmem_limit_bytes=LOAD_BYTES),
        cost_estimate=pl.CostEstimate(flops=0, bytes_accessed=2 * tiles.size, transcendentals=0),
    )(count, here, coord, tiles)


def part_kernel(spec, table_ref, tiles_ref, *refs):
    transposed, first_bin, bin_count, bin_total, source_count, carried, finish = spec
    source_refs = refs[:source_count]
    out_refs = refs[source_count + carried : -2]
    source, total = refs[-2:]
    slot_total, tile_size, _ = tiles_ref.shape
    group_total = slot_total // GROUP + bin_total + 1
    at = 0
    for ref in source_refs:
        source[at : at + ref.shape[0], :] = ref[...]
        at += ref.shape[0]
    source[at:, :] = jnp.zeros((source.shape[0] - at, source.shape[1]), source.dtype)
    total[...] = refs[source_count][...] if carried else jnp.zeros_like(total)
    begin = table_ref[2, first_bin]
    end = table_ref[2, first_bin + bin_count]
    contract = 0 if transposed else 1

    def step(number, carry):
        products = []
        for member in range(UNROLL):
            group = begin + number * UNROLL + member
            group = jnp.where(group < end, group, group_total - 1)
            left, right = [], []
            for k in range(GROUP):
                packed = table_ref[0, group * GROUP + k]
                left.append(tiles_ref[packed >> PACK_BITS])
                row = pl.multiple_of((packed & (PACK - 1)) * tile_size, tile_size)
                right.append(source[pl.ds(row, tile_size), :])
            product = lax.dot_general(
                jnp.concatenate(left, axis=contract),
                jnp.concatenate(right, axis=0),
                (((contract,), (0,)), ((), ())),
                preferred_element_type=F32,
            )
            products.append((jnp.minimum(table_ref[1, group] - first_bin, bin_count - 1), product))
        for place, product in products:
            rows = pl.ds(pl.multiple_of(place * tile_size, tile_size), tile_size)
            total[rows, :] += product
        return carry

    lax.fori_loop(0, (end - begin + UNROLL - 1) // UNROLL, step, 0)
    if finish:
        at = 0
        for ref in out_refs:
            ref[...] = total[at : at + ref.shape[0], :].astype(ref.dtype)
            at += ref.shape[0]
    else:
        out_refs[0][...] = total[...]


def tile_part(transposed, table, bins, bin_total, tiles, sources, empty, acc=None, pieces=None):
    first_bin, bin_count = bins
    slot_total, tile_size, _ = tiles.shape
    width = sources[0].shape[1]
    rows = bin_count * tile_size
    vmem = pl.BlockSpec(memory_space=pltpu.VMEM)
    if pieces is None:
        out_shape = [jax.ShapeDtypeStruct((rows, width), F32)]
    else:
        out_shape = [jax.ShapeDtypeStruct((pieces, width), BF16)] * (rows // pieces)
    carried = acc is not None
    share = slot_total * bin_count // bin_total
    given = [table, tiles, *sources] + ([] if acc is None else [acc])
    spec = (transposed, first_bin, bin_count, bin_total, len(sources), carried, pieces is not None)
    return pl.pallas_call(
        functools.partial(part_kernel, spec),
        out_shape=out_shape,
        in_specs=[pl.BlockSpec(memory_space=pltpu.SMEM)] + [vmem] * (len(given) - 1),
        out_specs=[vmem] * len(out_shape),
        scratch_shapes=[
            pltpu.VMEM(((empty + 1) * tile_size, width), BF16),
            pltpu.VMEM((rows, width), F32),
        ],
        compiler_params=pltpu.CompilerParams(vmem_limit_bytes=VMEM_BYTES),
        cost_estimate=pl.CostEstimate(
            flops=2 * share * tile_size * tile_size * width,
            bytes_accessed=2 * share * tile_size * tile_size,
            transcendentals=0,
        ),
    )(*given)


def grid_cycle(size):
    ny = 1
    while (2 * ny) ** 2 <= size:
        ny *= 2
    nz = size // ny
    walk = [0]
    for z in range(nz):
        ys = range(1, ny) if z % 2 == 0 else range(ny - 1, 0, -1)
        walk += [z * ny + y for y in ys]
    walk += [z * ny for z in range(nz - 1, 0, -1)]
    return walk


class Grid:
    def __init__(self, rows, cols):
        self.rows, self.cols, self.chips = rows, cols, rows // CORES
        self.walk = grid_cycle(cols)
        self.place_of = [self.walk.index(c) for c in range(cols)]
        self.row, self.col = lax.axis_index("row"), lax.axis_index("col")
        self.x, self.core = self.row // CORES, self.row % CORES
        place = sum(jnp.where(self.col == c, self.place_of[c], 0) for c in range(cols))
        self.ahead_of = [
            jnp.where(self.core == 0, self.place_of[c] - place, place - self.place_of[c]) % cols
            for c in range(cols)
        ]

    def along_walk(self, step):
        pairs = []
        for r in range(self.rows):
            walk = self.walk if r % CORES == 0 else self.walk[::-1]
            for k in range(self.cols):
                pairs.append((r * self.cols + walk[k], r * self.cols + walk[(k + step) % self.cols]))
        return pairs

    def along_x(self, step):
        return [
            (r * self.cols + c, ((r + step * CORES) % self.rows) * self.cols + c)
            for r in range(self.rows)
            for c in range(self.cols)
        ]

    def across(self, row_bit, col_bit):
        return [
            (r * self.cols + c, (r ^ row_bit) * self.cols + (c ^ col_bit))
            for r in range(self.rows)
            for c in range(self.cols)
        ]


def move(value, pairs):
    return lax.ppermute(value, ("row", "col"), pairs)


def after(value, *others):
    return lax.optimization_barrier((value, *others))[0]


def ring_hops(size):
    return (size - 1) // 2


def arrival_order(size):
    hops = ring_hops(size)
    groups = [[0]] + [[size - step, step] for step in range(1, hops + 1)]
    if size % 2 == 0:
        if hops:
            groups[1].append(size // 2)
        else:
            groups.append([size // 2])
    return groups


def ring_gather(own, size, pairs_of, hold):
    yield {0: own}
    ahead = behind = own
    for step, group in enumerate(arrival_order(size)[1:], 1):
        found = {}
        if step == 1:
            opposite = move(own, pairs_of(size // 2)) if size % 2 == 0 else None
        if step <= ring_hops(size):
            behind = move(after(behind, *hold.get(step, [])), pairs_of(1))
            ahead = move(ahead, pairs_of(-1))
            found = {size - step: behind, step: ahead}
        if size // 2 in group and size % 2 == 0:
            found[size // 2] = opposite
        yield found


def scatter_order(size):
    hops = ring_hops(size)
    groups = [[hop, size - hop] for hop in range(hops, 0, -1)] or [[]]
    if size % 2 == 0:
        groups[min(1, len(groups) - 1)].insert(0, size // 2)
    groups[-1].append(0)
    return groups


def ring_scatter(chunks_of, size, pairs_of):
    ahead = behind = opposite = None

    def onward(running, term):
        return term if running is None else (running.astype(F32) + term.astype(F32)).astype(BF16)

    for step, group in enumerate(scatter_order(size)):
        terms = dict(zip(group, chunks_of(step, ahead)))
        hop = ring_hops(size) - step
        if hop > 0:
            ahead = move(onward(ahead, terms[hop]), pairs_of(1))
            behind = move(onward(behind, terms[size - hop]), pairs_of(-1))
        if size // 2 in group and size % 2 == 0:
            opposite = move(terms[size // 2], pairs_of(size // 2))
    total = terms[0].astype(F32)
    for part in (opposite, ahead, behind):
        if part is not None:
            total = total + part.astype(F32)
    return total


def summed_everywhere(part, grid, gate):
    held = after(part.astype(BF16), *gate)
    got = move(held, grid.across(1, 0))
    yield None
    half = held.shape[0] // CORES
    chip = (held.astype(F32) + after(got, *gate).astype(F32)).astype(BF16)
    held = jnp.where(grid.core == 0, chip[:half], chip[half:])
    bits = [(0, 1 << k) for k in reversed(range(bits_of(grid.cols)))]
    bits += [(1 << k, 0) for k in range(1, bits_of(grid.rows))]
    for row_bit, col_bit in bits:
        got = move(held, grid.across(row_bit, col_bit))
        yield None
        held = (held.astype(F32) + after(got, *gate).astype(F32)).astype(BF16)
    got = move(held, grid.across(1, 0))
    yield None
    own_first, own_last = jnp.concatenate([held, got]), jnp.concatenate([got, held])
    yield jnp.where(grid.core == 0, own_first, own_last).astype(F32)


def per_device(features, node_order, tile_vals, tile_coord, tile_count, weight, cotangent):
    nodes_here, feat_width = features.shape
    tile_size = tile_vals.shape[3]
    row_devices = lax.axis_size("row")
    col_devices = lax.axis_size("col")
    piece = nodes_here // tile_size
    block_cols = row_devices * piece
    block_rows = col_devices * piece
    grad_scale = float(nodes_here * row_devices * col_devices) ** (-0.5)
    grid = Grid(row_devices, col_devices)
    chips = grid.chips

    onehot = permuter(node_order, nodes_here)
    placed = reorder(onehot, features)
    here = jnp.stack([*grid.ahead_of, grid.x, grid.core]).astype(jnp.int32)
    tiles, table_out, table_back = load_tiles(
        tile_vals[0, 0], tile_coord[0, 0], tile_count[0], here, (chips, col_devices, piece)
    )

    along_x = {}
    for found in ring_gather(placed, chips, grid.along_x, {}):
        along_x.update(found)
    along_x = [along_x[k] for k in range(chips)]
    other_core = [move(along_x[0], grid.across(1, 0))]
    other_core += [
        move(jnp.where(table_out[0, 0] < 0, 0, block), grid.across(1, 0)) for block in along_x[1:]
    ]
    sources_out = along_x + other_core
    grads_in = reorder(onehot, cotangent)
    order = scatter_order(col_devices)
    edges = [sum(len(group) for group in order[:k]) * piece for k in range(len(order) + 1)]

    def chunks_of(step, arrived):
        table = table_out if step < 2 else after(table_out, earlier[step - 1])
        earlier.append(arrived)
        bins = (edges[step], edges[step + 1] - edges[step])
        return tile_part(
            False, table, bins, block_rows, tiles, sources_out, block_cols, pieces=nodes_here
        )

    earlier = []
    own_rows = ring_scatter(chunks_of, col_devices, grid.along_walk).astype(BF16)

    pre_act = jnp.dot(own_rows, weight, preferred_element_type=F32)
    own_act = elu_value(pre_act).astype(BF16)
    own_grad = (grads_in.astype(F32) * elu_slope(pre_act)).astype(BF16)
    own_agg_grad = lax.dot_general(
        own_grad, weight, (((1,), (1,)), ((), ())), preferred_element_type=F32
    ).astype(BF16)
    activations = restore(onehot, own_act)

    arrivals = arrival_order(col_devices)
    bins_back = len(arrivals) * block_cols
    empty_back = max(len(group) for group in arrivals) * piece
    weight_part = (
        lax.dot_general(own_rows, own_grad, (((0,), (0,)), ((), ())), preferred_element_type=F32)
        * grad_scale
    )
    acc, gate, hold, weight_grad = None, [], {}, None
    weight_steps = summed_everywhere(weight_part, grid, gate)
    weight_grad = next(weight_steps)
    for number, found in enumerate(ring_gather(own_agg_grad, col_devices, grid.along_walk, hold)):
        blocks = [found[k] for k in arrivals[number]]
        if number == len(arrivals) - 1:
            break
        bins = (number * block_cols, block_cols)
        (acc,) = tile_part(True, table_back, bins, bins_back, tiles, blocks, empty_back, acc=acc)
        hold[number + 2] = [acc]
        gate[:] = [found[number]] if number else [acc]
        if number == 1:
            gate.append(activations)
        weight_grad = next(weight_steps, weight_grad)
    gate[:] = blocks
    weight_grad = next(weight_steps, weight_grad)
    bins = ((len(arrivals) - 1) * block_cols, block_cols)
    mine, theirs = tile_part(
        True, table_back, bins, bins_back, tiles, blocks, empty_back, acc=acc, pieces=chips * nodes_here
    )
    got = move(theirs, grid.across(1, 0))
    both = mine.astype(F32) + got.astype(F32)
    sums = [both[k * nodes_here : (k + 1) * nodes_here] for k in range(chips)]
    sums = [sums[0]] + [term.astype(BF16) for term in sums[1:]]
    gate[:] = sums[1:]
    while weight_grad is None:
        weight_grad = next(weight_steps)
    order = scatter_order(chips)
    placed_grad = ring_scatter(
        lambda step, arrived: [sums[k] for k in order[step]], chips, grid.along_x
    ).astype(BF16)
    feature_grad = restore(onehot, placed_grad)
    return (activations, weight_grad, feature_grad)


def solution(mesh):
    in_specs = (
        P(("row", "col"), None),
        P(("row", "col")),
        P("row", "col", None, None, None),
        P("row", "col", None),
        P("row", "col"),
        P(),
        P(("row", "col"), None),
    )
    out_specs = (P(("row", "col"), None), P(), P(("row", "col"), None))
    return jax.shard_map(
        per_device, mesh=mesh, in_specs=in_specs, out_specs=out_specs, check_vma=False
    )
```

profile of v0, /device:TPU:0, one launch (start us, length us, event | category | flops | bytes accessed | tf_op | source)
XLA Modules:
  0.0 74.8 jit_solution(13796052580769190198)
XLA Ops:
  0.6 0.7 and_select_fusion
  1.4 1.1 %convolution_convert_fusion.4.refs_0_ = bf16[256,256]{1,0:T(8,128)(2,1)S(1)} fusion(bf16[256,256]{1,0:T(8,128)(2,1)} %param.7, s32[256]{0:T(256)S(1)} %and_select_fusion), kind=kOutput, calls=%fused_computation.9 | convolution fusion | flops 33685504 | bytes 263168 | tf_op jit(solution)/shard_map/dot_general | solution.py:37
  2.5 3.0 %collective-permute-start = (bf16[256,256]{1,0:T(8,128)(2,1)S(1)}, bf16[256,256]{1,0:T(8,128)(2,1)S(1)}, u32[]{:S(2)}, u32[]{:S(2)}) collective-permute-start(bf16[256,256]{1,0:T(8,128)(2,1)S(1)} %convolution_convert_fusion.4.refs_0_), channel_id=1, source_target_pairs={{0,16},{1,17},{2,18},{3,19},{4,20},{5,21},{6,22},{7,23},{8,24},{9,... | collective-permute-start | bytes 393224 | tf_op jit(solution)/shard_map/ppermute | solution.py:314
  6.2 0.7 pad.4
  6.9 3.4 %shard_map.94 = (bf16[192,128,128]{2,1,0:T(8,128)(2,1)S(1)}, s32[8,384]{1,0:T(8,128)S(1)}, s32[8,384]{1,0:T(8,128)S(1)}) custom-call(s32[1]{0:T(128)} %bitcast.23.count_ref, s32[10]{0:T(128)S(1)} %stack.43.here_ref, s32[1,256]{1,0:T(1,128)S(1)} %bitcast.24, bf16[192,128,128]{2,1,0:T(8,128)(2,1)} %bitcast.25), custom_call_target="tpu_custom_call" | custom-call | bytes 6291456 | tf_op jit(solution)/shard_map/pallas_call | solution.py:167
  10.4 0.5 slice.16
  11.6 0.6 collective-permute-start.2
  12.2 1.0 %collective-permute-done.2.refs_3_ = bf16[256,256]{1,0:T(8,128)(2,1)S(1)} collective-permute-done((bf16[256,256]{1,0:T(8,128)(2,1)S(1)}, bf16[256,256]{1,0:T(8,128)(2,1)S(1)}, u32[]{:S(2)}, u32[]{:S(2)}) %collective-permute-start.2) | collective-permute-done | bytes 131104 | tf_op jit(solution)/shard_map/ppermute | solution.py:314
  13.1 1.2 %shard_map.95 = (bf16[256,256]{1,0:T(8,128)(2,1)S(1)}, bf16[256,256]{1,0:T(8,128)(2,1)S(1)}) custom-call(s32[8,384]{1,0:T(8,128)S(1)} %get-tuple-element.27.table_ref, bf16[192,128,128]{2,1,0:T(8,128)(2,1)S(1)} %get-tuple-element.25.tiles_ref, bf16[256,256]{1,0:T(8,128)(2,1)S(1)} %convolution_convert_fusion.4.refs_0_, ...), custom_call_target="tpu_custom_call" | custom-call | flops 402653184 | bytes 1572864 | tf_op jit(solution)/shard_map/pallas_call | solution.py:246
  14.3 1.6 %collective-permute-start.7 = (bf16[256,256]{1,0:T(8,128)(2,1)S(1)}, bf16[256,256]{1,0:T(8,128)(2,1)S(1)}, u32[]{:S(2)}, u32[]{:S(2)}) collective-permute-start(bf16[256,256]{1,0:T(8,128)(2,1)S(1)} %get-tuple-element.32), channel_id=1, source_target_pairs={{0,2},{1,0},{3,1},{5,3},{7,5},{6,7},{4,6},{2,4},{10,8},{12,10},{14... | collective-permute-start | bytes 393224 | tf_op jit(solution)/shard_map/ppermute | solution.py:314
  16.0 0.4 collective-permute-start.3
  16.4 1.5 %shard_map.97 = (bf16[256,256]{1,0:T(8,128)(2,1)S(1)}, bf16[256,256]{1,0:T(8,128)(2,1)S(1)}, bf16[256,256]{1,0:T(8,128)(2,1)S(1)}) custom-call(s32[8,384]{1,0:T(8,128)S(1)} %get-tuple-element.27.table_ref, bf16[192,128,128]{2,1,0:T(8,128)(2,1)S(1)} %get-tuple-element.25.tiles_ref, bf16[256,256]{1,0:T(8,128)(2,1)S(1)} %convolution_convert_fusion.4.refs_0_, ...), custom_call_target="tpu_custom_call" | custom-call | flops 603979776 | bytes 2359296 | tf_op jit(solution)/shard_map/pallas_call | solution.py:246
  18.0 4.3 %collective-permute-start.4 = (bf16[256,256]{1,0:T(8,128)(2,1)S(1)}, bf16[256,256]{1,0:T(8,128)(2,1)S(1)}, u32[]{:S(2)}, u32[]{:S(2)}) collective-permute-start(bf16[256,256]{1,0:T(8,128)(2,1)S(1)} %get-tuple-element.29), channel_id=1, source_target_pairs={{0,7},{1,6},{3,4},{5,2},{7,0},{6,1},{4,3},{2,5},{10,13},{12,11},{1... | collective-permute-start | bytes 393224 | tf_op jit(solution)/shard_map/ppermute | solution.py:314
  22.3 0.6 collective-permute-start.8
  23.0 1.5 %collective-permute-start.5 = (bf16[256,256]{1,0:T(8,128)(2,1)S(1)}, bf16[256,256]{1,0:T(8,128)(2,1)S(1)}, u32[]{:S(2)}, u32[]{:S(2)}) collective-permute-start(bf16[256,256]{1,0:T(8,128)(2,1)S(1)} %add_convert_fusion.5), channel_id=1, source_target_pairs={{0,1},{1,3},{3,5},{5,7},{7,6},{6,4},{4,2},{2,0},{10,12},{12,14},{1... | collective-permute-start | bytes 393224 | tf_op jit(solution)/shard_map/ppermute | solution.py:314
  24.5 1.5 %shard_map.96 = (bf16[256,256]{1,0:T(8,128)(2,1)S(1)}, bf16[256,256]{1,0:T(8,128)(2,1)S(1)}, bf16[256,256]{1,0:T(8,128)(2,1)S(1)}) custom-call(s32[8,384]{1,0:T(8,128)S(1)} %get-tuple-element.27.table_ref, bf16[192,128,128]{2,1,0:T(8,128)(2,1)S(1)} %get-tuple-element.25.tiles_ref, bf16[256,256]{1,0:T(8,128)(2,1)S(1)} %convolution_convert_fusion.4.refs_0_, ...), custom_call_target="tpu_custom_call" | custom-call | flops 603979776 | bytes 2359296 | tf_op jit(solution)/shard_map/pallas_call | solution.py:246
  26.0 3.8 %collective-permute-done.8 = bf16[256,256]{1,0:T(8,128)(2,1)S(1)} collective-permute-done((bf16[256,256]{1,0:T(8,128)(2,1)S(1)}, bf16[256,256]{1,0:T(8,128)(2,1)S(1)}, u32[]{:S(2)}, u32[]{:S(2)}) %collective-permute-start.8) | collective-permute-done | bytes 131104 | tf_op jit(solution)/shard_map/ppermute | solution.py:314
  29.8 1.6 %collective-permute-start.9 = (bf16[256,256]{1,0:T(8,128)(2,1)S(1)}, bf16[256,256]{1,0:T(8,128)(2,1)S(1)}, u32[]{:S(2)}, u32[]{:S(2)}) collective-permute-start(bf16[256,256]{1,0:T(8,128)(2,1)S(1)} %add_convert_fusion.2), channel_id=1, source_target_pairs={{0,2},{1,0},{3,1},{5,3},{7,5},{6,7},{4,6},{2,4},{10,8},{12,10},{14... | collective-permute-start | bytes 393224 | tf_op jit(solution)/shard_map/ppermute | solution.py:314
  31.5 0.5 collective-permute-start.6
  32.0 4.2 %collective-permute-done.9 = bf16[256,256]{1,0:T(8,128)(2,1)S(1)} collective-permute-done((bf16[256,256]{1,0:T(8,128)(2,1)S(1)}, bf16[256,256]{1,0:T(8,128)(2,1)S(1)}, u32[]{:S(2)}, u32[]{:S(2)}) %collective-permute-start.9) | collective-permute-done | bytes 131104 | tf_op jit(solution)/shard_map/ppermute | solution.py:314
  36.1 0.4 collective-permute-done.6
  36.8 0.2 fusion.3
  37.6 2.1 %collective-permute-start.12 = (bf16[256,256]{1,0:T(8,128)(2,1)S(1)}, bf16[256,256]{1,0:T(8,128)(2,1)S(1)}, u32[]{:S(2)}, u32[]{:S(2)}) collective-permute-start(bf16[256,256]{1,0:T(8,128)(2,1)S(1)} %convolution_convert_fusion.1.refs_0_), channel_id=1, source_target_pairs={{0,2},{1,0},{3,1},{5,3},{7,5},{6,7},{4,6},{2,4},{10,8},{12,10},{14... | collective-permute-start | bytes 393224 | tf_op jit(solution)/shard_map/ppermute | solution.py:314
  39.7 1.3 %shard_map.98.refs_3_ = f32[1024,256]{1,0:T(8,128)S(1)} custom-call(s32[8,384]{1,0:T(8,128)S(1)} %get-tuple-element.35.table_ref, bf16[192,128,128]{2,1,0:T(8,128)(2,1)S(1)} %get-tuple-element.25.tiles_ref, bf16[256,256]{1,0:T(8,128)(2,1)S(1)} %convolution_convert_fusion.1.refs_0_), custom_call_target="tpu_custom_call" | custom-call | flops 402653184 | bytes 1572864 | tf_op jit(solution)/shard_map/pallas_call | solution.py:246
  41.0 1.6 %collective-permute-start.11 = (bf16[128,256]{1,0:T(8,128)(2,1)S(1)}, bf16[128,256]{1,0:T(8,128)(2,1)S(1)}, u32[]{:S(2)}, u32[]{:S(2)}) collective-permute-start(bf16[128,256]{1,0:T(8,128)(2,1)S(1)} %slice_select_fusion), channel_id=1, source_target_pairs={{0,4},{1,5},{2,6},{3,7},{4,0},{5,1},{6,2},{7,3},{8,12},{9,13},{10,... | collective-permute-start | bytes 196616 | tf_op jit(solution)/shard_map/ppermute | solution.py:314
  42.6 1.0 %convolution_convert_fusion.3 = bf16[256,256]{1,0:T(8,128)(2,1)} fusion(f32[256,256]{1,0:T(8,128)S(1)} %fusion.16, s32[256]{0:T(256)S(1)} %and_select_fusion), kind=kOutput, calls=%fused_computation.8 | convolution fusion | flops 33947648 | bytes 394240 | tf_op jit(solution)/shard_map/dot_general | solution.py:41
  43.6 1.7 %collective-permute-start.18 = (bf16[256,256]{1,0:T(8,128)(2,1)S(1)}, bf16[256,256]{1,0:T(8,128)(2,1)S(1)}, u32[]{:S(2)}, u32[]{:S(2)}) collective-permute-start(bf16[256,256]{1,0:T(8,128)(2,1)S(1)} %convolution_convert_fusion.1.refs_0_), channel_id=1, source_target_pairs={{0,7},{1,6},{3,4},{5,2},{7,0},{6,1},{4,3},{2,5},{10,13},{12,11},{1... | collective-permute-start | bytes 393224 | tf_op jit(solution)/shard_map/ppermute | solution.py:314
  45.3 2.7 %collective-permute-start.17 = (bf16[256,256]{1,0:T(8,128)(2,1)S(1)}, bf16[256,256]{1,0:T(8,128)(2,1)S(1)}, u32[]{:S(2)}, u32[]{:S(2)}) collective-permute-start(bf16[256,256]{1,0:T(8,128)(2,1)S(1)} %collective-permute-done.16.refs_0_), channel_id=1, source_target_pairs={{0,1},{1,3},{3,5},{5,7},{7,6},{6,4},{4,2},{2,0},{10,12},{12,14},{1... | collective-permute-start | bytes 393224 | tf_op jit(solution)/shard_map/ppermute | solution.py:314
  47.9 1.6 %collective-permute-done.11 = bf16[128,256]{1,0:T(8,128)(2,1)S(1)} collective-permute-done((bf16[128,256]{1,0:T(8,128)(2,1)S(1)}, bf16[128,256]{1,0:T(8,128)(2,1)S(1)}, u32[]{:S(2)}, u32[]{:S(2)}) %collective-permute-start.11) | collective-permute-done | bytes 65568 | tf_op jit(solution)/shard_map/ppermute | solution.py:314
  49.6 0.2 collective-permute-start.13
  49.8 2.8 %collective-permute-done.18.refs_2_ = bf16[256,256]{1,0:T(8,128)(2,1)S(1)} collective-permute-done((bf16[256,256]{1,0:T(8,128)(2,1)S(1)}, bf16[256,256]{1,0:T(8,128)(2,1)S(1)}, u32[]{:S(2)}, u32[]{:S(2)}) %collective-permute-start.18) | collective-permute-done | bytes 131104 | tf_op jit(solution)/shard_map/ppermute | solution.py:314
  52.7 1.3 %shard_map.99.refs_2_ = f32[1024,256]{1,0:T(8,128)S(1)} custom-call(s32[8,384]{1,0:T(8,128)S(1)} %get-tuple-element.35.table_ref, bf16[192,128,128]{2,1,0:T(8,128)(2,1)S(1)} %get-tuple-element.25.tiles_ref, bf16[256,256]{1,0:T(8,128)(2,1)S(1)} %collective-permute-done.16.refs_0_, bf16[256,256]{1,0:T(8,128)(2,1)S(1)} %collective-permute-done.12.refs_1_, ...), custom_call_target="tpu_custom_call" | custom-call | flops 402653184 | bytes 1572864 | tf_op jit(solution)/shard_map/pallas_call | solution.py:246
  54.0 1.1 %collective-permute-done.13 = bf16[128,256]{1,0:T(8,128)(2,1)S(1)} collective-permute-done((bf16[128,256]{1,0:T(8,128)(2,1)S(1)}, bf16[128,256]{1,0:T(8,128)(2,1)S(1)}, u32[]{:S(2)}, u32[]{:S(2)}) %collective-permute-start.13) | collective-permute-done | bytes 65568 | tf_op jit(solution)/shard_map/ppermute | solution.py:314
  55.0 1.4 %collective-permute-start.19 = (bf16[256,256]{1,0:T(8,128)(2,1)S(1)}, bf16[256,256]{1,0:T(8,128)(2,1)S(1)}, u32[]{:S(2)}, u32[]{:S(2)}) collective-permute-start(bf16[256,256]{1,0:T(8,128)(2,1)S(1)} %collective-permute-done.17.refs_0_), channel_id=1, source_target_pairs={{0,1},{1,3},{3,5},{5,7},{7,6},{6,4},{4,2},{2,0},{10,12},{12,14},{1... | collective-permute-start | bytes 393224 | tf_op jit(solution)/shard_map/ppermute | solution.py:314
  56.5 0.6 collective-permute-start.20
  57.1 1.5 %collective-permute-start.15 = (bf16[128,256]{1,0:T(8,128)(2,1)S(1)}, bf16[128,256]{1,0:T(8,128)(2,1)S(1)}, u32[]{:S(2)}, u32[]{:S(2)}) collective-permute-start(bf16[128,256]{1,0:T(8,128)(2,1)S(1)} %add_convert_fusion.8), channel_id=1, source_target_pairs={{0,1},{1,0},{2,3},{3,2},{4,5},{5,4},{6,7},{7,6},{8,9},{9,8},{10,11... | collective-permute-start | bytes 196616 | tf_op jit(solution)/shard_map/ppermute | solution.py:314
  58.6 1.6 %shard_map.100.refs_2_ = f32[1024,256]{1,0:T(8,128)S(1)} custom-call(s32[8,384]{1,0:T(8,128)S(1)} %get-tuple-element.35.table_ref, bf16[192,128,128]{2,1,0:T(8,128)(2,1)S(1)} %get-tuple-element.25.tiles_ref, bf16[256,256]{1,0:T(8,128)(2,1)S(1)} %collective-permute-done.17.refs_0_, bf16[256,256]{1,0:T(8,128)(2,1)S(1)} %collective-permute-done.14.refs_1_, ...), custom_call_target="tpu_custom_call" | custom-call | flops 402653184 | bytes 1572864 | tf_op jit(solution)/shard_map/pallas_call | solution.py:246
  60.2 0.6 collective-permute-done.19.refs_0_
  60.8 0.7 collective-permute-done.20.refs_1_
  61.5 1.6 %shard_map.101 = (bf16[512,256]{1,0:T(8,128)(2,1)S(1)}, bf16[512,256]{1,0:T(8,128)(2,1)S(1)}) custom-call(s32[8,384]{1,0:T(8,128)S(1)} %get-tuple-element.35.table_ref, bf16[192,128,128]{2,1,0:T(8,128)(2,1)S(1)} %get-tuple-element.25.tiles_ref, bf16[256,256]{1,0:T(8,128)(2,1)S(1)} %collective-permute-done.19.refs_0_, ...), custom_call_target="tpu_custom_call" | custom-call | flops 402653184 | bytes 1572864 | tf_op jit(solution)/shard_map/pallas_call | solution.py:246
  63.2 1.0 %collective-permute-start.21 = (bf16[128,256]{1,0:T(8,128)(2,1)S(1)}, bf16[128,256]{1,0:T(8,128)(2,1)S(1)}, u32[]{:S(2)}, u32[]{:S(2)}) collective-permute-start(bf16[128,256]{1,0:T(8,128)(2,1)S(1)} %add_convert_fusion.7), channel_id=1, source_target_pairs={{0,16},{1,17},{2,18},{3,19},{4,20},{5,21},{6,22},{7,23},{8,24},{9,... | collective-permute-start | bytes 196616 | tf_op jit(solution)/shard_map/ppermute | solution.py:314
  64.3 0.4 collective-permute-done.22
  64.8 3.0 %collective-permute-done.21 = bf16[128,256]{1,0:T(8,128)(2,1)S(1)} collective-permute-done((bf16[128,256]{1,0:T(8,128)(2,1)S(1)}, bf16[128,256]{1,0:T(8,128)(2,1)S(1)}, u32[]{:S(2)}, u32[]{:S(2)}) %collective-permute-start.21) | collective-permute-done | bytes 65568 | tf_op jit(solution)/shard_map/ppermute | solution.py:314
  67.9 0.9 %collective-permute-start.24 = (bf16[256,256]{1,0:T(8,128)(2,1)S(1)}, bf16[256,256]{1,0:T(8,128)(2,1)S(1)}, u32[]{:S(2)}, u32[]{:S(2)}) collective-permute-start(bf16[256,256]{1,0:T(8,128)(2,1)S(1)} %slice.32), channel_id=1, source_target_pairs={{0,16},{1,17},{2,18},{3,19},{4,20},{5,21},{6,22},{7,23},{8,24},{9,... | collective-permute-start | bytes 393224 | tf_op jit(solution)/shard_map/ppermute | solution.py:314
  68.7 0.4 collective-permute-done.23
  69.1 0.7 fusion.8
  69.8 3.9 %collective-permute-done.24 = bf16[256,256]{1,0:T(8,128)(2,1)S(1)} collective-permute-done((bf16[256,256]{1,0:T(8,128)(2,1)S(1)}, bf16[256,256]{1,0:T(8,128)(2,1)S(1)}, u32[]{:S(2)}, u32[]{:S(2)}) %collective-permute-start.24) | collective-permute-done | bytes 131104 | tf_op jit(solution)/shard_map/ppermute | solution.py:314
  73.8 1.0 %convolution_convert_fusion = bf16[256,256]{1,0:T(8,128)(2,1)} fusion(f32[512,256]{1,0:T(8,128)S(1)} %convert_add_fusion, bf16[256,256]{1,0:T(8,128)(2,1)S(1)} %collective-permute-done.24, s32[256]{0:T(256)S(1)} %and_select_fusion), kind=kOutput, calls=%fused_computation.2 | convolution fusion | flops 33882112 | bytes 525312 | tf_op jit(solution)/shard_map/dot_general | solution.py:41
  (40 shorter events, 1.5 us)
Async XLA Ops:
  0.6 36.0 %copy-start = (bf16[256,256]{1,0:T(8,128)(2,1)S(1)}, bf16[256,256]{1,0:T(8,128)(2,1)}, u32[]{:S(2)}) copy-start(bf16[256,256]{1,0:T(8,128)(2,1)} %param.12) | copy-start | bytes 393220
  2.5 9.1 %collective-permute-start = (bf16[256,256]{1,0:T(8,128)(2,1)S(1)}, bf16[256,256]{1,0:T(8,128)(2,1)S(1)}, u32[]{:S(2)}, u32[]{:S(2)}) collective-permute-start(bf16[256,256]{1,0:T(8,128)(2,1)S(1)} %convolution_convert_fusion.4.refs_0_), channel_id=1, source_target_pairs={{0,16},{1,17},{2,18},{3,19},{4,20},{5,21},{6,22},{7,23},{8,24},{9,... | collective-permute-start | bytes 393224 | tf_op jit(solution)/shard_map/ppermute | solution.py:314
  5.5 6.7 %collective-permute-start.1 = (bf16[256,256]{1,0:T(8,128)(2,1)S(1)}, bf16[256,256]{1,0:T(8,128)(2,1)S(1)}, u32[]{:S(2)}, u32[]{:S(2)}) collective-permute-start(bf16[256,256]{1,0:T(8,128)(2,1)S(1)} %convolution_convert_fusion.4.refs_0_), channel_id=1, source_target_pairs={{0,8},{1,9},{2,10},{3,11},{4,12},{5,13},{6,14},{7,15},{8,0},{9,1},... | collective-permute-start | bytes 393224 | tf_op jit(solution)/shard_map/ppermute | solution.py:314
  11.6 1.6 %collective-permute-start.2 = (bf16[256,256]{1,0:T(8,128)(2,1)S(1)}, bf16[256,256]{1,0:T(8,128)(2,1)S(1)}, u32[]{:S(2)}, u32[]{:S(2)}) collective-permute-start(bf16[256,256]{1,0:T(8,128)(2,1)S(1)} %broadcast_select_fusion), channel_id=1, source_target_pairs={{0,8},{1,9},{2,10},{3,11},{4,12},{5,13},{6,14},{7,15},{8,0},{9,1},... | collective-permute-start | bytes 393224 | tf_op jit(solution)/shard_map/ppermute | solution.py:314
  14.3 7.9 %collective-permute-start.7 = (bf16[256,256]{1,0:T(8,128)(2,1)S(1)}, bf16[256,256]{1,0:T(8,128)(2,1)S(1)}, u32[]{:S(2)}, u32[]{:S(2)}) collective-permute-start(bf16[256,256]{1,0:T(8,128)(2,1)S(1)} %get-tuple-element.32), channel_id=1, source_target_pairs={{0,2},{1,0},{3,1},{5,3},{7,5},{6,7},{4,6},{2,4},{10,8},{12,10},{14... | collective-permute-start | bytes 393224 | tf_op jit(solution)/shard_map/ppermute | solution.py:314
  16.0 7.0 %collective-permute-start.3 = (bf16[256,256]{1,0:T(8,128)(2,1)S(1)}, bf16[256,256]{1,0:T(8,128)(2,1)S(1)}, u32[]{:S(2)}, u32[]{:S(2)}) collective-permute-start(bf16[256,256]{1,0:T(8,128)(2,1)S(1)} %get-tuple-element.26), channel_id=1, source_target_pairs={{0,1},{1,3},{3,5},{5,7},{7,6},{6,4},{4,2},{2,0},{10,12},{12,14},{1... | collective-permute-start | bytes 393224 | tf_op jit(solution)/shard_map/ppermute | solution.py:314
  18.0 18.9 %copy-start.1 = (bf16[256,256]{1,0:T(8,128)(2,1)S(1)}, bf16[256,256]{1,0:T(8,128)(2,1)}, u32[]{:S(2)}) copy-start(bf16[256,256]{1,0:T(8,128)(2,1)} %param.13) | copy-start | bytes 393220
  18.0 14.0 %collective-permute-start.4 = (bf16[256,256]{1,0:T(8,128)(2,1)S(1)}, bf16[256,256]{1,0:T(8,128)(2,1)S(1)}, u32[]{:S(2)}, u32[]{:S(2)}) collective-permute-start(bf16[256,256]{1,0:T(8,128)(2,1)S(1)} %get-tuple-element.29), channel_id=1, source_target_pairs={{0,7},{1,6},{3,4},{5,2},{7,0},{6,1},{4,3},{2,5},{10,13},{12,11},{1... | collective-permute-start | bytes 393224 | tf_op jit(solution)/shard_map/ppermute | solution.py:314
  22.3 7.5 %collective-permute-start.8 = (bf16[256,256]{1,0:T(8,128)(2,1)S(1)}, bf16[256,256]{1,0:T(8,128)(2,1)S(1)}, u32[]{:S(2)}, u32[]{:S(2)}) collective-permute-start(bf16[256,256]{1,0:T(8,128)(2,1)S(1)} %add_convert_fusion.3), channel_id=1, source_target_pairs={{0,2},{1,0},{3,1},{5,3},{7,5},{6,7},{4,6},{2,4},{10,8},{12,10},{14... | collective-permute-start | bytes 393224 | tf_op jit(solution)/shard_map/ppermute | solution.py:314
  23.0 8.5 %collective-permute-start.5 = (bf16[256,256]{1,0:T(8,128)(2,1)S(1)}, bf16[256,256]{1,0:T(8,128)(2,1)S(1)}, u32[]{:S(2)}, u32[]{:S(2)}) collective-permute-start(bf16[256,256]{1,0:T(8,128)(2,1)S(1)} %add_convert_fusion.5), channel_id=1, source_target_pairs={{0,1},{1,3},{3,5},{5,7},{7,6},{6,4},{4,2},{2,0},{10,12},{12,14},{1... | collective-permute-start | bytes 393224 | tf_op jit(solution)/shard_map/ppermute | solution.py:314
  29.8 6.3 %collective-permute-start.9 = (bf16[256,256]{1,0:T(8,128)(2,1)S(1)}, bf16[256,256]{1,0:T(8,128)(2,1)S(1)}, u32[]{:S(2)}, u32[]{:S(2)}) collective-permute-start(bf16[256,256]{1,0:T(8,128)(2,1)S(1)} %add_convert_fusion.2), channel_id=1, source_target_pairs={{0,2},{1,0},{3,1},{5,3},{7,5},{6,7},{4,6},{2,4},{10,8},{12,10},{14... | collective-permute-start | bytes 393224 | tf_op jit(solution)/shard_map/ppermute | solution.py:314
  31.5 5.1 %collective-permute-start.6 = (bf16[256,256]{1,0:T(8,128)(2,1)S(1)}, bf16[256,256]{1,0:T(8,128)(2,1)S(1)}, u32[]{:S(2)}, u32[]{:S(2)}) collective-permute-start(bf16[256,256]{1,0:T(8,128)(2,1)S(1)} %add_convert_fusion.4), channel_id=1, source_target_pairs={{0,1},{1,3},{3,5},{5,7},{7,6},{6,4},{4,2},{2,0},{10,12},{12,14},{1... | collective-permute-start | bytes 393224 | tf_op jit(solution)/shard_map/ppermute | solution.py:314
  37.3 3.7 %collective-permute-start.10 = (bf16[256,256]{1,0:T(8,128)(2,1)S(1)}, bf16[256,256]{1,0:T(8,128)(2,1)S(1)}, u32[]{:S(2)}, u32[]{:S(2)}) collective-permute-start(bf16[256,256]{1,0:T(8,128)(2,1)S(1)} %fusion), channel_id=1, source_target_pairs={{0,8},{1,9},{2,10},{3,11},{4,12},{5,13},{6,14},{7,15},{8,0},{9,1},... | collective-permute-start | bytes 393224 | tf_op jit(solution)/shard_map/ppermute | solution.py:314
  37.6 10.3 %collective-permute-start.12 = (bf16[256,256]{1,0:T(8,128)(2,1)S(1)}, bf16[256,256]{1,0:T(8,128)(2,1)S(1)}, u32[]{:S(2)}, u32[]{:S(2)}) collective-permute-start(bf16[256,256]{1,0:T(8,128)(2,1)S(1)} %convolution_convert_fusion.1.refs_0_), channel_id=1, source_target_pairs={{0,2},{1,0},{3,1},{5,3},{7,5},{6,7},{4,6},{2,4},{10,8},{12,10},{14... | collective-permute-start | bytes 393224 | tf_op jit(solution)/shard_map/ppermute | solution.py:314
  39.7 5.6 %collective-permute-start.16 = (bf16[256,256]{1,0:T(8,128)(2,1)S(1)}, bf16[256,256]{1,0:T(8,128)(2,1)S(1)}, u32[]{:S(2)}, u32[]{:S(2)}) collective-permute-start(bf16[256,256]{1,0:T(8,128)(2,1)S(1)} %convolution_convert_fusion.1.refs_0_), channel_id=1, source_target_pairs={{0,1},{1,3},{3,5},{5,7},{7,6},{6,4},{4,2},{2,0},{10,12},{12,14},{1... | collective-permute-start | bytes 393224 | tf_op jit(solution)/shard_map/ppermute | solution.py:314
  41.0 8.6 %collective-permute-start.11 = (bf16[128,256]{1,0:T(8,128)(2,1)S(1)}, bf16[128,256]{1,0:T(8,128)(2,1)S(1)}, u32[]{:S(2)}, u32[]{:S(2)}) collective-permute-start(bf16[128,256]{1,0:T(8,128)(2,1)S(1)} %slice_select_fusion), channel_id=1, source_target_pairs={{0,4},{1,5},{2,6},{3,7},{4,0},{5,1},{6,2},{7,3},{8,12},{9,13},{10,... | collective-permute-start | bytes 196616 | tf_op jit(solution)/shard_map/ppermute | solution.py:314
  43.6 9.1 %collective-permute-start.18 = (bf16[256,256]{1,0:T(8,128)(2,1)S(1)}, bf16[256,256]{1,0:T(8,128)(2,1)S(1)}, u32[]{:S(2)}, u32[]{:S(2)}) collective-permute-start(bf16[256,256]{1,0:T(8,128)(2,1)S(1)} %convolution_convert_fusion.1.refs_0_), channel_id=1, source_target_pairs={{0,7},{1,6},{3,4},{5,2},{7,0},{6,1},{4,3},{2,5},{10,13},{12,11},{1... | collective-permute-start | bytes 393224 | tf_op jit(solution)/shard_map/ppermute | solution.py:314
  45.3 9.8 %collective-permute-start.17 = (bf16[256,256]{1,0:T(8,128)(2,1)S(1)}, bf16[256,256]{1,0:T(8,128)(2,1)S(1)}, u32[]{:S(2)}, u32[]{:S(2)}) collective-permute-start(bf16[256,256]{1,0:T(8,128)(2,1)S(1)} %collective-permute-done.16.refs_0_), channel_id=1, source_target_pairs={{0,1},{1,3},{3,5},{5,7},{7,6},{6,4},{4,2},{2,0},{10,12},{12,14},{1... | collective-permute-start | bytes 393224 | tf_op jit(solution)/shard_map/ppermute | solution.py:314
  47.9 7.1 %collective-permute-start.14 = (bf16[256,256]{1,0:T(8,128)(2,1)S(1)}, bf16[256,256]{1,0:T(8,128)(2,1)S(1)}, u32[]{:S(2)}, u32[]{:S(2)}) collective-permute-start(bf16[256,256]{1,0:T(8,128)(2,1)S(1)} %collective-permute-done.12.refs_1_), channel_id=1, source_target_pairs={{0,2},{1,0},{3,1},{5,3},{7,5},{6,7},{4,6},{2,4},{10,8},{12,10},{14... | collective-permute-start | bytes 393224 | tf_op jit(solution)/shard_map/ppermute | solution.py:314
  49.6 5.4 %collective-permute-start.13 = (bf16[128,256]{1,0:T(8,128)(2,1)S(1)}, bf16[128,256]{1,0:T(8,128)(2,1)S(1)}, u32[]{:S(2)}, u32[]{:S(2)}) collective-permute-start(bf16[128,256]{1,0:T(8,128)(2,1)S(1)} %add_convert_fusion.9), channel_id=1, source_target_pairs={{0,2},{1,3},{2,0},{3,1},{4,6},{5,7},{6,4},{7,5},{8,10},{9,11},{10,... | collective-permute-start | bytes 196616 | tf_op jit(solution)/shard_map/ppermute | solution.py:314
  55.0 5.7 %collective-permute-start.19 = (bf16[256,256]{1,0:T(8,128)(2,1)S(1)}, bf16[256,256]{1,0:T(8,128)(2,1)S(1)}, u32[]{:S(2)}, u32[]{:S(2)}) collective-permute-start(bf16[256,256]{1,0:T(8,128)(2,1)S(1)} %collective-permute-done.17.refs_0_), channel_id=1, source_target_pairs={{0,1},{1,3},{3,5},{5,7},{7,6},{6,4},{4,2},{2,0},{10,12},{12,14},{1... | collective-permute-start | bytes 393224 | tf_op jit(solution)/shard_map/ppermute | solution.py:314
  56.5 5.0 %collective-permute-start.20 = (bf16[256,256]{1,0:T(8,128)(2,1)S(1)}, bf16[256,256]{1,0:T(8,128)(2,1)S(1)}, u32[]{:S(2)}, u32[]{:S(2)}) collective-permute-start(bf16[256,256]{1,0:T(8,128)(2,1)S(1)} %collective-permute-done.14.refs_1_), channel_id=1, source_target_pairs={{0,2},{1,0},{3,1},{5,3},{7,5},{6,7},{4,6},{2,4},{10,8},{12,10},{14... | collective-permute-start | bytes 393224 | tf_op jit(solution)/shard_map/ppermute | solution.py:314
  57.1 6.1 %collective-permute-start.15 = (bf16[128,256]{1,0:T(8,128)(2,1)S(1)}, bf16[128,256]{1,0:T(8,128)(2,1)S(1)}, u32[]{:S(2)}, u32[]{:S(2)}) collective-permute-start(bf16[128,256]{1,0:T(8,128)(2,1)S(1)} %add_convert_fusion.8), channel_id=1, source_target_pairs={{0,1},{1,0},{2,3},{3,2},{4,5},{5,4},{6,7},{7,6},{8,9},{9,8},{10,11... | collective-permute-start | bytes 196616 | tf_op jit(solution)/shard_map/ppermute | solution.py:314
  63.1 1.6 %collective-permute-start.22 = (bf16[512,256]{1,0:T(8,128)(2,1)S(1)}, bf16[512,256]{1,0:T(8,128)(2,1)S(1)}, u32[]{:S(2)}, u32[]{:S(2)}) collective-permute-start(bf16[512,256]{1,0:T(8,128)(2,1)S(1)} %get-tuple-element.43), channel_id=1, source_target_pairs={{0,8},{1,9},{2,10},{3,11},{4,12},{5,13},{6,14},{7,15},{8,0},{9,1},... | collective-permute-start | bytes 786440 | tf_op jit(solution)/shard_map/ppermute | solution.py:314
  63.2 4.5 %collective-permute-start.21 = (bf16[128,256]{1,0:T(8,128)(2,1)S(1)}, bf16[128,256]{1,0:T(8,128)(2,1)S(1)}, u32[]{:S(2)}, u32[]{:S(2)}) collective-permute-start(bf16[128,256]{1,0:T(8,128)(2,1)S(1)} %add_convert_fusion.7), channel_id=1, source_target_pairs={{0,16},{1,17},{2,18},{3,19},{4,20},{5,21},{6,22},{7,23},{8,24},{9,... | collective-permute-start | bytes 196616 | tf_op jit(solution)/shard_map/ppermute | solution.py:314
  67.8 1.3 %collective-permute-start.23 = (bf16[128,256]{1,0:T(8,128)(2,1)S(1)}, bf16[128,256]{1,0:T(8,128)(2,1)S(1)}, u32[]{:S(2)}, u32[]{:S(2)}) collective-permute-start(bf16[128,256]{1,0:T(8,128)(2,1)S(1)} %add_convert_fusion.6), channel_id=1, source_target_pairs={{0,8},{1,9},{2,10},{3,11},{4,12},{5,13},{6,14},{7,15},{8,0},{9,1},... | collective-permute-start | bytes 196616 | tf_op jit(solution)/shard_map/ppermute | solution.py:314
  67.9 5.9 %collective-permute-start.24 = (bf16[256,256]{1,0:T(8,128)(2,1)S(1)}, bf16[256,256]{1,0:T(8,128)(2,1)S(1)}, u32[]{:S(2)}, u32[]{:S(2)}) collective-permute-start(bf16[256,256]{1,0:T(8,128)(2,1)S(1)} %slice.32), channel_id=1, source_target_pairs={{0,16},{1,17},{2,18},{3,19},{4,20},{5,21},{6,22},{7,23},{8,24},{9,... | collective-permute-start | bytes 393224 | tf_op jit(solution)/shard_map/ppermute | solution.py:314
where the time goes:
time: 74.7 us; the launch traced here: 74.8 us
  starting transfers between devices  28.1 us (38%)
  waiting for transfers between devices  23.9 us (32%)
  Pallas kernels  13.4 us (18%)
  matrix products  3.97 us (5%)
  between operations  2.2 us (3%)
  other arithmetic  1.87 us (3%)
  local copies, waits for them, and re-layouts  1.31 us (2%)
    ppermute x25, starting transfers between devices, move(): return lax.ppermute(value, ('row', 'col'), pairs)  28.1 us
    ppermute x25, waiting for transfers between devices, move(): return lax.ppermute(value, ('row', 'col'), pairs)  23.9 us
    pallas_call x7, Pallas kernels, tile_part(): pl.pallas_call(functools.partial(part_kernel, spec), out_shape=out_shape,...  9.99 us
    pallas_call x1, Pallas kernels, load_tiles(): pl.pallas_call(functools.partial(load_kernel, sizes), out_shape=[jax.Shap...  3.44 us
    dot_general x2, matrix products, restore(): lax.dot_general(onehot, values, (((0,), (0,)), ((), ())), preferred_eleme...  1.99 us
  transfers between devices with their start and end apart: 25, of which 13 were waited for; matrix products, arithmetic and copies ran while one was open for 5% of the time, Pallas kernels for 16%

commit v1 on v0

--- a/solution.py
+++ b/solution.py
@@ -28,17 +28,17 @@
     return jnp.where(pre_act > 0, 1.0, jnp.exp(jnp.minimum(pre_act, 0.0)))
 
 
-def permuter(node_order, nodes_here):
-    local_pos = node_order % nodes_here
-    return (local_pos[:, None] == jnp.arange(nodes_here, dtype=jnp.int32)[None, :]).astype(BF16)
-
-
-def reorder(onehot, values):
-    return jnp.dot(onehot, values, preferred_element_type=F32).astype(BF16)
-
-
-def restore(onehot, values):
-    moved = lax.dot_general(onehot, values, (((0,), (0,)), ((), ())), preferred_element_type=F32)
+def row_moves(node_order, first_node, nodes_here):
+    own = first_node + jnp.arange(nodes_here, dtype=jnp.int32)
+    return (node_order[:, None] == own[None, :]).astype(BF16)
+
+
+def reorder(moves, values):
+    return jnp.dot(moves, values, preferred_element_type=F32).astype(BF16)
+
+
+def restore(moves, values):
+    moved = lax.dot_general(moves, values, (((0,), (0,)), ((), ())), preferred_element_type=F32)
     return moved.astype(BF16)
 
 
@@ -109,7 +109,7 @@
     )
 
 
-def load_kernel(sizes, count_ref, here_ref, coord_ref, tiles_ref, out_ref, ahead_ref, back_ref, sems):
+def load_kernel(sizes, here_ref, facts_ref, tiles_ref, out_ref, ahead_ref, back_ref, gate_ref, sems):
     chips, cols, piece = sizes
     slot_total = tiles_ref.shape[0]
     share = slot_total // LOADS
@@ -121,9 +121,10 @@
     ]
     for copy in copies:
         copy.start()
-    coord = coord_ref[...]
+    gate_ref[...] = jnp.zeros_like(gate_ref)
+    coord = facts_ref[0:1, :]
     slots = lax.broadcasted_iota(jnp.int32, coord.shape, 1)
-    tile_total = count_ref[0]
+    tile_total = facts_ref[1:2, 0:1]
     row_place, col_piece, ahead, row_piece = block_places(coord, here_ref, chips, cols, piece)
     block_rows, block_cols = cols * piece, chips * CORES * piece
 
@@ -156,13 +157,12 @@
         copy.wait()
 
 
-def load_tiles(tiles, coord, count, here, sizes):
+def load_tiles(tiles, coord, count, here, sizes, gate_shape):
     chips, cols, piece = sizes
     slot_total = tiles.shape[0]
+    bins_back = len(arrival_order(cols)) * chips * CORES * piece
     lanes = -(-slot_total // LANES) * LANES
-    bins_back = len(arrival_order(cols)) * chips * CORES * piece
-    coord = jnp.pad(coord, (0, lanes - slot_total))[None, :]
-    smem = pl.BlockSpec(memory_space=pltpu.SMEM)
+    facts = jnp.concatenate([jnp.pad(row, ((0, 0), (0, lanes - row.shape[1]))) for row in (coord, count)])
     vmem = pl.BlockSpec(memory_space=pltpu.VMEM)
     return pl.pallas_call(
         functools.partial(load_kernel, sizes),
@@ -170,13 +170,14 @@
             jax.ShapeDtypeStruct(tiles.shape, tiles.dtype),
             jax.ShapeDtypeStruct((8, table_width(slot_total, cols * piece)), jnp.int32),
             jax.ShapeDtypeStruct((8, table_width(slot_total, bins_back)), jnp.int32),
+            jax.ShapeDtypeStruct(gate_shape, BF16),
         ],
-        in_specs=[smem, smem, vmem, pl.BlockSpec(memory_space=pl.ANY)],
-        out_specs=[vmem] * 3,
+        in_specs=[pl.BlockSpec(memory_space=pltpu.SMEM), vmem, pl.BlockSpec(memory_space=pl.ANY)],
+        out_specs=[vmem] * 4,
         scratch_shapes=[pltpu.SemaphoreType.DMA((LOADS,))],
         compiler_params=pltpu.CompilerParams(vmem_limit_bytes=LOAD_BYTES),
         cost_estimate=pl.CostEstimate(flops=0, bytes_accessed=2 * tiles.size, transcendentals=0),
-    )(count, here, coord, tiles)
+    )(here, facts, tiles)
 
 
 def part_kernel(spec, table_ref, tiles_ref, *refs):
@@ -327,7 +328,7 @@
     groups = [[0]] + [[size - step, step] for step in range(1, hops + 1)]
     if size % 2 == 0:
         if hops:
-            groups[1].append(size // 2)
+            groups[min(2, hops)].append(size // 2)
         else:
             groups.append([size // 2])
     return groups
@@ -410,11 +411,12 @@
     grid = Grid(row_devices, col_devices)
     chips = grid.chips
 
-    onehot = permuter(node_order, nodes_here)
-    placed = reorder(onehot, features)
+    first_node = (grid.row * col_devices + grid.col) * nodes_here
+    moves = row_moves(node_order, first_node, nodes_here)
+    placed = reorder(moves, features)
     here = jnp.stack([*grid.ahead_of, grid.x, grid.core]).astype(jnp.int32)
-    tiles, table_out, table_back = load_tiles(
-        tile_vals[0, 0], tile_coord[0, 0], tile_count[0], here, (chips, col_devices, piece)
+    tiles, table_out, table_back, loaded = load_tiles(
+        tile_vals[0, 0], tile_coord[0], tile_count, here, (chips, col_devices, piece), placed.shape
     )
 
     along_x = {}
@@ -423,10 +425,10 @@
     along_x = [along_x[k] for k in range(chips)]
     other_core = [move(along_x[0], grid.across(1, 0))]
     other_core += [
-        move(jnp.where(table_out[0, 0] < 0, 0, block), grid.across(1, 0)) for block in along_x[1:]
+        move(jnp.where(loaded == 0, block, 0), grid.across(1, 0)) for block in along_x[1:]
     ]
     sources_out = along_x + other_core
-    grads_in = reorder(onehot, cotangent)
+    grads_in = reorder(moves, cotangent)
     order = scatter_order(col_devices)
     edges = [sum(len(group) for group in order[:k]) * piece for k in range(len(order) + 1)]
 
@@ -447,8 +449,6 @@
     own_agg_grad = lax.dot_general(
         own_grad, weight, (((1,), (1,)), ((), ())), preferred_element_type=F32
     ).astype(BF16)
-    activations = restore(onehot, own_act)
-
     arrivals = arrival_order(col_devices)
     bins_back = len(arrivals) * block_cols
     empty_back = max(len(group) for group in arrivals) * piece
@@ -467,8 +467,6 @@
         (acc,) = tile_part(True, table_back, bins, bins_back, tiles, blocks, empty_back, acc=acc)
         hold[number + 2] = [acc]
         gate[:] = [found[number]] if number else [acc]
-        if number == 1:
-            gate.append(activations)
         weight_grad = next(weight_steps, weight_grad)
     gate[:] = blocks
     weight_grad = next(weight_steps, weight_grad)
@@ -487,7 +485,8 @@
     placed_grad = ring_scatter(
         lambda step, arrived: [sums[k] for k in order[step]], chips, grid.along_x
     ).astype(BF16)
-    feature_grad = restore(onehot, placed_grad)
+    activations = restore(moves, own_act)
+    feature_grad = restore(moves, placed_grad)
     return (activations, weight_grad, feature_grad)
 
 

time: 74.7 us -> 67.9 us (0.909)
  waiting for transfers between devices: 23.9 us -> 18.8 us
  local copies, waits for them, and re-layouts: 1.31 us -> 0.13 us
    ppermute x25, waiting for transfers between devices: 23.9 us -> 18.8 us  [move(): return lax.ppermute(value, ('row', 'col'), pairs)]
  transfers between devices with their start and end apart: 25 -> 25, of which waited for: 13 -> 12; matrix products, arithmetic and copies ran while one was open for 5% -> 5% of each run, Pallas kernels for 16% -> 18%
where the time goes in v1:
time: 67.9 us; the launch traced here: 67.7 us
  starting transfers between devices  28.2 us (42%)
  waiting for transfers between devices  18.8 us (28%)
  Pallas kernels  13.1 us (19%)
  matrix products  4.02 us (6%)
  other arithmetic  1.85 us (3%)
  between operations  1.64 us (2%)
    ppermute x25, starting transfers between devices, move(): return lax.ppermute(value, ('row', 'col'), pairs)  28.2 us
    ppermute x25, waiting for transfers between devices, move(): return lax.ppermute(value, ('row', 'col'), pairs)  18.8 us
    pallas_call x7, Pallas kernels, tile_part(): pl.pallas_call(functools.partial(part_kernel, spec), out_shape=out_shape,...  9.64 us
    pallas_call x1, Pallas kernels, load_tiles(): pl.pallas_call(functools.partial(load_kernel, sizes), out_shape=[jax.Shap...  3.41 us
    dot_general x2, matrix products, restore(): lax.dot_general(moves, values, (((0,), (0,)), ((), ())), preferred_elemen...  1.99 us
    dot_general x2, matrix products, reorder(): return jnp.dot(moves, values, preferred_element_type=F32).astype(BF16)  1.41 us
  transfers between devices with their start and end apart: 25, of which 12 were waited for; matrix products, arithmetic and copies ran while one was open for 5% of the time, Pallas kernels for 18%

profile of v1, /device:TPU:0, one launch (start us, length us, event | category | flops | bytes accessed | tf_op | source)
XLA Modules:
  0.0 67.7 jit_solution(14176535951904383785)
XLA Ops:
  0.7 1.2 %convolution_convert_fusion.4.refs_0_ = bf16[256,256]{1,0:T(8,128)(2,1)S(1)} fusion(bf16[256,256]{1,0:T(8,128)(2,1)} %param.7, s32[256]{0:T(256)S(1)} %iota_add_fusion, s32[256]{0:T(256)} %param.8), kind=kOutput, calls=%fused_computation.9 | convolution fusion | flops 33685504 | bytes 264192 | tf_op jit(solution)/shard_map/dot_general | solution.py:37
  1.9 3.0 %collective-permute-start = (bf16[256,256]{1,0:T(8,128)(2,1)S(1)}, bf16[256,256]{1,0:T(8,128)(2,1)S(1)}, u32[]{:S(2)}, u32[]{:S(2)}) collective-permute-start(bf16[256,256]{1,0:T(8,128)(2,1)S(1)} %convolution_convert_fusion.4.refs_0_), channel_id=1, source_target_pairs={{0,16},{1,17},{2,18},{3,19},{4,20},{5,21},{6,22},{7,23},{8,24},{9,... | collective-permute-start | bytes 393224 | tf_op jit(solution)/shard_map/ppermute | solution.py:315
  5.6 0.7 %pad_add_fusion.facts_ref = s32[2,256]{1,0:T(2,128)S(1)} fusion(s32[1,1]{1,0:T(1,128)S(6)} %copy.10, s32[1,192]{1,0:T(1,128)} %bitcast.21), kind=kLoop, calls=%fused_computation.44 | loop fusion | flops 512 | bytes 2820 | tf_op jit(solution)/shard_map/concatenate | solution.py:165
  6.3 3.4 %shard_map.94 = (bf16[192,128,128]{2,1,0:T(8,128)(2,1)S(1)}, s32[8,384]{1,0:T(8,128)S(1)}, s32[8,384]{1,0:T(8,128)S(1)}, bf16[256,256]{1,0:T(8,128)(2,1)S(1)}) custom-call(s32[10]{0:T(128)S(1)} %stack.43.here_ref, s32[2,256]{1,0:T(2,128)S(1)} %pad_add_fusion.facts_ref, bf16[192,128,128]{2,1,0:T(8,128)(2,1)} %bitcast.20), custom_call_target="tpu_custom_call" | custom-call | bytes 6291456 | tf_op jit(solution)/shard_map/pallas_call | solution.py:167
  9.8 0.6 collective-permute-start.2
  10.4 1.0 %collective-permute-done.2.refs_3_ = bf16[256,256]{1,0:T(8,128)(2,1)S(1)} collective-permute-done((bf16[256,256]{1,0:T(8,128)(2,1)S(1)}, bf16[256,256]{1,0:T(8,128)(2,1)S(1)}, u32[]{:S(2)}, u32[]{:S(2)}) %collective-permute-start.2) | collective-permute-done | bytes 131104 | tf_op jit(solution)/shard_map/ppermute | solution.py:315
  11.3 1.2 %shard_map.95 = (bf16[256,256]{1,0:T(8,128)(2,1)S(1)}, bf16[256,256]{1,0:T(8,128)(2,1)S(1)}) custom-call(s32[8,384]{1,0:T(8,128)S(1)} %get-tuple-element.29.table_ref, bf16[192,128,128]{2,1,0:T(8,128)(2,1)S(1)} %get-tuple-element.26.tiles_ref, bf16[256,256]{1,0:T(8,128)(2,1)S(1)} %convolution_convert_fusion.4.refs_0_, ...), custom_call_target="tpu_custom_call" | custom-call | flops 402653184 | bytes 1572864 | tf_op jit(solution)/shard_map/pallas_call | solution.py:247
  12.5 2.0 %collective-permute-start.7 = (bf16[256,256]{1,0:T(8,128)(2,1)S(1)}, bf16[256,256]{1,0:T(8,128)(2,1)S(1)}, u32[]{:S(2)}, u32[]{:S(2)}) collective-permute-start(bf16[256,256]{1,0:T(8,128)(2,1)S(1)} %get-tuple-element.34), channel_id=1, source_target_pairs={{0,2},{1,0},{3,1},{5,3},{7,5},{6,7},{4,6},{2,4},{10,8},{12,10},{14... | collective-permute-start | bytes 393224 | tf_op jit(solution)/shard_map/ppermute | solution.py:315
  14.5 0.1 collective-permute-start.3
  14.6 1.5 %shard_map.97 = (bf16[256,256]{1,0:T(8,128)(2,1)S(1)}, bf16[256,256]{1,0:T(8,128)(2,1)S(1)}, bf16[256,256]{1,0:T(8,128)(2,1)S(1)}) custom-call(s32[8,384]{1,0:T(8,128)S(1)} %get-tuple-element.29.table_ref, bf16[192,128,128]{2,1,0:T(8,128)(2,1)S(1)} %get-tuple-element.26.tiles_ref, bf16[256,256]{1,0:T(8,128)(2,1)S(1)} %convolution_convert_fusion.4.refs_0_, ...), custom_call_target="tpu_custom_call" | custom-call | flops 603979776 | bytes 2359296 | tf_op jit(solution)/shard_map/pallas_call | solution.py:247
  16.2 4.3 %collective-permute-start.4 = (bf16[256,256]{1,0:T(8,128)(2,1)S(1)}, bf16[256,256]{1,0:T(8,128)(2,1)S(1)}, u32[]{:S(2)}, u32[]{:S(2)}) collective-permute-start(bf16[256,256]{1,0:T(8,128)(2,1)S(1)} %get-tuple-element.31), channel_id=1, source_target_pairs={{0,7},{1,6},{3,4},{5,2},{7,0},{6,1},{4,3},{2,5},{10,13},{12,11},{1... | collective-permute-start | bytes 393224 | tf_op jit(solution)/shard_map/ppermute | solution.py:315
  20.5 1.0 %collective-permute-start.8 = (bf16[256,256]{1,0:T(8,128)(2,1)S(1)}, bf16[256,256]{1,0:T(8,128)(2,1)S(1)}, u32[]{:S(2)}, u32[]{:S(2)}) collective-permute-start(bf16[256,256]{1,0:T(8,128)(2,1)S(1)} %add_convert_fusion.3), channel_id=1, source_target_pairs={{0,2},{1,0},{3,1},{5,3},{7,5},{6,7},{4,6},{2,4},{10,8},{12,10},{14... | collective-permute-start | bytes 393224 | tf_op jit(solution)/shard_map/ppermute | solution.py:315
  21.5 1.2 %collective-permute-start.5 = (bf16[256,256]{1,0:T(8,128)(2,1)S(1)}, bf16[256,256]{1,0:T(8,128)(2,1)S(1)}, u32[]{:S(2)}, u32[]{:S(2)}) collective-permute-start(bf16[256,256]{1,0:T(8,128)(2,1)S(1)} %add_convert_fusion.5), channel_id=1, source_target_pairs={{0,1},{1,3},{3,5},{5,7},{7,6},{6,4},{4,2},{2,0},{10,12},{12,14},{1... | collective-permute-start | bytes 393224 | tf_op jit(solution)/shard_map/ppermute | solution.py:315
  22.7 1.5 %shard_map.96 = (bf16[256,256]{1,0:T(8,128)(2,1)S(1)}, bf16[256,256]{1,0:T(8,128)(2,1)S(1)}, bf16[256,256]{1,0:T(8,128)(2,1)S(1)}) custom-call(s32[8,384]{1,0:T(8,128)S(1)} %get-tuple-element.29.table_ref, bf16[192,128,128]{2,1,0:T(8,128)(2,1)S(1)} %get-tuple-element.26.tiles_ref, bf16[256,256]{1,0:T(8,128)(2,1)S(1)} %convolution_convert_fusion.4.refs_0_, ...), custom_call_target="tpu_custom_call" | custom-call | flops 603979776 | bytes 2359296 | tf_op jit(solution)/shard_map/pallas_call | solution.py:247
  24.2 3.7 %collective-permute-done.8 = bf16[256,256]{1,0:T(8,128)(2,1)S(1)} collective-permute-done((bf16[256,256]{1,0:T(8,128)(2,1)S(1)}, bf16[256,256]{1,0:T(8,128)(2,1)S(1)}, u32[]{:S(2)}, u32[]{:S(2)}) %collective-permute-start.8) | collective-permute-done | bytes 131104 | tf_op jit(solution)/shard_map/ppermute | solution.py:315
  28.0 1.8 %collective-permute-start.9 = (bf16[256,256]{1,0:T(8,128)(2,1)S(1)}, bf16[256,256]{1,0:T(8,128)(2,1)S(1)}, u32[]{:S(2)}, u32[]{:S(2)}) collective-permute-start(bf16[256,256]{1,0:T(8,128)(2,1)S(1)} %add_convert_fusion.2), channel_id=1, source_target_pairs={{0,2},{1,0},{3,1},{5,3},{7,5},{6,7},{4,6},{2,4},{10,8},{12,10},{14... | collective-permute-start | bytes 393224 | tf_op jit(solution)/shard_map/ppermute | solution.py:315
  29.8 0.3 collective-permute-start.6
  30.2 3.4 %collective-permute-done.9 = bf16[256,256]{1,0:T(8,128)(2,1)S(1)} collective-permute-done((bf16[256,256]{1,0:T(8,128)(2,1)S(1)}, bf16[256,256]{1,0:T(8,128)(2,1)S(1)}, u32[]{:S(2)}, u32[]{:S(2)}) %collective-permute-start.9) | collective-permute-done | bytes 131104 | tf_op jit(solution)/shard_map/ppermute | solution.py:315
  33.6 1.7 %collective-permute-done.6 = bf16[256,256]{1,0:T(8,128)(2,1)S(1)} collective-permute-done((bf16[256,256]{1,0:T(8,128)(2,1)S(1)}, bf16[256,256]{1,0:T(8,128)(2,1)S(1)}, u32[]{:S(2)}, u32[]{:S(2)}) %collective-permute-start.6) | collective-permute-done | bytes 131104 | tf_op jit(solution)/shard_map/ppermute | solution.py:315
  35.4 0.2 fusion.23
  35.6 0.2 fusion.3
  35.9 0.2 fusion
  36.2 0.2 convolution_convert_fusion.1.refs_0_
  36.4 2.1 %collective-permute-start.12 = (bf16[256,256]{1,0:T(8,128)(2,1)S(1)}, bf16[256,256]{1,0:T(8,128)(2,1)S(1)}, u32[]{:S(2)}, u32[]{:S(2)}) collective-permute-start(bf16[256,256]{1,0:T(8,128)(2,1)S(1)} %convolution_convert_fusion.1.refs_0_), channel_id=1, source_target_pairs={{0,2},{1,0},{3,1},{5,3},{7,5},{6,7},{4,6},{2,4},{10,8},{12,10},{14... | collective-permute-start | bytes 393224 | tf_op jit(solution)/shard_map/ppermute | solution.py:315
  38.5 1.3 %shard_map.98.refs_2_ = f32[1024,256]{1,0:T(8,128)S(1)} custom-call(s32[8,384]{1,0:T(8,128)S(1)} %get-tuple-element.37.table_ref, bf16[192,128,128]{2,1,0:T(8,128)(2,1)S(1)} %get-tuple-element.26.tiles_ref, bf16[256,256]{1,0:T(8,128)(2,1)S(1)} %convolution_convert_fusion.1.refs_0_), custom_call_target="tpu_custom_call" | custom-call | flops 402653184 | bytes 1572864 | tf_op jit(solution)/shard_map/pallas_call | solution.py:247
  39.8 1.9 %collective-permute-start.11 = (bf16[128,256]{1,0:T(8,128)(2,1)S(1)}, bf16[128,256]{1,0:T(8,128)(2,1)S(1)}, u32[]{:S(2)}, u32[]{:S(2)}) collective-permute-start(bf16[128,256]{1,0:T(8,128)(2,1)S(1)} %slice_select_fusion), channel_id=1, source_target_pairs={{0,4},{1,5},{2,6},{3,7},{4,0},{5,1},{6,2},{7,3},{8,12},{9,13},{10,... | collective-permute-start | bytes 196616 | tf_op jit(solution)/shard_map/ppermute | solution.py:315
  41.8 1.7 %collective-permute-done.16.refs_0_ = bf16[256,256]{1,0:T(8,128)(2,1)S(1)} collective-permute-done((bf16[256,256]{1,0:T(8,128)(2,1)S(1)}, bf16[256,256]{1,0:T(8,128)(2,1)S(1)}, u32[]{:S(2)}, u32[]{:S(2)}) %collective-permute-start.16) | collective-permute-done | bytes 131104 | tf_op jit(solution)/shard_map/ppermute | solution.py:315
  43.5 2.0 %collective-permute-start.14 = (bf16[256,256]{1,0:T(8,128)(2,1)S(1)}, bf16[256,256]{1,0:T(8,128)(2,1)S(1)}, u32[]{:S(2)}, u32[]{:S(2)}) collective-permute-start(bf16[256,256]{1,0:T(8,128)(2,1)S(1)} %collective-permute-done.12.refs_1_), channel_id=1, source_target_pairs={{0,2},{1,0},{3,1},{5,3},{7,5},{6,7},{4,6},{2,4},{10,8},{12,10},{14... | collective-permute-start | bytes 393224 | tf_op jit(solution)/shard_map/ppermute | solution.py:315
  45.5 2.0 %collective-permute-start.13 = (bf16[128,256]{1,0:T(8,128)(2,1)S(1)}, bf16[128,256]{1,0:T(8,128)(2,1)S(1)}, u32[]{:S(2)}, u32[]{:S(2)}) collective-permute-start(bf16[128,256]{1,0:T(8,128)(2,1)S(1)} %add_convert_fusion.9), channel_id=1, source_target_pairs={{0,2},{1,3},{2,0},{3,1},{4,6},{5,7},{6,4},{7,5},{8,10},{9,11},{10,... | collective-permute-start | bytes 196616 | tf_op jit(solution)/shard_map/ppermute | solution.py:315
  47.5 1.2 %collective-permute-start.21 = (bf16[256,256]{1,0:T(8,128)(2,1)S(1)}, bf16[256,256]{1,0:T(8,128)(2,1)S(1)}, u32[]{:S(2)}, u32[]{:S(2)}) collective-permute-start(bf16[256,256]{1,0:T(8,128)(2,1)S(1)} %convolution_convert_fusion.1.refs_0_), channel_id=1, source_target_pairs={{0,7},{1,6},{3,4},{5,2},{7,0},{6,1},{4,3},{2,5},{10,13},{12,11},{1... | collective-permute-start | bytes 393224 | tf_op jit(solution)/shard_map/ppermute | solution.py:315
  48.7 1.3 %shard_map.99.refs_3_ = f32[1024,256]{1,0:T(8,128)S(1)} custom-call(s32[8,384]{1,0:T(8,128)S(1)} %get-tuple-element.37.table_ref, bf16[192,128,128]{2,1,0:T(8,128)(2,1)S(1)} %get-tuple-element.26.tiles_ref, bf16[256,256]{1,0:T(8,128)(2,1)S(1)} %collective-permute-done.16.refs_0_, bf16[256,256]{1,0:T(8,128)(2,1)S(1)} %collective-permute-done.12.refs_1_, ...), custom_call_target="tpu_custom_call" | custom-call | flops 402653184 | bytes 1572864 | tf_op jit(solution)/shard_map/pallas_call | solution.py:247
  50.0 0.8 %collective-permute-done.13 = bf16[128,256]{1,0:T(8,128)(2,1)S(1)} collective-permute-done((bf16[128,256]{1,0:T(8,128)(2,1)S(1)}, bf16[128,256]{1,0:T(8,128)(2,1)S(1)}, u32[]{:S(2)}, u32[]{:S(2)}) %collective-permute-start.13) | collective-permute-done | bytes 65568 | tf_op jit(solution)/shard_map/ppermute | solution.py:315
  50.8 1.5 %collective-permute-start.18 = (bf16[256,256]{1,0:T(8,128)(2,1)S(1)}, bf16[256,256]{1,0:T(8,128)(2,1)S(1)}, u32[]{:S(2)}, u32[]{:S(2)}) collective-permute-start(bf16[256,256]{1,0:T(8,128)(2,1)S(1)} %collective-permute-done.17.refs_0_), channel_id=1, source_target_pairs={{0,1},{1,3},{3,5},{5,7},{7,6},{6,4},{4,2},{2,0},{10,12},{12,14},{1... | collective-permute-start | bytes 393224 | tf_op jit(solution)/shard_map/ppermute | solution.py:315
  52.2 0.6 collective-permute-start.19
  52.8 1.5 %collective-permute-start.15 = (bf16[128,256]{1,0:T(8,128)(2,1)S(1)}, bf16[128,256]{1,0:T(8,128)(2,1)S(1)}, u32[]{:S(2)}, u32[]{:S(2)}) collective-permute-start(bf16[128,256]{1,0:T(8,128)(2,1)S(1)} %add_convert_fusion.8), channel_id=1, source_target_pairs={{0,1},{1,0},{2,3},{3,2},{4,5},{5,4},{6,7},{7,6},{8,9},{9,8},{10,11... | collective-permute-start | bytes 196616 | tf_op jit(solution)/shard_map/ppermute | solution.py:315
  54.3 1.7 %collective-permute-done.21.refs_2_ = bf16[256,256]{1,0:T(8,128)(2,1)S(1)} collective-permute-done((bf16[256,256]{1,0:T(8,128)(2,1)S(1)}, bf16[256,256]{1,0:T(8,128)(2,1)S(1)}, u32[]{:S(2)}, u32[]{:S(2)}) %collective-permute-start.21) | collective-permute-done | bytes 131104 | tf_op jit(solution)/shard_map/ppermute | solution.py:315
  56.0 1.6 %shard_map.100.refs_2_ = f32[1024,256]{1,0:T(8,128)S(1)} custom-call(s32[8,384]{1,0:T(8,128)S(1)} %get-tuple-element.37.table_ref, bf16[192,128,128]{2,1,0:T(8,128)(2,1)S(1)} %get-tuple-element.26.tiles_ref, bf16[256,256]{1,0:T(8,128)(2,1)S(1)} %collective-permute-done.17.refs_0_, bf16[256,256]{1,0:T(8,128)(2,1)S(1)} %collective-permute-done.14.refs_1_, ...), custom_call_target="tpu_custom_call" | custom-call | flops 402653184 | bytes 1572864 | tf_op jit(solution)/shard_map/pallas_call | solution.py:247
  57.6 0.3 collective-permute-done.19.refs_1_
  58.0 1.2 %shard_map.101 = (bf16[512,256]{1,0:T(8,128)(2,1)S(1)}, bf16[512,256]{1,0:T(8,128)(2,1)S(1)}) custom-call(s32[8,384]{1,0:T(8,128)S(1)} %get-tuple-element.37.table_ref, bf16[192,128,128]{2,1,0:T(8,128)(2,1)S(1)} %get-tuple-element.26.tiles_ref, bf16[256,256]{1,0:T(8,128)(2,1)S(1)} %collective-permute-done.18.refs_0_, ...), custom_call_target="tpu_custom_call" | custom-call | flops 402653184 | bytes 1572864 | tf_op jit(solution)/shard_map/pallas_call | solution.py:247
  59.3 0.3 collective-permute-start.20
  59.6 1.2 %collective-permute-done.22 = bf16[512,256]{1,0:T(8,128)(2,1)S(1)} collective-permute-done((bf16[512,256]{1,0:T(8,128)(2,1)S(1)}, bf16[512,256]{1,0:T(8,128)(2,1)S(1)}, u32[]{:S(2)}, u32[]{:S(2)}) %collective-permute-start.22) | collective-permute-done | bytes 262176 | tf_op jit(solution)/shard_map/ppermute | solution.py:315
  60.9 0.7 collective-permute-start.24
  61.6 2.5 %collective-permute-done.20 = bf16[128,256]{1,0:T(8,128)(2,1)S(1)} collective-permute-done((bf16[128,256]{1,0:T(8,128)(2,1)S(1)}, bf16[128,256]{1,0:T(8,128)(2,1)S(1)}, u32[]{:S(2)}, u32[]{:S(2)}) %collective-permute-start.20) | collective-permute-done | bytes 65568 | tf_op jit(solution)/shard_map/ppermute | solution.py:315
  64.2 1.0 %convolution_convert_fusion.3 = bf16[256,256]{1,0:T(8,128)(2,1)} fusion(f32[256,256]{1,0:T(8,128)S(1)} %fusion.23, s32[256]{0:T(256)S(1)} %iota_add_fusion, s32[256]{0:T(256)S(1)} %copy-done.1), kind=kOutput, calls=%fused_computation.8 | convolution fusion | flops 33947648 | bytes 395264 | tf_op jit(solution)/shard_map/dot_general | solution.py:41
  65.2 0.2 collective-permute-done.23
  65.5 0.7 %fusion.12 = f32[256,256]{1,0:T(8,128)} fusion(bf16[128,256]{1,0:T(8,128)(2,1)S(1)} %collective-permute-done.23, bf16[128,256]{1,0:T(8,128)(2,1)S(1)} %add_convert_fusion.6, pred[]{:T(512)S(6)} %eq.67), kind=kLoop, calls=%fused_computation.29 | loop fusion | flops 655360 | bytes 393217 | tf_op jit(solution)/shard_map/convert_element_type | solution.py:399
  66.2 0.5 collective-permute-done.24
  66.7 1.0 %convolution_convert_fusion = bf16[256,256]{1,0:T(8,128)(2,1)} fusion(f32[512,256]{1,0:T(8,128)S(1)} %convert_add_fusion, bf16[256,256]{1,0:T(8,128)(2,1)S(1)} %collective-permute-done.24, s32[256]{0:T(256)S(1)} %iota_add_fusion, s32[256]{0:T(256)S(1)} %copy-done.1), kind=kOutput, calls=%fused_computation.2 | convolution fusion | flops 33882112 | bytes 526336 | tf_op jit(solution)/shard_map/dot_general | solution.py:41
  (41 shorter events, 0.8 us)
Async XLA Ops:
  0.6 34.8 %copy-start = (bf16[256,256]{1,0:T(8,128)(2,1)S(1)}, bf16[256,256]{1,0:T(8,128)(2,1)}, u32[]{:S(2)}) copy-start(bf16[256,256]{1,0:T(8,128)(2,1)} %param.12) | copy-start | bytes 393220
  1.9 7.9 %collective-permute-start = (bf16[256,256]{1,0:T(8,128)(2,1)S(1)}, bf16[256,256]{1,0:T(8,128)(2,1)S(1)}, u32[]{:S(2)}, u32[]{:S(2)}) collective-permute-start(bf16[256,256]{1,0:T(8,128)(2,1)S(1)} %convolution_convert_fusion.4.refs_0_), channel_id=1, source_target_pairs={{0,16},{1,17},{2,18},{3,19},{4,20},{5,21},{6,22},{7,23},{8,24},{9,... | collective-permute-start | bytes 393224 | tf_op jit(solution)/shard_map/ppermute | solution.py:315
  4.9 5.5 %collective-permute-start.1 = (bf16[256,256]{1,0:T(8,128)(2,1)S(1)}, bf16[256,256]{1,0:T(8,128)(2,1)S(1)}, u32[]{:S(2)}, u32[]{:S(2)}) collective-permute-start(bf16[256,256]{1,0:T(8,128)(2,1)S(1)} %convolution_convert_fusion.4.refs_0_), channel_id=1, source_target_pairs={{0,8},{1,9},{2,10},{3,11},{4,12},{5,13},{6,14},{7,15},{8,0},{9,1},... | collective-permute-start | bytes 393224 | tf_op jit(solution)/shard_map/ppermute | solution.py:315
  9.8 1.6 %collective-permute-start.2 = (bf16[256,256]{1,0:T(8,128)(2,1)S(1)}, bf16[256,256]{1,0:T(8,128)(2,1)S(1)}, u32[]{:S(2)}, u32[]{:S(2)}) collective-permute-start(bf16[256,256]{1,0:T(8,128)(2,1)S(1)} %compare_select_fusion.2), channel_id=1, source_target_pairs={{0,8},{1,9},{2,10},{3,11},{4,12},{5,13},{6,14},{7,15},{8,0},{9,1},... | collective-permute-start | bytes 393224 | tf_op jit(solution)/shard_map/ppermute | solution.py:315
  12.5 7.9 %collective-permute-start.7 = (bf16[256,256]{1,0:T(8,128)(2,1)S(1)}, bf16[256,256]{1,0:T(8,128)(2,1)S(1)}, u32[]{:S(2)}, u32[]{:S(2)}) collective-permute-start(bf16[256,256]{1,0:T(8,128)(2,1)S(1)} %get-tuple-element.34), channel_id=1, source_target_pairs={{0,2},{1,0},{3,1},{5,3},{7,5},{6,7},{4,6},{2,4},{10,8},{12,10},{14... | collective-permute-start | bytes 393224 | tf_op jit(solution)/shard_map/ppermute | solution.py:315
  14.5 7.0 %collective-permute-start.3 = (bf16[256,256]{1,0:T(8,128)(2,1)S(1)}, bf16[256,256]{1,0:T(8,128)(2,1)S(1)}, u32[]{:S(2)}, u32[]{:S(2)}) collective-permute-start(bf16[256,256]{1,0:T(8,128)(2,1)S(1)} %get-tuple-element.28), channel_id=1, source_target_pairs={{0,1},{1,3},{3,5},{5,7},{7,6},{6,4},{4,2},{2,0},{10,12},{12,14},{1... | collective-permute-start | bytes 393224 | tf_op jit(solution)/shard_map/ppermute | solution.py:315
  16.2 19.5 %copy-start.1 = (s32[256]{0:T(256)S(1)}, s32[256]{0:T(256)}, u32[]{:S(2)}) copy-start(s32[256]{0:T(256)} %param.8) | copy-start | bytes 3076
  16.2 19.5 %copy-start.2 = (bf16[256,256]{1,0:T(8,128)(2,1)S(1)}, bf16[256,256]{1,0:T(8,128)(2,1)}, u32[]{:S(2)}) copy-start(bf16[256,256]{1,0:T(8,128)(2,1)} %param.13) | copy-start | bytes 393220
  16.2 14.0 %collective-permute-start.4 = (bf16[256,256]{1,0:T(8,128)(2,1)S(1)}, bf16[256,256]{1,0:T(8,128)(2,1)S(1)}, u32[]{:S(2)}, u32[]{:S(2)}) collective-permute-start(bf16[256,256]{1,0:T(8,128)(2,1)S(1)} %get-tuple-element.31), channel_id=1, source_target_pairs={{0,7},{1,6},{3,4},{5,2},{7,0},{6,1},{4,3},{2,5},{10,13},{12,11},{1... | collective-permute-start | bytes 393224 | tf_op jit(solution)/shard_map/ppermute | solution.py:315
  20.5 7.5 %collective-permute-start.8 = (bf16[256,256]{1,0:T(8,128)(2,1)S(1)}, bf16[256,256]{1,0:T(8,128)(2,1)S(1)}, u32[]{:S(2)}, u32[]{:S(2)}) collective-permute-start(bf16[256,256]{1,0:T(8,128)(2,1)S(1)} %add_convert_fusion.3), channel_id=1, source_target_pairs={{0,2},{1,0},{3,1},{5,3},{7,5},{6,7},{4,6},{2,4},{10,8},{12,10},{14... | collective-permute-start | bytes 393224 | tf_op jit(solution)/shard_map/ppermute | solution.py:315
  21.5 8.3 %collective-permute-start.5 = (bf16[256,256]{1,0:T(8,128)(2,1)S(1)}, bf16[256,256]{1,0:T(8,128)(2,1)S(1)}, u32[]{:S(2)}, u32[]{:S(2)}) collective-permute-start(bf16[256,256]{1,0:T(8,128)(2,1)S(1)} %add_convert_fusion.5), channel_id=1, source_target_pairs={{0,1},{1,3},{3,5},{5,7},{7,6},{6,4},{4,2},{2,0},{10,12},{12,14},{1... | collective-permute-start | bytes 393224 | tf_op jit(solution)/shard_map/ppermute | solution.py:315
  28.0 5.6 %collective-permute-start.9 = (bf16[256,256]{1,0:T(8,128)(2,1)S(1)}, bf16[256,256]{1,0:T(8,128)(2,1)S(1)}, u32[]{:S(2)}, u32[]{:S(2)}) collective-permute-start(bf16[256,256]{1,0:T(8,128)(2,1)S(1)} %add_convert_fusion.2), channel_id=1, source_target_pairs={{0,2},{1,0},{3,1},{5,3},{7,5},{6,7},{4,6},{2,4},{10,8},{12,10},{14... | collective-permute-start | bytes 393224 | tf_op jit(solution)/shard_map/ppermute | solution.py:315
  29.8 5.5 %collective-permute-start.6 = (bf16[256,256]{1,0:T(8,128)(2,1)S(1)}, bf16[256,256]{1,0:T(8,128)(2,1)S(1)}, u32[]{:S(2)}, u32[]{:S(2)}) collective-permute-start(bf16[256,256]{1,0:T(8,128)(2,1)S(1)} %add_convert_fusion.4), channel_id=1, source_target_pairs={{0,1},{1,3},{3,5},{5,7},{7,6},{6,4},{4,2},{2,0},{10,12},{12,14},{1... | collective-permute-start | bytes 393224 | tf_op jit(solution)/shard_map/ppermute | solution.py:315
  36.1 3.7 %collective-permute-start.10 = (bf16[256,256]{1,0:T(8,128)(2,1)S(1)}, bf16[256,256]{1,0:T(8,128)(2,1)S(1)}, u32[]{:S(2)}, u32[]{:S(2)}) collective-permute-start(bf16[256,256]{1,0:T(8,128)(2,1)S(1)} %fusion), channel_id=1, source_target_pairs={{0,8},{1,9},{2,10},{3,11},{4,12},{5,13},{6,14},{7,15},{8,0},{9,1},... | collective-permute-start | bytes 393224 | tf_op jit(solution)/shard_map/ppermute | solution.py:315
  36.4 7.0 %collective-permute-start.12 = (bf16[256,256]{1,0:T(8,128)(2,1)S(1)}, bf16[256,256]{1,0:T(8,128)(2,1)S(1)}, u32[]{:S(2)}, u32[]{:S(2)}) collective-permute-start(bf16[256,256]{1,0:T(8,128)(2,1)S(1)} %convolution_convert_fusion.1.refs_0_), channel_id=1, source_target_pairs={{0,2},{1,0},{3,1},{5,3},{7,5},{6,7},{4,6},{2,4},{10,8},{12,10},{14... | collective-permute-start | bytes 393224 | tf_op jit(solution)/shard_map/ppermute | solution.py:315
  38.5 5.0 %collective-permute-start.16 = (bf16[256,256]{1,0:T(8,128)(2,1)S(1)}, bf16[256,256]{1,0:T(8,128)(2,1)S(1)}, u32[]{:S(2)}, u32[]{:S(2)}) collective-permute-start(bf16[256,256]{1,0:T(8,128)(2,1)S(1)} %convolution_convert_fusion.1.refs_0_), channel_id=1, source_target_pairs={{0,1},{1,3},{3,5},{5,7},{7,6},{6,4},{4,2},{2,0},{10,12},{12,14},{1... | collective-permute-start | bytes 393224 | tf_op jit(solution)/shard_map/ppermute | solution.py:315
  39.8 5.7 %collective-permute-start.11 = (bf16[128,256]{1,0:T(8,128)(2,1)S(1)}, bf16[128,256]{1,0:T(8,128)(2,1)S(1)}, u32[]{:S(2)}, u32[]{:S(2)}) collective-permute-start(bf16[128,256]{1,0:T(8,128)(2,1)S(1)} %slice_select_fusion), channel_id=1, source_target_pairs={{0,4},{1,5},{2,6},{3,7},{4,0},{5,1},{6,2},{7,3},{8,12},{9,13},{10,... | collective-permute-start | bytes 196616 | tf_op jit(solution)/shard_map/ppermute | solution.py:315
  43.4 7.3 %collective-permute-start.17 = (bf16[256,256]{1,0:T(8,128)(2,1)S(1)}, bf16[256,256]{1,0:T(8,128)(2,1)S(1)}, u32[]{:S(2)}, u32[]{:S(2)}) collective-permute-start(bf16[256,256]{1,0:T(8,128)(2,1)S(1)} %collective-permute-done.16.refs_0_), channel_id=1, source_target_pairs={{0,1},{1,3},{3,5},{5,7},{7,6},{6,4},{4,2},{2,0},{10,12},{12,14},{1... | collective-permute-start | bytes 393224 | tf_op jit(solution)/shard_map/ppermute | solution.py:315
  43.5 7.3 %collective-permute-start.14 = (bf16[256,256]{1,0:T(8,128)(2,1)S(1)}, bf16[256,256]{1,0:T(8,128)(2,1)S(1)}, u32[]{:S(2)}, u32[]{:S(2)}) collective-permute-start(bf16[256,256]{1,0:T(8,128)(2,1)S(1)} %collective-permute-done.12.refs_1_), channel_id=1, source_target_pairs={{0,2},{1,0},{3,1},{5,3},{7,5},{6,7},{4,6},{2,4},{10,8},{12,10},{14... | collective-permute-start | bytes 393224 | tf_op jit(solution)/shard_map/ppermute | solution.py:315
  45.5 5.2 %collective-permute-start.13 = (bf16[128,256]{1,0:T(8,128)(2,1)S(1)}, bf16[128,256]{1,0:T(8,128)(2,1)S(1)}, u32[]{:S(2)}, u32[]{:S(2)}) collective-permute-start(bf16[128,256]{1,0:T(8,128)(2,1)S(1)} %add_convert_fusion.9), channel_id=1, source_target_pairs={{0,2},{1,3},{2,0},{3,1},{4,6},{5,7},{6,4},{7,5},{8,10},{9,11},{10,... | collective-permute-start | bytes 196616 | tf_op jit(solution)/shard_map/ppermute | solution.py:315
  47.5 8.5 %collective-permute-start.21 = (bf16[256,256]{1,0:T(8,128)(2,1)S(1)}, bf16[256,256]{1,0:T(8,128)(2,1)S(1)}, u32[]{:S(2)}, u32[]{:S(2)}) collective-permute-start(bf16[256,256]{1,0:T(8,128)(2,1)S(1)} %convolution_convert_fusion.1.refs_0_), channel_id=1, source_target_pairs={{0,7},{1,6},{3,4},{5,2},{7,0},{6,1},{4,3},{2,5},{10,13},{12,11},{1... | collective-permute-start | bytes 393224 | tf_op jit(solution)/shard_map/ppermute | solution.py:315
  50.8 6.9 %collective-permute-start.18 = (bf16[256,256]{1,0:T(8,128)(2,1)S(1)}, bf16[256,256]{1,0:T(8,128)(2,1)S(1)}, u32[]{:S(2)}, u32[]{:S(2)}) collective-permute-start(bf16[256,256]{1,0:T(8,128)(2,1)S(1)} %collective-permute-done.17.refs_0_), channel_id=1, source_target_pairs={{0,1},{1,3},{3,5},{5,7},{7,6},{6,4},{4,2},{2,0},{10,12},{12,14},{1... | collective-permute-start | bytes 393224 | tf_op jit(solution)/shard_map/ppermute | solution.py:315
  52.2 5.8 %collective-permute-start.19 = (bf16[256,256]{1,0:T(8,128)(2,1)S(1)}, bf16[256,256]{1,0:T(8,128)(2,1)S(1)}, u32[]{:S(2)}, u32[]{:S(2)}) collective-permute-start(bf16[256,256]{1,0:T(8,128)(2,1)S(1)} %collective-permute-done.14.refs_1_), channel_id=1, source_target_pairs={{0,2},{1,0},{3,1},{5,3},{7,5},{6,7},{4,6},{2,4},{10,8},{12,10},{14... | collective-permute-start | bytes 393224 | tf_op jit(solution)/shard_map/ppermute | solution.py:315
  52.8 6.5 %collective-permute-start.15 = (bf16[128,256]{1,0:T(8,128)(2,1)S(1)}, bf16[128,256]{1,0:T(8,128)(2,1)S(1)}, u32[]{:S(2)}, u32[]{:S(2)}) collective-permute-start(bf16[128,256]{1,0:T(8,128)(2,1)S(1)} %add_convert_fusion.8), channel_id=1, source_target_pairs={{0,1},{1,0},{2,3},{3,2},{4,5},{5,4},{6,7},{7,6},{8,9},{9,8},{10,11... | collective-permute-start | bytes 196616 | tf_op jit(solution)/shard_map/ppermute | solution.py:315
  59.2 1.6 %collective-permute-start.22 = (bf16[512,256]{1,0:T(8,128)(2,1)S(1)}, bf16[512,256]{1,0:T(8,128)(2,1)S(1)}, u32[]{:S(2)}, u32[]{:S(2)}) collective-permute-start(bf16[512,256]{1,0:T(8,128)(2,1)S(1)} %get-tuple-element.45), channel_id=1, source_target_pairs={{0,8},{1,9},{2,10},{3,11},{4,12},{5,13},{6,14},{7,15},{8,0},{9,1},... | collective-permute-start | bytes 786440 | tf_op jit(solution)/shard_map/ppermute | solution.py:315
  59.3 4.8 %collective-permute-start.20 = (bf16[128,256]{1,0:T(8,128)(2,1)S(1)}, bf16[128,256]{1,0:T(8,128)(2,1)S(1)}, u32[]{:S(2)}, u32[]{:S(2)}) collective-permute-start(bf16[128,256]{1,0:T(8,128)(2,1)S(1)} %add_convert_fusion.7), channel_id=1, source_target_pairs={{0,16},{1,17},{2,18},{3,19},{4,20},{5,21},{6,22},{7,23},{8,24},{9,... | collective-permute-start | bytes 196616 | tf_op jit(solution)/shard_map/ppermute | solution.py:315
  60.9 5.8 %collective-permute-start.24 = (bf16[256,256]{1,0:T(8,128)(2,1)S(1)}, bf16[256,256]{1,0:T(8,128)(2,1)S(1)}, u32[]{:S(2)}, u32[]{:S(2)}) collective-permute-start(bf16[256,256]{1,0:T(8,128)(2,1)S(1)} %slice.28), channel_id=1, source_target_pairs={{0,16},{1,17},{2,18},{3,19},{4,20},{5,21},{6,22},{7,23},{8,24},{9,... | collective-permute-start | bytes 393224 | tf_op jit(solution)/shard_map/ppermute | solution.py:315
  64.1 1.3 %collective-permute-start.23 = (bf16[128,256]{1,0:T(8,128)(2,1)S(1)}, bf16[128,256]{1,0:T(8,128)(2,1)S(1)}, u32[]{:S(2)}, u32[]{:S(2)}) collective-permute-start(bf16[128,256]{1,0:T(8,128)(2,1)S(1)} %add_convert_fusion.6), channel_id=1, source_target_pairs={{0,8},{1,9},{2,10},{3,11},{4,12},{5,13},{6,14},{7,15},{8,0},{9,1},... | collective-permute-start | bytes 196616 | tf_op jit(solution)/shard_map/ppermute | solution.py:315

commit v2 on v1

--- a/solution.py
+++ b/solution.py
@@ -9,13 +9,13 @@
 
 CORES = 2
 GROUP = 4
-UNROLL = 4
+UNROLL = 8
 LANES = 128
 PACK_BITS = 8
 PACK = 1 << PACK_BITS
 VMEM_BYTES = 16 * 1024 * 1024
 LOAD_BYTES = 45 * 1024 * 1024
-LOADS = 4
+LOADS = 16
 F32 = jnp.float32
 BF16 = jnp.bfloat16
 
@@ -387,7 +387,7 @@
     half = held.shape[0] // CORES
     chip = (held.astype(F32) + after(got, *gate).astype(F32)).astype(BF16)
     held = jnp.where(grid.core == 0, chip[:half], chip[half:])
-    bits = [(0, 1 << k) for k in reversed(range(bits_of(grid.cols)))]
+    bits = [(0, 1 << k) for k in range(bits_of(grid.cols))]
     bits += [(1 << k, 0) for k in range(1, bits_of(grid.rows))]
     for row_bit, col_bit in bits:
         got = move(held, grid.across(row_bit, col_bit))

time: 67.9 us -> 68.7 us (1.012)
  starting transfers between devices: 28.2 us -> 29.1 us
  waiting for transfers between devices: 18.8 us -> 18.1 us
    ppermute x25, starting transfers between devices: 28.2 us -> 29.1 us  [move(): return lax.ppermute(value, ('row', 'col'), pairs)]
where the time goes in v2:
time: 68.7 us; the launch traced here: 68.5 us
  starting transfers between devices  29.1 us (42%)
  waiting for transfers between devices  18.1 us (26%)
  Pallas kernels  13.6 us (20%)
  matrix products  4.02 us (6%)
  other arithmetic  1.85 us (3%)
  between operations  1.63 us (2%)
    ppermute x25, starting transfers between devices, move(): return lax.ppermute(value, ('row', 'col'), pairs)  29.1 us
    ppermute x25, waiting for transfers between devices, move(): return lax.ppermute(value, ('row', 'col'), pairs)  18.1 us
    pallas_call x7, Pallas kernels, tile_part(): pl.pallas_call(functools.partial(part_kernel, spec), out_shape=out_shape,...  9.94 us
    pallas_call x1, Pallas kernels, load_tiles(): pl.pallas_call(functools.partial(load_kernel, sizes), out_shape=[jax.Shap...  3.7 us
    dot_general x2, matrix products, restore(): lax.dot_general(moves, values, (((0,), (0,)), ((), ())), preferred_elemen...  1.99 us
    dot_general x2, matrix products, reorder(): return jnp.dot(moves, values, preferred_element_type=F32).astype(BF16)  1.41 us
  transfers between devices with their start and end apart: 25, of which 12 were waited for; matrix products, arithmetic and copies ran while one was open for 5% of the time, Pallas kernels for 18%

profile of v2, /device:TPU:0, one launch (start us, length us, event | category | flops | bytes accessed | tf_op | source)
XLA Modules:
  0.0 68.5 jit_solution(18195977487143399748)
XLA Ops:
  0.7 1.2 %convolution_convert_fusion.4.refs_0_ = bf16[256,256]{1,0:T(8,128)(2,1)S(1)} fusion(bf16[256,256]{1,0:T(8,128)(2,1)} %param.7, s32[256]{0:T(256)S(1)} %iota_add_fusion, s32[256]{0:T(256)} %param.8), kind=kOutput, calls=%fused_computation.9 | convolution fusion | flops 33685504 | bytes 264192 | tf_op jit(solution)/shard_map/dot_general | solution.py:37
  1.9 3.0 %collective-permute-start = (bf16[256,256]{1,0:T(8,128)(2,1)S(1)}, bf16[256,256]{1,0:T(8,128)(2,1)S(1)}, u32[]{:S(2)}, u32[]{:S(2)}) collective-permute-start(bf16[256,256]{1,0:T(8,128)(2,1)S(1)} %convolution_convert_fusion.4.refs_0_), channel_id=1, source_target_pairs={{0,16},{1,17},{2,18},{3,19},{4,20},{5,21},{6,22},{7,23},{8,24},{9,... | collective-permute-start | bytes 393224 | tf_op jit(solution)/shard_map/ppermute | solution.py:315
  5.6 0.1 stack.43.here_ref
  5.6 0.7 %pad_add_fusion.facts_ref = s32[2,256]{1,0:T(2,128)S(1)} fusion(s32[1,1]{1,0:T(1,128)S(6)} %copy.10, s32[1,192]{1,0:T(1,128)} %bitcast.21), kind=kLoop, calls=%fused_computation.44 | loop fusion | flops 512 | bytes 2820 | tf_op jit(solution)/shard_map/concatenate | solution.py:165
  6.3 3.7 %shard_map.94 = (bf16[192,128,128]{2,1,0:T(8,128)(2,1)S(1)}, s32[8,384]{1,0:T(8,128)S(1)}, s32[8,384]{1,0:T(8,128)S(1)}, bf16[256,256]{1,0:T(8,128)(2,1)S(1)}) custom-call(s32[10]{0:T(128)S(1)} %stack.43.here_ref, s32[2,256]{1,0:T(2,128)S(1)} %pad_add_fusion.facts_ref, bf16[192,128,128]{2,1,0:T(8,128)(2,1)} %bitcast.20), custom_call_target="tpu_custom_call" | custom-call | bytes 6291456 | tf_op jit(solution)/shard_map/pallas_call | solution.py:167
  10.1 0.6 collective-permute-start.2
  10.6 1.0 %collective-permute-done.2.refs_3_ = bf16[256,256]{1,0:T(8,128)(2,1)S(1)} collective-permute-done((bf16[256,256]{1,0:T(8,128)(2,1)S(1)}, bf16[256,256]{1,0:T(8,128)(2,1)S(1)}, u32[]{:S(2)}, u32[]{:S(2)}) %collective-permute-start.2) | collective-permute-done | bytes 131104 | tf_op jit(solution)/shard_map/ppermute | solution.py:315
  11.6 1.4 %shard_map.95 = (bf16[256,256]{1,0:T(8,128)(2,1)S(1)}, bf16[256,256]{1,0:T(8,128)(2,1)S(1)}) custom-call(s32[8,384]{1,0:T(8,128)S(1)} %get-tuple-element.29.table_ref, bf16[192,128,128]{2,1,0:T(8,128)(2,1)S(1)} %get-tuple-element.26.tiles_ref, bf16[256,256]{1,0:T(8,128)(2,1)S(1)} %convolution_convert_fusion.4.refs_0_, ...), custom_call_target="tpu_custom_call" | custom-call | flops 402653184 | bytes 1572864 | tf_op jit(solution)/shard_map/pallas_call | solution.py:247
  13.0 2.2 %collective-permute-start.7 = (bf16[256,256]{1,0:T(8,128)(2,1)S(1)}, bf16[256,256]{1,0:T(8,128)(2,1)S(1)}, u32[]{:S(2)}, u32[]{:S(2)}) collective-permute-start(bf16[256,256]{1,0:T(8,128)(2,1)S(1)} %get-tuple-element.34), channel_id=1, source_target_pairs={{0,2},{1,0},{3,1},{5,3},{7,5},{6,7},{4,6},{2,4},{10,8},{12,10},{14... | collective-permute-start | bytes 393224 | tf_op jit(solution)/shard_map/ppermute | solution.py:315
  15.2 1.4 %shard_map.97 = (bf16[256,256]{1,0:T(8,128)(2,1)S(1)}, bf16[256,256]{1,0:T(8,128)(2,1)S(1)}, bf16[256,256]{1,0:T(8,128)(2,1)S(1)}) custom-call(s32[8,384]{1,0:T(8,128)S(1)} %get-tuple-element.29.table_ref, bf16[192,128,128]{2,1,0:T(8,128)(2,1)S(1)} %get-tuple-element.26.tiles_ref, bf16[256,256]{1,0:T(8,128)(2,1)S(1)} %convolution_convert_fusion.4.refs_0_, ...), custom_call_target="tpu_custom_call" | custom-call | flops 603979776 | bytes 2359296 | tf_op jit(solution)/shard_map/pallas_call | solution.py:247
  16.6 4.5 %collective-permute-start.4 = (bf16[256,256]{1,0:T(8,128)(2,1)S(1)}, bf16[256,256]{1,0:T(8,128)(2,1)S(1)}, u32[]{:S(2)}, u32[]{:S(2)}) collective-permute-start(bf16[256,256]{1,0:T(8,128)(2,1)S(1)} %get-tuple-element.31), channel_id=1, source_target_pairs={{0,7},{1,6},{3,4},{5,2},{7,0},{6,1},{4,3},{2,5},{10,13},{12,11},{1... | collective-permute-start | bytes 393224 | tf_op jit(solution)/shard_map/ppermute | solution.py:315
  21.3 2.1 %collective-permute-start.5 = (bf16[256,256]{1,0:T(8,128)(2,1)S(1)}, bf16[256,256]{1,0:T(8,128)(2,1)S(1)}, u32[]{:S(2)}, u32[]{:S(2)}) collective-permute-start(bf16[256,256]{1,0:T(8,128)(2,1)S(1)} %add_convert_fusion.5), channel_id=1, source_target_pairs={{0,1},{1,3},{3,5},{5,7},{7,6},{6,4},{4,2},{2,0},{10,12},{12,14},{1... | collective-permute-start | bytes 393224 | tf_op jit(solution)/shard_map/ppermute | solution.py:315
  23.4 1.4 %shard_map.96 = (bf16[256,256]{1,0:T(8,128)(2,1)S(1)}, bf16[256,256]{1,0:T(8,128)(2,1)S(1)}, bf16[256,256]{1,0:T(8,128)(2,1)S(1)}) custom-call(s32[8,384]{1,0:T(8,128)S(1)} %get-tuple-element.29.table_ref, bf16[192,128,128]{2,1,0:T(8,128)(2,1)S(1)} %get-tuple-element.26.tiles_ref, bf16[256,256]{1,0:T(8,128)(2,1)S(1)} %convolution_convert_fusion.4.refs_0_, ...), custom_call_target="tpu_custom_call" | custom-call | flops 603979776 | bytes 2359296 | tf_op jit(solution)/shard_map/pallas_call | solution.py:247
  24.8 3.4 %collective-permute-done.8 = bf16[256,256]{1,0:T(8,128)(2,1)S(1)} collective-permute-done((bf16[256,256]{1,0:T(8,128)(2,1)S(1)}, bf16[256,256]{1,0:T(8,128)(2,1)S(1)}, u32[]{:S(2)}, u32[]{:S(2)}) %collective-permute-start.8) | collective-permute-done | bytes 131104 | tf_op jit(solution)/shard_map/ppermute | solution.py:315
  28.2 1.1 %collective-permute-start.9 = (bf16[256,256]{1,0:T(8,128)(2,1)S(1)}, bf16[256,256]{1,0:T(8,128)(2,1)S(1)}, u32[]{:S(2)}, u32[]{:S(2)}) collective-permute-start(bf16[256,256]{1,0:T(8,128)(2,1)S(1)} %add_convert_fusion.2), channel_id=1, source_target_pairs={{0,2},{1,0},{3,1},{5,3},{7,5},{6,7},{4,6},{2,4},{10,8},{12,10},{14... | collective-permute-start | bytes 393224 | tf_op jit(solution)/shard_map/ppermute | solution.py:315
  29.4 1.0 %collective-permute-start.6 = (bf16[256,256]{1,0:T(8,128)(2,1)S(1)}, bf16[256,256]{1,0:T(8,128)(2,1)S(1)}, u32[]{:S(2)}, u32[]{:S(2)}) collective-permute-start(bf16[256,256]{1,0:T(8,128)(2,1)S(1)} %add_convert_fusion.4), channel_id=1, source_target_pairs={{0,1},{1,3},{3,5},{5,7},{7,6},{6,4},{4,2},{2,0},{10,12},{12,14},{1... | collective-permute-start | bytes 393224 | tf_op jit(solution)/shard_map/ppermute | solution.py:315
  30.4 3.3 %collective-permute-done.9 = bf16[256,256]{1,0:T(8,128)(2,1)S(1)} collective-permute-done((bf16[256,256]{1,0:T(8,128)(2,1)S(1)}, bf16[256,256]{1,0:T(8,128)(2,1)S(1)}, u32[]{:S(2)}, u32[]{:S(2)}) %collective-permute-start.9) | collective-permute-done | bytes 131104 | tf_op jit(solution)/shard_map/ppermute | solution.py:315
  33.7 1.0 %collective-permute-done.6 = bf16[256,256]{1,0:T(8,128)(2,1)S(1)} collective-permute-done((bf16[256,256]{1,0:T(8,128)(2,1)S(1)}, bf16[256,256]{1,0:T(8,128)(2,1)S(1)}, u32[]{:S(2)}, u32[]{:S(2)}) %collective-permute-start.6) | collective-permute-done | bytes 131104 | tf_op jit(solution)/shard_map/ppermute | solution.py:315
  34.7 0.1 add_convert_fusion.1
  34.8 0.2 fusion.23
  35.0 0.2 fusion.3
  35.2 0.2 fusion
  35.5 0.2 convolution_convert_fusion.1.refs_0_
  35.7 2.1 %collective-permute-start.12 = (bf16[256,256]{1,0:T(8,128)(2,1)S(1)}, bf16[256,256]{1,0:T(8,128)(2,1)S(1)}, u32[]{:S(2)}, u32[]{:S(2)}) collective-permute-start(bf16[256,256]{1,0:T(8,128)(2,1)S(1)} %convolution_convert_fusion.1.refs_0_), channel_id=1, source_target_pairs={{0,2},{1,0},{3,1},{5,3},{7,5},{6,7},{4,6},{2,4},{10,8},{12,10},{14... | collective-permute-start | bytes 393224 | tf_op jit(solution)/shard_map/ppermute | solution.py:315
  37.8 1.4 %shard_map.98.refs_2_ = f32[1024,256]{1,0:T(8,128)S(1)} custom-call(s32[8,384]{1,0:T(8,128)S(1)} %get-tuple-element.37.table_ref, bf16[192,128,128]{2,1,0:T(8,128)(2,1)S(1)} %get-tuple-element.26.tiles_ref, bf16[256,256]{1,0:T(8,128)(2,1)S(1)} %convolution_convert_fusion.1.refs_0_), custom_call_target="tpu_custom_call" | custom-call | flops 402653184 | bytes 1572864 | tf_op jit(solution)/shard_map/pallas_call | solution.py:247
  39.3 0.9 %collective-permute-start.11 = (bf16[128,256]{1,0:T(8,128)(2,1)S(1)}, bf16[128,256]{1,0:T(8,128)(2,1)S(1)}, u32[]{:S(2)}, u32[]{:S(2)}) collective-permute-start(bf16[128,256]{1,0:T(8,128)(2,1)S(1)} %slice_select_fusion), channel_id=1, source_target_pairs={{0,1},{1,0},{2,3},{3,2},{4,5},{5,4},{6,7},{7,6},{8,9},{9,8},{10,11... | collective-permute-start | bytes 196616 | tf_op jit(solution)/shard_map/ppermute | solution.py:315
  40.3 2.5 %collective-permute-done.16.refs_0_ = bf16[256,256]{1,0:T(8,128)(2,1)S(1)} collective-permute-done((bf16[256,256]{1,0:T(8,128)(2,1)S(1)}, bf16[256,256]{1,0:T(8,128)(2,1)S(1)}, u32[]{:S(2)}, u32[]{:S(2)}) %collective-permute-start.16) | collective-permute-done | bytes 131104 | tf_op jit(solution)/shard_map/ppermute | solution.py:315
  42.8 2.0 %collective-permute-start.14 = (bf16[256,256]{1,0:T(8,128)(2,1)S(1)}, bf16[256,256]{1,0:T(8,128)(2,1)S(1)}, u32[]{:S(2)}, u32[]{:S(2)}) collective-permute-start(bf16[256,256]{1,0:T(8,128)(2,1)S(1)} %collective-permute-done.12.refs_1_), channel_id=1, source_target_pairs={{0,2},{1,0},{3,1},{5,3},{7,5},{6,7},{4,6},{2,4},{10,8},{12,10},{14... | collective-permute-start | bytes 393224 | tf_op jit(solution)/shard_map/ppermute | solution.py:315
  44.8 1.5 %collective-permute-start.13 = (bf16[128,256]{1,0:T(8,128)(2,1)S(1)}, bf16[128,256]{1,0:T(8,128)(2,1)S(1)}, u32[]{:S(2)}, u32[]{:S(2)}) collective-permute-start(bf16[128,256]{1,0:T(8,128)(2,1)S(1)} %add_convert_fusion.9), channel_id=1, source_target_pairs={{0,2},{1,3},{2,0},{3,1},{4,6},{5,7},{6,4},{7,5},{8,10},{9,11},{10,... | collective-permute-start | bytes 196616 | tf_op jit(solution)/shard_map/ppermute | solution.py:315
  46.3 1.8 %collective-permute-start.21 = (bf16[256,256]{1,0:T(8,128)(2,1)S(1)}, bf16[256,256]{1,0:T(8,128)(2,1)S(1)}, u32[]{:S(2)}, u32[]{:S(2)}) collective-permute-start(bf16[256,256]{1,0:T(8,128)(2,1)S(1)} %convolution_convert_fusion.1.refs_0_), channel_id=1, source_target_pairs={{0,7},{1,6},{3,4},{5,2},{7,0},{6,1},{4,3},{2,5},{10,13},{12,11},{1... | collective-permute-start | bytes 393224 | tf_op jit(solution)/shard_map/ppermute | solution.py:315
  48.1 1.4 %shard_map.99.refs_3_ = f32[1024,256]{1,0:T(8,128)S(1)} custom-call(s32[8,384]{1,0:T(8,128)S(1)} %get-tuple-element.37.table_ref, bf16[192,128,128]{2,1,0:T(8,128)(2,1)S(1)} %get-tuple-element.26.tiles_ref, bf16[256,256]{1,0:T(8,128)(2,1)S(1)} %collective-permute-done.16.refs_0_, bf16[256,256]{1,0:T(8,128)(2,1)S(1)} %collective-permute-done.12.refs_1_, ...), custom_call_target="tpu_custom_call" | custom-call | flops 402653184 | bytes 1572864 | tf_op jit(solution)/shard_map/pallas_call | solution.py:247
  49.5 0.5 collective-permute-done.13
  50.1 1.1 %collective-permute-start.18 = (bf16[256,256]{1,0:T(8,128)(2,1)S(1)}, bf16[256,256]{1,0:T(8,128)(2,1)S(1)}, u32[]{:S(2)}, u32[]{:S(2)}) collective-permute-start(bf16[256,256]{1,0:T(8,128)(2,1)S(1)} %collective-permute-done.17.refs_0_), channel_id=1, source_target_pairs={{0,1},{1,3},{3,5},{5,7},{7,6},{6,4},{4,2},{2,0},{10,12},{12,14},{1... | collective-permute-start | bytes 393224 | tf_op jit(solution)/shard_map/ppermute | solution.py:315
  51.2 0.9 %collective-permute-start.19 = (bf16[256,256]{1,0:T(8,128)(2,1)S(1)}, bf16[256,256]{1,0:T(8,128)(2,1)S(1)}, u32[]{:S(2)}, u32[]{:S(2)}) collective-permute-start(bf16[256,256]{1,0:T(8,128)(2,1)S(1)} %collective-permute-done.14.refs_1_), channel_id=1, source_target_pairs={{0,2},{1,0},{3,1},{5,3},{7,5},{6,7},{4,6},{2,4},{10,8},{12,10},{14... | collective-permute-start | bytes 393224 | tf_op jit(solution)/shard_map/ppermute | solution.py:315
  52.1 1.9 %collective-permute-start.15 = (bf16[128,256]{1,0:T(8,128)(2,1)S(1)}, bf16[128,256]{1,0:T(8,128)(2,1)S(1)}, u32[]{:S(2)}, u32[]{:S(2)}) collective-permute-start(bf16[128,256]{1,0:T(8,128)(2,1)S(1)} %add_convert_fusion.8), channel_id=1, source_target_pairs={{0,4},{1,5},{2,6},{3,7},{4,0},{5,1},{6,2},{7,3},{8,12},{9,13},{10,... | collective-permute-start | bytes 196616 | tf_op jit(solution)/shard_map/ppermute | solution.py:315
  54.0 0.9 %collective-permute-done.21.refs_2_ = bf16[256,256]{1,0:T(8,128)(2,1)S(1)} collective-permute-done((bf16[256,256]{1,0:T(8,128)(2,1)S(1)}, bf16[256,256]{1,0:T(8,128)(2,1)S(1)}, u32[]{:S(2)}, u32[]{:S(2)}) %collective-permute-start.21) | collective-permute-done | bytes 131104 | tf_op jit(solution)/shard_map/ppermute | solution.py:315
  54.9 1.4 %shard_map.100.refs_2_ = f32[1024,256]{1,0:T(8,128)S(1)} custom-call(s32[8,384]{1,0:T(8,128)S(1)} %get-tuple-element.37.table_ref, bf16[192,128,128]{2,1,0:T(8,128)(2,1)S(1)} %get-tuple-element.26.tiles_ref, bf16[256,256]{1,0:T(8,128)(2,1)S(1)} %collective-permute-done.17.refs_0_, bf16[256,256]{1,0:T(8,128)(2,1)S(1)} %collective-permute-done.14.refs_1_, ...), custom_call_target="tpu_custom_call" | custom-call | flops 402653184 | bytes 1572864 | tf_op jit(solution)/shard_map/pallas_call | solution.py:247
  56.4 0.3 collective-permute-done.18.refs_0_
  56.7 1.4 %shard_map.101 = (bf16[512,256]{1,0:T(8,128)(2,1)S(1)}, bf16[512,256]{1,0:T(8,128)(2,1)S(1)}) custom-call(s32[8,384]{1,0:T(8,128)S(1)} %get-tuple-element.37.table_ref, bf16[192,128,128]{2,1,0:T(8,128)(2,1)S(1)} %get-tuple-element.26.tiles_ref, bf16[256,256]{1,0:T(8,128)(2,1)S(1)} %collective-permute-done.18.refs_0_, ...), custom_call_target="tpu_custom_call" | custom-call | flops 402653184 | bytes 1572864 | tf_op jit(solution)/shard_map/pallas_call | solution.py:247
  58.2 2.1 %collective-permute-done.15 = bf16[128,256]{1,0:T(8,128)(2,1)S(1)} collective-permute-done((bf16[128,256]{1,0:T(8,128)(2,1)S(1)}, bf16[128,256]{1,0:T(8,128)(2,1)S(1)}, u32[]{:S(2)}, u32[]{:S(2)}) %collective-permute-start.15) | collective-permute-done | bytes 65568 | tf_op jit(solution)/shard_map/ppermute | solution.py:315
  60.4 1.9 %collective-permute-start.20 = (bf16[128,256]{1,0:T(8,128)(2,1)S(1)}, bf16[128,256]{1,0:T(8,128)(2,1)S(1)}, u32[]{:S(2)}, u32[]{:S(2)}) collective-permute-start(bf16[128,256]{1,0:T(8,128)(2,1)S(1)} %add_convert_fusion.7), channel_id=1, source_target_pairs={{0,16},{1,17},{2,18},{3,19},{4,20},{5,21},{6,22},{7,23},{8,24},{9,... | collective-permute-start | bytes 196616 | tf_op jit(solution)/shard_map/ppermute | solution.py:315
  62.3 0.3 collective-permute-start.24
  62.6 2.2 %collective-permute-done.20 = bf16[128,256]{1,0:T(8,128)(2,1)S(1)} collective-permute-done((bf16[128,256]{1,0:T(8,128)(2,1)S(1)}, bf16[128,256]{1,0:T(8,128)(2,1)S(1)}, u32[]{:S(2)}, u32[]{:S(2)}) %collective-permute-start.20) | collective-permute-done | bytes 65568 | tf_op jit(solution)/shard_map/ppermute | solution.py:315
  64.9 1.0 %convolution_convert_fusion.3 = bf16[256,256]{1,0:T(8,128)(2,1)} fusion(f32[256,256]{1,0:T(8,128)S(1)} %fusion.23, s32[256]{0:T(256)S(1)} %iota_add_fusion, s32[256]{0:T(256)S(1)} %copy-done.1), kind=kOutput, calls=%fused_computation.8 | convolution fusion | flops 33947648 | bytes 395264 | tf_op jit(solution)/shard_map/dot_general | solution.py:41
  65.9 0.2 collective-permute-done.23
  66.2 0.7 %fusion.12 = f32[256,256]{1,0:T(8,128)} fusion(bf16[128,256]{1,0:T(8,128)(2,1)S(1)} %collective-permute-done.23, bf16[128,256]{1,0:T(8,128)(2,1)S(1)} %add_convert_fusion.6, pred[]{:T(512)S(6)} %eq.67), kind=kLoop, calls=%fused_computation.29 | loop fusion | flops 655360 | bytes 393217 | tf_op jit(solution)/shard_map/convert_element_type | solution.py:399
  66.9 0.6 collective-permute-done.24
  67.5 1.0 %convolution_convert_fusion = bf16[256,256]{1,0:T(8,128)(2,1)} fusion(f32[512,256]{1,0:T(8,128)S(1)} %convert_add_fusion, bf16[256,256]{1,0:T(8,128)(2,1)S(1)} %collective-permute-done.24, s32[256]{0:T(256)S(1)} %iota_add_fusion, s32[256]{0:T(256)S(1)} %copy-done.1), kind=kOutput, calls=%fused_computation.2 | convolution fusion | flops 33882112 | bytes 526336 | tf_op jit(solution)/shard_map/dot_general | solution.py:41
  (41 shorter events, 0.7 us)
Async XLA Ops:
  0.6 34.1 %copy-start = (bf16[256,256]{1,0:T(8,128)(2,1)S(1)}, bf16[256,256]{1,0:T(8,128)(2,1)}, u32[]{:S(2)}) copy-start(bf16[256,256]{1,0:T(8,128)(2,1)} %param.12) | copy-start | bytes 393220
  1.9 8.2 %collective-permute-start = (bf16[256,256]{1,0:T(8,128)(2,1)S(1)}, bf16[256,256]{1,0:T(8,128)(2,1)S(1)}, u32[]{:S(2)}, u32[]{:S(2)}) collective-permute-start(bf16[256,256]{1,0:T(8,128)(2,1)S(1)} %convolution_convert_fusion.4.refs_0_), channel_id=1, source_target_pairs={{0,16},{1,17},{2,18},{3,19},{4,20},{5,21},{6,22},{7,23},{8,24},{9,... | collective-permute-start | bytes 393224 | tf_op jit(solution)/shard_map/ppermute | solution.py:315
  4.9 5.8 %collective-permute-start.1 = (bf16[256,256]{1,0:T(8,128)(2,1)S(1)}, bf16[256,256]{1,0:T(8,128)(2,1)S(1)}, u32[]{:S(2)}, u32[]{:S(2)}) collective-permute-start(bf16[256,256]{1,0:T(8,128)(2,1)S(1)} %convolution_convert_fusion.4.refs_0_), channel_id=1, source_target_pairs={{0,8},{1,9},{2,10},{3,11},{4,12},{5,13},{6,14},{7,15},{8,0},{9,1},... | collective-permute-start | bytes 393224 | tf_op jit(solution)/shard_map/ppermute | solution.py:315
  10.1 1.6 %collective-permute-start.2 = (bf16[256,256]{1,0:T(8,128)(2,1)S(1)}, bf16[256,256]{1,0:T(8,128)(2,1)S(1)}, u32[]{:S(2)}, u32[]{:S(2)}) collective-permute-start(bf16[256,256]{1,0:T(8,128)(2,1)S(1)} %compare_select_fusion.2), channel_id=1, source_target_pairs={{0,8},{1,9},{2,10},{3,11},{4,12},{5,13},{6,14},{7,15},{8,0},{9,1},... | collective-permute-start | bytes 393224 | tf_op jit(solution)/shard_map/ppermute | solution.py:315
  13.0 8.1 %collective-permute-start.7 = (bf16[256,256]{1,0:T(8,128)(2,1)S(1)}, bf16[256,256]{1,0:T(8,128)(2,1)S(1)}, u32[]{:S(2)}, u32[]{:S(2)}) collective-permute-start(bf16[256,256]{1,0:T(8,128)(2,1)S(1)} %get-tuple-element.34), channel_id=1, source_target_pairs={{0,2},{1,0},{3,1},{5,3},{7,5},{6,7},{4,6},{2,4},{10,8},{12,10},{14... | collective-permute-start | bytes 393224 | tf_op jit(solution)/shard_map/ppermute | solution.py:315
  15.2 6.1 %collective-permute-start.3 = (bf16[256,256]{1,0:T(8,128)(2,1)S(1)}, bf16[256,256]{1,0:T(8,128)(2,1)S(1)}, u32[]{:S(2)}, u32[]{:S(2)}) collective-permute-start(bf16[256,256]{1,0:T(8,128)(2,1)S(1)} %get-tuple-element.28), channel_id=1, source_target_pairs={{0,1},{1,3},{3,5},{5,7},{7,6},{6,4},{4,2},{2,0},{10,12},{12,14},{1... | collective-permute-start | bytes 393224 | tf_op jit(solution)/shard_map/ppermute | solution.py:315
  16.6 18.3 %copy-start.1 = (s32[256]{0:T(256)S(1)}, s32[256]{0:T(256)}, u32[]{:S(2)}) copy-start(s32[256]{0:T(256)} %param.8) | copy-start | bytes 3076
  16.6 18.3 %copy-start.2 = (bf16[256,256]{1,0:T(8,128)(2,1)S(1)}, bf16[256,256]{1,0:T(8,128)(2,1)}, u32[]{:S(2)}) copy-start(bf16[256,256]{1,0:T(8,128)(2,1)} %param.13) | copy-start | bytes 393220
  16.6 13.7 %collective-permute-start.4 = (bf16[256,256]{1,0:T(8,128)(2,1)S(1)}, bf16[256,256]{1,0:T(8,128)(2,1)S(1)}, u32[]{:S(2)}, u32[]{:S(2)}) collective-permute-start(bf16[256,256]{1,0:T(8,128)(2,1)S(1)} %get-tuple-element.31), channel_id=1, source_target_pairs={{0,7},{1,6},{3,4},{5,2},{7,0},{6,1},{4,3},{2,5},{10,13},{12,11},{1... | collective-permute-start | bytes 393224 | tf_op jit(solution)/shard_map/ppermute | solution.py:315
  21.2 7.0 %collective-permute-start.8 = (bf16[256,256]{1,0:T(8,128)(2,1)S(1)}, bf16[256,256]{1,0:T(8,128)(2,1)S(1)}, u32[]{:S(2)}, u32[]{:S(2)}) collective-permute-start(bf16[256,256]{1,0:T(8,128)(2,1)S(1)} %add_convert_fusion.3), channel_id=1, source_target_pairs={{0,2},{1,0},{3,1},{5,3},{7,5},{6,7},{4,6},{2,4},{10,8},{12,10},{14... | collective-permute-start | bytes 393224 | tf_op jit(solution)/shard_map/ppermute | solution.py:315
  21.3 8.0 %collective-permute-start.5 = (bf16[256,256]{1,0:T(8,128)(2,1)S(1)}, bf16[256,256]{1,0:T(8,128)(2,1)S(1)}, u32[]{:S(2)}, u32[]{:S(2)}) collective-permute-start(bf16[256,256]{1,0:T(8,128)(2,1)S(1)} %add_convert_fusion.5), channel_id=1, source_target_pairs={{0,1},{1,3},{3,5},{5,7},{7,6},{6,4},{4,2},{2,0},{10,12},{12,14},{1... | collective-permute-start | bytes 393224 | tf_op jit(solution)/shard_map/ppermute | solution.py:315
  28.2 5.5 %collective-permute-start.9 = (bf16[256,256]{1,0:T(8,128)(2,1)S(1)}, bf16[256,256]{1,0:T(8,128)(2,1)S(1)}, u32[]{:S(2)}, u32[]{:S(2)}) collective-permute-start(bf16[256,256]{1,0:T(8,128)(2,1)S(1)} %add_convert_fusion.2), channel_id=1, source_target_pairs={{0,2},{1,0},{3,1},{5,3},{7,5},{6,7},{4,6},{2,4},{10,8},{12,10},{14... | collective-permute-start | bytes 393224 | tf_op jit(solution)/shard_map/ppermute | solution.py:315
  29.4 5.3 %collective-permute-start.6 = (bf16[256,256]{1,0:T(8,128)(2,1)S(1)}, bf16[256,256]{1,0:T(8,128)(2,1)S(1)}, u32[]{:S(2)}, u32[]{:S(2)}) collective-permute-start(bf16[256,256]{1,0:T(8,128)(2,1)S(1)} %add_convert_fusion.4), channel_id=1, source_target_pairs={{0,1},{1,3},{3,5},{5,7},{7,6},{6,4},{4,2},{2,0},{10,12},{12,14},{1... | collective-permute-start | bytes 393224 | tf_op jit(solution)/shard_map/ppermute | solution.py:315
  35.4 3.8 %collective-permute-start.10 = (bf16[256,256]{1,0:T(8,128)(2,1)S(1)}, bf16[256,256]{1,0:T(8,128)(2,1)S(1)}, u32[]{:S(2)}, u32[]{:S(2)}) collective-permute-start(bf16[256,256]{1,0:T(8,128)(2,1)S(1)} %fusion), channel_id=1, source_target_pairs={{0,8},{1,9},{2,10},{3,11},{4,12},{5,13},{6,14},{7,15},{8,0},{9,1},... | collective-permute-start | bytes 393224 | tf_op jit(solution)/shard_map/ppermute | solution.py:315
  35.7 7.0 %collective-permute-start.12 = (bf16[256,256]{1,0:T(8,128)(2,1)S(1)}, bf16[256,256]{1,0:T(8,128)(2,1)S(1)}, u32[]{:S(2)}, u32[]{:S(2)}) collective-permute-start(bf16[256,256]{1,0:T(8,128)(2,1)S(1)} %convolution_convert_fusion.1.refs_0_), channel_id=1, source_target_pairs={{0,2},{1,0},{3,1},{5,3},{7,5},{6,7},{4,6},{2,4},{10,8},{12,10},{14... | collective-permute-start | bytes 393224 | tf_op jit(solution)/shard_map/ppermute | solution.py:315
  37.8 5.0 %collective-permute-start.16 = (bf16[256,256]{1,0:T(8,128)(2,1)S(1)}, bf16[256,256]{1,0:T(8,128)(2,1)S(1)}, u32[]{:S(2)}, u32[]{:S(2)}) collective-permute-start(bf16[256,256]{1,0:T(8,128)(2,1)S(1)} %convolution_convert_fusion.1.refs_0_), channel_id=1, source_target_pairs={{0,1},{1,3},{3,5},{5,7},{7,6},{6,4},{4,2},{2,0},{10,12},{12,14},{1... | collective-permute-start | bytes 393224 | tf_op jit(solution)/shard_map/ppermute | solution.py:315
  39.3 5.5 %collective-permute-start.11 = (bf16[128,256]{1,0:T(8,128)(2,1)S(1)}, bf16[128,256]{1,0:T(8,128)(2,1)S(1)}, u32[]{:S(2)}, u32[]{:S(2)}) collective-permute-start(bf16[128,256]{1,0:T(8,128)(2,1)S(1)} %slice_select_fusion), channel_id=1, source_target_pairs={{0,1},{1,0},{2,3},{3,2},{4,5},{5,4},{6,7},{7,6},{8,9},{9,8},{10,11... | collective-permute-start | bytes 196616 | tf_op jit(solution)/shard_map/ppermute | solution.py:315
  42.8 7.3 %collective-permute-start.17 = (bf16[256,256]{1,0:T(8,128)(2,1)S(1)}, bf16[256,256]{1,0:T(8,128)(2,1)S(1)}, u32[]{:S(2)}, u32[]{:S(2)}) collective-permute-start(bf16[256,256]{1,0:T(8,128)(2,1)S(1)} %collective-permute-done.16.refs_0_), channel_id=1, source_target_pairs={{0,1},{1,3},{3,5},{5,7},{7,6},{6,4},{4,2},{2,0},{10,12},{12,14},{1... | collective-permute-start | bytes 393224 | tf_op jit(solution)/shard_map/ppermute | solution.py:315
  42.8 7.3 %collective-permute-start.14 = (bf16[256,256]{1,0:T(8,128)(2,1)S(1)}, bf16[256,256]{1,0:T(8,128)(2,1)S(1)}, u32[]{:S(2)}, u32[]{:S(2)}) collective-permute-start(bf16[256,256]{1,0:T(8,128)(2,1)S(1)} %collective-permute-done.12.refs_1_), channel_id=1, source_target_pairs={{0,2},{1,0},{3,1},{5,3},{7,5},{6,7},{4,6},{2,4},{10,8},{12,10},{14... | collective-permute-start | bytes 393224 | tf_op jit(solution)/shard_map/ppermute | solution.py:315
  44.8 5.2 %collective-permute-start.13 = (bf16[128,256]{1,0:T(8,128)(2,1)S(1)}, bf16[128,256]{1,0:T(8,128)(2,1)S(1)}, u32[]{:S(2)}, u32[]{:S(2)}) collective-permute-start(bf16[128,256]{1,0:T(8,128)(2,1)S(1)} %add_convert_fusion.9), channel_id=1, source_target_pairs={{0,2},{1,3},{2,0},{3,1},{4,6},{5,7},{6,4},{7,5},{8,10},{9,11},{10,... | collective-permute-start | bytes 196616 | tf_op jit(solution)/shard_map/ppermute | solution.py:315
  46.3 8.6 %collective-permute-start.21 = (bf16[256,256]{1,0:T(8,128)(2,1)S(1)}, bf16[256,256]{1,0:T(8,128)(2,1)S(1)}, u32[]{:S(2)}, u32[]{:S(2)}) collective-permute-start(bf16[256,256]{1,0:T(8,128)(2,1)S(1)} %convolution_convert_fusion.1.refs_0_), channel_id=1, source_target_pairs={{0,7},{1,6},{3,4},{5,2},{7,0},{6,1},{4,3},{2,5},{10,13},{12,11},{1... | collective-permute-start | bytes 393224 | tf_op jit(solution)/shard_map/ppermute | solution.py:315
  50.1 6.6 %collective-permute-start.18 = (bf16[256,256]{1,0:T(8,128)(2,1)S(1)}, bf16[256,256]{1,0:T(8,128)(2,1)S(1)}, u32[]{:S(2)}, u32[]{:S(2)}) collective-permute-start(bf16[256,256]{1,0:T(8,128)(2,1)S(1)} %collective-permute-done.17.refs_0_), channel_id=1, source_target_pairs={{0,1},{1,3},{3,5},{5,7},{7,6},{6,4},{4,2},{2,0},{10,12},{12,14},{1... | collective-permute-start | bytes 393224 | tf_op jit(solution)/shard_map/ppermute | solution.py:315
  51.2 5.5 %collective-permute-start.19 = (bf16[256,256]{1,0:T(8,128)(2,1)S(1)}, bf16[256,256]{1,0:T(8,128)(2,1)S(1)}, u32[]{:S(2)}, u32[]{:S(2)}) collective-permute-start(bf16[256,256]{1,0:T(8,128)(2,1)S(1)} %collective-permute-done.14.refs_1_), channel_id=1, source_target_pairs={{0,2},{1,0},{3,1},{5,3},{7,5},{6,7},{4,6},{2,4},{10,8},{12,10},{14... | collective-permute-start | bytes 393224 | tf_op jit(solution)/shard_map/ppermute | solution.py:315
  52.1 8.2 %collective-permute-start.15 = (bf16[128,256]{1,0:T(8,128)(2,1)S(1)}, bf16[128,256]{1,0:T(8,128)(2,1)S(1)}, u32[]{:S(2)}, u32[]{:S(2)}) collective-permute-start(bf16[128,256]{1,0:T(8,128)(2,1)S(1)} %add_convert_fusion.8), channel_id=1, source_target_pairs={{0,4},{1,5},{2,6},{3,7},{4,0},{5,1},{6,2},{7,3},{8,12},{9,13},{10,... | collective-permute-start | bytes 196616 | tf_op jit(solution)/shard_map/ppermute | solution.py:315
  58.1 4.1 %collective-permute-start.22 = (bf16[512,256]{1,0:T(8,128)(2,1)S(1)}, bf16[512,256]{1,0:T(8,128)(2,1)S(1)}, u32[]{:S(2)}, u32[]{:S(2)}) collective-permute-start(bf16[512,256]{1,0:T(8,128)(2,1)S(1)} %get-tuple-element.45), channel_id=1, source_target_pairs={{0,8},{1,9},{2,10},{3,11},{4,12},{5,13},{6,14},{7,15},{8,0},{9,1},... | collective-permute-start | bytes 786440 | tf_op jit(solution)/shard_map/ppermute | solution.py:315
  60.4 4.5 %collective-permute-start.20 = (bf16[128,256]{1,0:T(8,128)(2,1)S(1)}, bf16[128,256]{1,0:T(8,128)(2,1)S(1)}, u32[]{:S(2)}, u32[]{:S(2)}) collective-permute-start(bf16[128,256]{1,0:T(8,128)(2,1)S(1)} %add_convert_fusion.7), channel_id=1, source_target_pairs={{0,16},{1,17},{2,18},{3,19},{4,20},{5,21},{6,22},{7,23},{8,24},{9,... | collective-permute-start | bytes 196616 | tf_op jit(solution)/shard_map/ppermute | solution.py:315
  62.3 5.2 %collective-permute-start.24 = (bf16[256,256]{1,0:T(8,128)(2,1)S(1)}, bf16[256,256]{1,0:T(8,128)(2,1)S(1)}, u32[]{:S(2)}, u32[]{:S(2)}) collective-permute-start(bf16[256,256]{1,0:T(8,128)(2,1)S(1)} %slice.28), channel_id=1, source_target_pairs={{0,16},{1,17},{2,18},{3,19},{4,20},{5,21},{6,22},{7,23},{8,24},{9,... | collective-permute-start | bytes 393224 | tf_op jit(solution)/shard_map/ppermute | solution.py:315
  64.9 1.3 %collective-permute-start.23 = (bf16[128,256]{1,0:T(8,128)(2,1)S(1)}, bf16[128,256]{1,0:T(8,128)(2,1)S(1)}, u32[]{:S(2)}, u32[]{:S(2)}) collective-permute-start(bf16[128,256]{1,0:T(8,128)(2,1)S(1)} %add_convert_fusion.6), channel_id=1, source_target_pairs={{0,8},{1,9},{2,10},{3,11},{4,12},{5,13},{6,14},{7,15},{8,0},{9,1},... | collective-permute-start | bytes 196616 | tf_op jit(solution)/shard_map/ppermute | solution.py:315

commit v3 on v2

--- a/solution.py
+++ b/solution.py
@@ -15,7 +15,7 @@
 PACK = 1 << PACK_BITS
 VMEM_BYTES = 16 * 1024 * 1024
 LOAD_BYTES = 45 * 1024 * 1024
-LOADS = 16
+LOADS = 4
 F32 = jnp.float32
 BF16 = jnp.bfloat16
 
@@ -354,7 +354,7 @@
     hops = ring_hops(size)
     groups = [[hop, size - hop] for hop in range(hops, 0, -1)] or [[]]
     if size % 2 == 0:
-        groups[min(1, len(groups) - 1)].insert(0, size // 2)
+        groups[0].append(size // 2)
     groups[-1].append(0)
     return groups
 
@@ -387,7 +387,7 @@
     half = held.shape[0] // CORES
     chip = (held.astype(F32) + after(got, *gate).astype(F32)).astype(BF16)
     held = jnp.where(grid.core == 0, chip[:half], chip[half:])
-    bits = [(0, 1 << k) for k in range(bits_of(grid.cols))]
+    bits = [(0, 1)] + [(0, 1 << k) for k in range(bits_of(grid.cols) - 1, 0, -1)]
     bits += [(1 << k, 0) for k in range(1, bits_of(grid.rows))]
     for row_bit, col_bit in bits:
         got = move(held, grid.across(row_bit, col_bit))

time: 68.7 us -> 72.1 us (1.049)
  waiting for transfers between devices: 18.1 us -> 21.3 us
  Pallas kernels: 13.6 us -> 16.6 us
  starting transfers between devices: 29.1 us -> 26.5 us
    pallas_call x7, Pallas kernels: 9.94 us -> 13.2 us  [tile_part(): pl.pallas_call(functools.partial(part_kernel, spec), out_shape=out_shape,...]
    ppermute x25, waiting for transfers between devices: 18.1 us -> 21.3 us  [move(): return lax.ppermute(value, ('row', 'col'), pairs)]
    ppermute x25, starting transfers between devices: 29.1 us -> 26.5 us  [move(): return lax.ppermute(value, ('row', 'col'), pairs)]
  transfers between devices with their start and end apart: 25 -> 25, of which waited for: 12 -> 11; matrix products, arithmetic and copies ran while one was open for 5% -> 4% of each run, Pallas kernels for 18% -> 20%
where the time goes in v3:
time: 72.1 us
  starting transfers between devices  26.5 us (37%)
  waiting for transfers between devices  21.3 us (30%)
  Pallas kernels  16.6 us (23%)
  matrix products  4.02 us (6%)
  other arithmetic  1.85 us (3%)
  between operations  1.67 us (2%)
    ppermute x25, starting transfers between devices, move(): return lax.ppermute(value, ('row', 'col'), pairs)  26.5 us
    ppermute x25, waiting for transfers between devices, move(): return lax.ppermute(value, ('row', 'col'), pairs)  21.3 us
    pallas_call x7, Pallas kernels, tile_part(): pl.pallas_call(functools.partial(part_kernel, spec), out_shape=out_shape,...  13.2 us
    pallas_call x1, Pallas kernels, load_tiles(): pl.pallas_call(functools.partial(load_kernel, sizes), out_shape=[jax.Shap...  3.41 us
    dot_general x2, matrix products, restore(): lax.dot_general(moves, values, (((0,), (0,)), ((), ())), preferred_elemen...  1.99 us
  transfers between devices with their start and end apart: 25, of which 11 were waited for; matrix products, arithmetic and copies ran while one was open for 4% of the time, Pallas kernels for 20%

profile of v3, /device:TPU:0, one launch (start us, length us, event | category | flops | bytes accessed | tf_op | source)
XLA Modules:
  0.0 72.1 jit_solution(2569926962698559475)
XLA Ops:
  0.7 1.2 %convolution_convert_fusion.4.refs_0_ = bf16[256,256]{1,0:T(8,128)(2,1)S(1)} fusion(bf16[256,256]{1,0:T(8,128)(2,1)} %param.7, s32[256]{0:T(256)S(1)} %iota_add_fusion, s32[256]{0:T(256)} %param.8), kind=kOutput, calls=%fused_computation.9 | convolution fusion | flops 33685504 | bytes 264192 | tf_op jit(solution)/shard_map/dot_general | solution.py:37
  1.9 3.0 %collective-permute-start = (bf16[256,256]{1,0:T(8,128)(2,1)S(1)}, bf16[256,256]{1,0:T(8,128)(2,1)S(1)}, u32[]{:S(2)}, u32[]{:S(2)}) collective-permute-start(bf16[256,256]{1,0:T(8,128)(2,1)S(1)} %convolution_convert_fusion.4.refs_0_), channel_id=1, source_target_pairs={{0,16},{1,17},{2,18},{3,19},{4,20},{5,21},{6,22},{7,23},{8,24},{9,... | collective-permute-start | bytes 393224 | tf_op jit(solution)/shard_map/ppermute | solution.py:315
  5.6 0.1 stack.43.here_ref
  5.6 0.7 pad_add_fusion.facts_ref
  6.3 3.4 %shard_map.94 = (bf16[192,128,128]{2,1,0:T(8,128)(2,1)S(1)}, s32[8,384]{1,0:T(8,128)S(1)}, s32[8,384]{1,0:T(8,128)S(1)}, bf16[256,256]{1,0:T(8,128)(2,1)S(1)}) custom-call(s32[10]{0:T(128)S(1)} %stack.43.here_ref, s32[2,256]{1,0:T(2,128)S(1)} %pad_add_fusion.facts_ref, bf16[192,128,128]{2,1,0:T(8,128)(2,1)} %bitcast.20), custom_call_target="tpu_custom_call" | custom-call | bytes 6291456 | tf_op jit(solution)/shard_map/pallas_call | solution.py:167
  9.8 0.6 collective-permute-start.2
  10.4 1.0 %collective-permute-done.2.refs_3_ = bf16[256,256]{1,0:T(8,128)(2,1)S(1)} collective-permute-done((bf16[256,256]{1,0:T(8,128)(2,1)S(1)}, bf16[256,256]{1,0:T(8,128)(2,1)S(1)}, u32[]{:S(2)}, u32[]{:S(2)}) %collective-permute-start.2) | collective-permute-done | bytes 131104 | tf_op jit(solution)/shard_map/ppermute | solution.py:315
  11.3 2.0 %shard_map.95 = (bf16[256,256]{1,0:T(8,128)(2,1)S(1)}, bf16[256,256]{1,0:T(8,128)(2,1)S(1)}, bf16[256,256]{1,0:T(8,128)(2,1)S(1)}) custom-call(s32[8,384]{1,0:T(8,128)S(1)} %get-tuple-element.29.table_ref, bf16[192,128,128]{2,1,0:T(8,128)(2,1)S(1)} %get-tuple-element.26.tiles_ref, bf16[256,256]{1,0:T(8,128)(2,1)S(1)} %convolution_convert_fusion.4.refs_0_, ...), custom_call_target="tpu_custom_call" | custom-call | flops 603979776 | bytes 2359296 | tf_op jit(solution)/shard_map/pallas_call | solution.py:247
  13.3 1.6 %collective-permute-start.7 = (bf16[256,256]{1,0:T(8,128)(2,1)S(1)}, bf16[256,256]{1,0:T(8,128)(2,1)S(1)}, u32[]{:S(2)}, u32[]{:S(2)}) collective-permute-start(bf16[256,256]{1,0:T(8,128)(2,1)S(1)} %get-tuple-element.34), channel_id=1, source_target_pairs={{0,2},{1,0},{3,1},{5,3},{7,5},{6,7},{4,6},{2,4},{10,8},{12,10},{14... | collective-permute-start | bytes 393224 | tf_op jit(solution)/shard_map/ppermute | solution.py:315
  14.9 0.5 collective-permute-start.3
  15.4 4.0 %collective-permute-start.4 = (bf16[256,256]{1,0:T(8,128)(2,1)S(1)}, bf16[256,256]{1,0:T(8,128)(2,1)S(1)}, u32[]{:S(2)}, u32[]{:S(2)}) collective-permute-start(bf16[256,256]{1,0:T(8,128)(2,1)S(1)} %get-tuple-element.31), channel_id=1, source_target_pairs={{0,7},{1,6},{3,4},{5,2},{7,0},{6,1},{4,3},{2,5},{10,13},{12,11},{1... | collective-permute-start | bytes 393224 | tf_op jit(solution)/shard_map/ppermute | solution.py:315
  19.4 1.9 %shard_map.97 = (bf16[256,256]{1,0:T(8,128)(2,1)S(1)}, bf16[256,256]{1,0:T(8,128)(2,1)S(1)}) custom-call(s32[8,384]{1,0:T(8,128)S(1)} %get-tuple-element.29.table_ref, bf16[192,128,128]{2,1,0:T(8,128)(2,1)S(1)} %get-tuple-element.26.tiles_ref, bf16[256,256]{1,0:T(8,128)(2,1)S(1)} %convolution_convert_fusion.4.refs_0_, ...), custom_call_target="tpu_custom_call" | custom-call | flops 402653184 | bytes 1572864 | tf_op jit(solution)/shard_map/pallas_call | solution.py:247
  21.4 0.1 collective-permute-start.8
  21.6 2.0 %collective-permute-start.5 = (bf16[256,256]{1,0:T(8,128)(2,1)S(1)}, bf16[256,256]{1,0:T(8,128)(2,1)S(1)}, u32[]{:S(2)}, u32[]{:S(2)}) collective-permute-start(bf16[256,256]{1,0:T(8,128)(2,1)S(1)} %add_convert_fusion.5), channel_id=1, source_target_pairs={{0,1},{1,3},{3,5},{5,7},{7,6},{6,4},{4,2},{2,0},{10,12},{12,14},{1... | collective-permute-start | bytes 393224 | tf_op jit(solution)/shard_map/ppermute | solution.py:315
  23.6 2.0 %shard_map.96 = (bf16[256,256]{1,0:T(8,128)(2,1)S(1)}, bf16[256,256]{1,0:T(8,128)(2,1)S(1)}, bf16[256,256]{1,0:T(8,128)(2,1)S(1)}) custom-call(s32[8,384]{1,0:T(8,128)S(1)} %get-tuple-element.29.table_ref, bf16[192,128,128]{2,1,0:T(8,128)(2,1)S(1)} %get-tuple-element.26.tiles_ref, bf16[256,256]{1,0:T(8,128)(2,1)S(1)} %convolution_convert_fusion.4.refs_0_, ...), custom_call_target="tpu_custom_call" | custom-call | flops 603979776 | bytes 2359296 | tf_op jit(solution)/shard_map/pallas_call | solution.py:247
  25.6 2.9 %collective-permute-done.8 = bf16[256,256]{1,0:T(8,128)(2,1)S(1)} collective-permute-done((bf16[256,256]{1,0:T(8,128)(2,1)S(1)}, bf16[256,256]{1,0:T(8,128)(2,1)S(1)}, u32[]{:S(2)}, u32[]{:S(2)}) %collective-permute-start.8) | collective-permute-done | bytes 131104 | tf_op jit(solution)/shard_map/ppermute | solution.py:315
  28.6 2.1 %collective-permute-start.6 = (bf16[256,256]{1,0:T(8,128)(2,1)S(1)}, bf16[256,256]{1,0:T(8,128)(2,1)S(1)}, u32[]{:S(2)}, u32[]{:S(2)}) collective-permute-start(bf16[256,256]{1,0:T(8,128)(2,1)S(1)} %add_convert_fusion.4), channel_id=1, source_target_pairs={{0,1},{1,3},{3,5},{5,7},{7,6},{6,4},{4,2},{2,0},{10,12},{12,14},{1... | collective-permute-start | bytes 393224 | tf_op jit(solution)/shard_map/ppermute | solution.py:315
  30.7 3.3 %collective-permute-done.9 = bf16[256,256]{1,0:T(8,128)(2,1)S(1)} collective-permute-done((bf16[256,256]{1,0:T(8,128)(2,1)S(1)}, bf16[256,256]{1,0:T(8,128)(2,1)S(1)}, u32[]{:S(2)}, u32[]{:S(2)}) %collective-permute-start.9) | collective-permute-done | bytes 131104 | tf_op jit(solution)/shard_map/ppermute | solution.py:315
  34.0 0.1 add_convert_fusion.1
  34.1 0.2 fusion.23
  34.3 0.2 fusion.3
  34.5 0.2 fusion
  34.8 0.1 collective-permute-start.10
  34.9 0.2 convolution_convert_fusion.1.refs_0_
  35.1 2.1 %collective-permute-start.12 = (bf16[256,256]{1,0:T(8,128)(2,1)S(1)}, bf16[256,256]{1,0:T(8,128)(2,1)S(1)}, u32[]{:S(2)}, u32[]{:S(2)}) collective-permute-start(bf16[256,256]{1,0:T(8,128)(2,1)S(1)} %convolution_convert_fusion.1.refs_0_), channel_id=1, source_target_pairs={{0,2},{1,0},{3,1},{5,3},{7,5},{6,7},{4,6},{2,4},{10,8},{12,10},{14... | collective-permute-start | bytes 393224 | tf_op jit(solution)/shard_map/ppermute | solution.py:315
  37.2 1.4 %shard_map.98.refs_2_ = f32[1024,256]{1,0:T(8,128)S(1)} custom-call(s32[8,384]{1,0:T(8,128)S(1)} %get-tuple-element.37.table_ref, bf16[192,128,128]{2,1,0:T(8,128)(2,1)S(1)} %get-tuple-element.26.tiles_ref, bf16[256,256]{1,0:T(8,128)(2,1)S(1)} %convolution_convert_fusion.1.refs_0_), custom_call_target="tpu_custom_call" | custom-call | flops 402653184 | bytes 1572864 | tf_op jit(solution)/shard_map/pallas_call | solution.py:247
  38.7 1.7 %collective-permute-start.11 = (bf16[128,256]{1,0:T(8,128)(2,1)S(1)}, bf16[128,256]{1,0:T(8,128)(2,1)S(1)}, u32[]{:S(2)}, u32[]{:S(2)}) collective-permute-start(bf16[128,256]{1,0:T(8,128)(2,1)S(1)} %slice_select_fusion), channel_id=1, source_target_pairs={{0,1},{1,0},{2,3},{3,2},{4,5},{5,4},{6,7},{7,6},{8,9},{9,8},{10,11... | collective-permute-start | bytes 196616 | tf_op jit(solution)/shard_map/ppermute | solution.py:315
  40.4 1.8 %collective-permute-done.16.refs_0_ = bf16[256,256]{1,0:T(8,128)(2,1)S(1)} collective-permute-done((bf16[256,256]{1,0:T(8,128)(2,1)S(1)}, bf16[256,256]{1,0:T(8,128)(2,1)S(1)}, u32[]{:S(2)}, u32[]{:S(2)}) %collective-permute-start.16) | collective-permute-done | bytes 131104 | tf_op jit(solution)/shard_map/ppermute | solution.py:315
  42.1 0.5 collective-permute-start.17
  42.7 1.5 %collective-permute-start.14 = (bf16[256,256]{1,0:T(8,128)(2,1)S(1)}, bf16[256,256]{1,0:T(8,128)(2,1)S(1)}, u32[]{:S(2)}, u32[]{:S(2)}) collective-permute-start(bf16[256,256]{1,0:T(8,128)(2,1)S(1)} %collective-permute-done.12.refs_1_), channel_id=1, source_target_pairs={{0,2},{1,0},{3,1},{5,3},{7,5},{6,7},{4,6},{2,4},{10,8},{12,10},{14... | collective-permute-start | bytes 393224 | tf_op jit(solution)/shard_map/ppermute | solution.py:315
  44.2 0.6 collective-permute-start.13
  44.8 2.9 %collective-permute-start.21 = (bf16[256,256]{1,0:T(8,128)(2,1)S(1)}, bf16[256,256]{1,0:T(8,128)(2,1)S(1)}, u32[]{:S(2)}, u32[]{:S(2)}) collective-permute-start(bf16[256,256]{1,0:T(8,128)(2,1)S(1)} %convolution_convert_fusion.1.refs_0_), channel_id=1, source_target_pairs={{0,7},{1,6},{3,4},{5,2},{7,0},{6,1},{4,3},{2,5},{10,13},{12,11},{1... | collective-permute-start | bytes 393224 | tf_op jit(solution)/shard_map/ppermute | solution.py:315
  47.7 2.0 %shard_map.99.refs_3_ = f32[1024,256]{1,0:T(8,128)S(1)} custom-call(s32[8,384]{1,0:T(8,128)S(1)} %get-tuple-element.37.table_ref, bf16[192,128,128]{2,1,0:T(8,128)(2,1)S(1)} %get-tuple-element.26.tiles_ref, bf16[256,256]{1,0:T(8,128)(2,1)S(1)} %collective-permute-done.16.refs_0_, bf16[256,256]{1,0:T(8,128)(2,1)S(1)} %collective-permute-done.12.refs_1_, ...), custom_call_target="tpu_custom_call" | custom-call | flops 402653184 | bytes 1572864 | tf_op jit(solution)/shard_map/pallas_call | solution.py:247
  49.7 4.8 %collective-permute-done.13 = bf16[128,256]{1,0:T(8,128)(2,1)S(1)} collective-permute-done((bf16[128,256]{1,0:T(8,128)(2,1)S(1)}, bf16[128,256]{1,0:T(8,128)(2,1)S(1)}, u32[]{:S(2)}, u32[]{:S(2)}) %collective-permute-start.13) | collective-permute-done | bytes 65568 | tf_op jit(solution)/shard_map/ppermute | solution.py:315
  54.5 2.3 %collective-permute-start.18 = (bf16[256,256]{1,0:T(8,128)(2,1)S(1)}, bf16[256,256]{1,0:T(8,128)(2,1)S(1)}, u32[]{:S(2)}, u32[]{:S(2)}) collective-permute-start(bf16[256,256]{1,0:T(8,128)(2,1)S(1)} %collective-permute-done.17.refs_0_), channel_id=1, source_target_pairs={{0,1},{1,3},{3,5},{5,7},{7,6},{6,4},{4,2},{2,0},{10,12},{12,14},{1... | collective-permute-start | bytes 393224 | tf_op jit(solution)/shard_map/ppermute | solution.py:315
  56.8 0.1 collective-permute-start.15
  56.9 2.0 %shard_map.100.refs_2_ = f32[1024,256]{1,0:T(8,128)S(1)} custom-call(s32[8,384]{1,0:T(8,128)S(1)} %get-tuple-element.37.table_ref, bf16[192,128,128]{2,1,0:T(8,128)(2,1)S(1)} %get-tuple-element.26.tiles_ref, bf16[256,256]{1,0:T(8,128)(2,1)S(1)} %collective-permute-done.17.refs_0_, bf16[256,256]{1,0:T(8,128)(2,1)S(1)} %collective-permute-done.14.refs_1_, ...), custom_call_target="tpu_custom_call" | custom-call | flops 402653184 | bytes 1572864 | tf_op jit(solution)/shard_map/pallas_call | solution.py:247
  58.8 0.6 collective-permute-done.18.refs_0_
  59.5 2.3 %collective-permute-done.19.refs_1_ = bf16[256,256]{1,0:T(8,128)(2,1)S(1)} collective-permute-done((bf16[256,256]{1,0:T(8,128)(2,1)S(1)}, bf16[256,256]{1,0:T(8,128)(2,1)S(1)}, u32[]{:S(2)}, u32[]{:S(2)}) %collective-permute-start.19) | collective-permute-done | bytes 131104 | tf_op jit(solution)/shard_map/ppermute | solution.py:315
  61.7 2.0 %shard_map.101 = (bf16[512,256]{1,0:T(8,128)(2,1)S(1)}, bf16[512,256]{1,0:T(8,128)(2,1)S(1)}) custom-call(s32[8,384]{1,0:T(8,128)S(1)} %get-tuple-element.37.table_ref, bf16[192,128,128]{2,1,0:T(8,128)(2,1)S(1)} %get-tuple-element.26.tiles_ref, bf16[256,256]{1,0:T(8,128)(2,1)S(1)} %collective-permute-done.18.refs_0_, ...), custom_call_target="tpu_custom_call" | custom-call | flops 402653184 | bytes 1572864 | tf_op jit(solution)/shard_map/pallas_call | solution.py:247
  63.9 1.4 %collective-permute-done.22 = bf16[512,256]{1,0:T(8,128)(2,1)S(1)} collective-permute-done((bf16[512,256]{1,0:T(8,128)(2,1)S(1)}, bf16[512,256]{1,0:T(8,128)(2,1)S(1)}, u32[]{:S(2)}, u32[]{:S(2)}) %collective-permute-start.22) | collective-permute-done | bytes 262176 | tf_op jit(solution)/shard_map/ppermute | solution.py:315
  65.4 0.7 collective-permute-start.24
  66.0 2.5 %collective-permute-done.20 = bf16[128,256]{1,0:T(8,128)(2,1)S(1)} collective-permute-done((bf16[128,256]{1,0:T(8,128)(2,1)S(1)}, bf16[128,256]{1,0:T(8,128)(2,1)S(1)}, u32[]{:S(2)}, u32[]{:S(2)}) %collective-permute-start.20) | collective-permute-done | bytes 65568 | tf_op jit(solution)/shard_map/ppermute | solution.py:315
  68.7 1.0 %convolution_convert_fusion.3 = bf16[256,256]{1,0:T(8,128)(2,1)} fusion(f32[256,256]{1,0:T(8,128)S(1)} %fusion.23, s32[256]{0:T(256)S(1)} %iota_add_fusion, s32[256]{0:T(256)S(1)} %copy-done.1), kind=kOutput, calls=%fused_computation.8 | convolution fusion | flops 33947648 | bytes 395264 | tf_op jit(solution)/shard_map/dot_general | solution.py:41
  69.7 0.2 collective-permute-done.23
  69.9 0.7 %fusion.12 = f32[256,256]{1,0:T(8,128)} fusion(bf16[128,256]{1,0:T(8,128)(2,1)S(1)} %collective-permute-done.23, bf16[128,256]{1,0:T(8,128)(2,1)S(1)} %add_convert_fusion.6, pred[]{:T(512)S(6)} %eq.67), kind=kLoop, calls=%fused_computation.29 | loop fusion | flops 655360 | bytes 393217 | tf_op jit(solution)/shard_map/convert_element_type | solution.py:399
  70.6 0.5 collective-permute-done.24
  71.2 1.0 %convolution_convert_fusion = bf16[256,256]{1,0:T(8,128)(2,1)} fusion(f32[512,256]{1,0:T(8,128)S(1)} %convert_add_fusion, bf16[256,256]{1,0:T(8,128)(2,1)S(1)} %collective-permute-done.24, s32[256]{0:T(256)S(1)} %iota_add_fusion, s32[256]{0:T(256)S(1)} %copy-done.1), kind=kOutput, calls=%fused_computation.2 | convolution fusion | flops 33882112 | bytes 526336 | tf_op jit(solution)/shard_map/dot_general | solution.py:41
  (41 shorter events, 0.7 us)
Async XLA Ops:
  0.6 33.5 %copy-start = (bf16[256,256]{1,0:T(8,128)(2,1)S(1)}, bf16[256,256]{1,0:T(8,128)(2,1)}, u32[]{:S(2)}) copy-start(bf16[256,256]{1,0:T(8,128)(2,1)} %param.12) | copy-start | bytes 393220
  1.9 7.9 %collective-permute-start = (bf16[256,256]{1,0:T(8,128)(2,1)S(1)}, bf16[256,256]{1,0:T(8,128)(2,1)S(1)}, u32[]{:S(2)}, u32[]{:S(2)}) collective-permute-start(bf16[256,256]{1,0:T(8,128)(2,1)S(1)} %convolution_convert_fusion.4.refs_0_), channel_id=1, source_target_pairs={{0,16},{1,17},{2,18},{3,19},{4,20},{5,21},{6,22},{7,23},{8,24},{9,... | collective-permute-start | bytes 393224 | tf_op jit(solution)/shard_map/ppermute | solution.py:315
  4.9 5.5 %collective-permute-start.1 = (bf16[256,256]{1,0:T(8,128)(2,1)S(1)}, bf16[256,256]{1,0:T(8,128)(2,1)S(1)}, u32[]{:S(2)}, u32[]{:S(2)}) collective-permute-start(bf16[256,256]{1,0:T(8,128)(2,1)S(1)} %convolution_convert_fusion.4.refs_0_), channel_id=1, source_target_pairs={{0,8},{1,9},{2,10},{3,11},{4,12},{5,13},{6,14},{7,15},{8,0},{9,1},... | collective-permute-start | bytes 393224 | tf_op jit(solution)/shard_map/ppermute | solution.py:315
  9.8 1.6 %collective-permute-start.2 = (bf16[256,256]{1,0:T(8,128)(2,1)S(1)}, bf16[256,256]{1,0:T(8,128)(2,1)S(1)}, u32[]{:S(2)}, u32[]{:S(2)}) collective-permute-start(bf16[256,256]{1,0:T(8,128)(2,1)S(1)} %compare_select_fusion.2), channel_id=1, source_target_pairs={{0,8},{1,9},{2,10},{3,11},{4,12},{5,13},{6,14},{7,15},{8,0},{9,1},... | collective-permute-start | bytes 393224 | tf_op jit(solution)/shard_map/ppermute | solution.py:315
  13.3 8.1 %collective-permute-start.7 = (bf16[256,256]{1,0:T(8,128)(2,1)S(1)}, bf16[256,256]{1,0:T(8,128)(2,1)S(1)}, u32[]{:S(2)}, u32[]{:S(2)}) collective-permute-start(bf16[256,256]{1,0:T(8,128)(2,1)S(1)} %get-tuple-element.34), channel_id=1, source_target_pairs={{0,2},{1,0},{3,1},{5,3},{7,5},{6,7},{4,6},{2,4},{10,8},{12,10},{14... | collective-permute-start | bytes 393224 | tf_op jit(solution)/shard_map/ppermute | solution.py:315
  14.9 6.6 %collective-permute-start.3 = (bf16[256,256]{1,0:T(8,128)(2,1)S(1)}, bf16[256,256]{1,0:T(8,128)(2,1)S(1)}, u32[]{:S(2)}, u32[]{:S(2)}) collective-permute-start(bf16[256,256]{1,0:T(8,128)(2,1)S(1)} %get-tuple-element.28), channel_id=1, source_target_pairs={{0,1},{1,3},{3,5},{5,7},{7,6},{6,4},{4,2},{2,0},{10,12},{12,14},{1... | collective-permute-start | bytes 393224 | tf_op jit(solution)/shard_map/ppermute | solution.py:315
  15.4 15.3 %collective-permute-start.4 = (bf16[256,256]{1,0:T(8,128)(2,1)S(1)}, bf16[256,256]{1,0:T(8,128)(2,1)S(1)}, u32[]{:S(2)}, u32[]{:S(2)}) collective-permute-start(bf16[256,256]{1,0:T(8,128)(2,1)S(1)} %get-tuple-element.31), channel_id=1, source_target_pairs={{0,7},{1,6},{3,4},{5,2},{7,0},{6,1},{4,3},{2,5},{10,13},{12,11},{1... | collective-permute-start | bytes 393224 | tf_op jit(solution)/shard_map/ppermute | solution.py:315
  21.3 13.0 %copy-start.1 = (s32[256]{0:T(256)S(1)}, s32[256]{0:T(256)}, u32[]{:S(2)}) copy-start(s32[256]{0:T(256)} %param.8) | copy-start | bytes 3076
  21.4 12.9 %copy-start.2 = (bf16[256,256]{1,0:T(8,128)(2,1)S(1)}, bf16[256,256]{1,0:T(8,128)(2,1)}, u32[]{:S(2)}) copy-start(bf16[256,256]{1,0:T(8,128)(2,1)} %param.13) | copy-start | bytes 393220
  21.4 7.0 %collective-permute-start.8 = (bf16[256,256]{1,0:T(8,128)(2,1)S(1)}, bf16[256,256]{1,0:T(8,128)(2,1)S(1)}, u32[]{:S(2)}, u32[]{:S(2)}) collective-permute-start(bf16[256,256]{1,0:T(8,128)(2,1)S(1)} %add_convert_fusion.3), channel_id=1, source_target_pairs={{0,2},{1,0},{3,1},{5,3},{7,5},{6,7},{4,6},{2,4},{10,8},{12,10},{14... | collective-permute-start | bytes 393224 | tf_op jit(solution)/shard_map/ppermute | solution.py:315
  21.6 7.0 %collective-permute-start.5 = (bf16[256,256]{1,0:T(8,128)(2,1)S(1)}, bf16[256,256]{1,0:T(8,128)(2,1)S(1)}, u32[]{:S(2)}, u32[]{:S(2)}) collective-permute-start(bf16[256,256]{1,0:T(8,128)(2,1)S(1)} %add_convert_fusion.5), channel_id=1, source_target_pairs={{0,1},{1,3},{3,5},{5,7},{7,6},{6,4},{4,2},{2,0},{10,12},{12,14},{1... | collective-permute-start | bytes 393224 | tf_op jit(solution)/shard_map/ppermute | solution.py:315
  28.5 5.5 %collective-permute-start.9 = (bf16[256,256]{1,0:T(8,128)(2,1)S(1)}, bf16[256,256]{1,0:T(8,128)(2,1)S(1)}, u32[]{:S(2)}, u32[]{:S(2)}) collective-permute-start(bf16[256,256]{1,0:T(8,128)(2,1)S(1)} %add_convert_fusion.2), channel_id=1, source_target_pairs={{0,2},{1,0},{3,1},{5,3},{7,5},{6,7},{4,6},{2,4},{10,8},{12,10},{14... | collective-permute-start | bytes 393224 | tf_op jit(solution)/shard_map/ppermute | solution.py:315
  28.6 5.4 %collective-permute-start.6 = (bf16[256,256]{1,0:T(8,128)(2,1)S(1)}, bf16[256,256]{1,0:T(8,128)(2,1)S(1)}, u32[]{:S(2)}, u32[]{:S(2)}) collective-permute-start(bf16[256,256]{1,0:T(8,128)(2,1)S(1)} %add_convert_fusion.4), channel_id=1, source_target_pairs={{0,1},{1,3},{3,5},{5,7},{7,6},{6,4},{4,2},{2,0},{10,12},{12,14},{1... | collective-permute-start | bytes 393224 | tf_op jit(solution)/shard_map/ppermute | solution.py:315
  34.8 3.8 %collective-permute-start.10 = (bf16[256,256]{1,0:T(8,128)(2,1)S(1)}, bf16[256,256]{1,0:T(8,128)(2,1)S(1)}, u32[]{:S(2)}, u32[]{:S(2)}) collective-permute-start(bf16[256,256]{1,0:T(8,128)(2,1)S(1)} %fusion), channel_id=1, source_target_pairs={{0,8},{1,9},{2,10},{3,11},{4,12},{5,13},{6,14},{7,15},{8,0},{9,1},... | collective-permute-start | bytes 393224 | tf_op jit(solution)/shard_map/ppermute | solution.py:315
  35.1 7.6 %collective-permute-start.12 = (bf16[256,256]{1,0:T(8,128)(2,1)S(1)}, bf16[256,256]{1,0:T(8,128)(2,1)S(1)}, u32[]{:S(2)}, u32[]{:S(2)}) collective-permute-start(bf16[256,256]{1,0:T(8,128)(2,1)S(1)} %convolution_convert_fusion.1.refs_0_), channel_id=1, source_target_pairs={{0,2},{1,0},{3,1},{5,3},{7,5},{6,7},{4,6},{2,4},{10,8},{12,10},{14... | collective-permute-start | bytes 393224 | tf_op jit(solution)/shard_map/ppermute | solution.py:315
  37.2 5.0 %collective-permute-start.16 = (bf16[256,256]{1,0:T(8,128)(2,1)S(1)}, bf16[256,256]{1,0:T(8,128)(2,1)S(1)}, u32[]{:S(2)}, u32[]{:S(2)}) collective-permute-start(bf16[256,256]{1,0:T(8,128)(2,1)S(1)} %convolution_convert_fusion.1.refs_0_), channel_id=1, source_target_pairs={{0,1},{1,3},{3,5},{5,7},{7,6},{6,4},{4,2},{2,0},{10,12},{12,14},{1... | collective-permute-start | bytes 393224 | tf_op jit(solution)/shard_map/ppermute | solution.py:315
  38.7 5.5 %collective-permute-start.11 = (bf16[128,256]{1,0:T(8,128)(2,1)S(1)}, bf16[128,256]{1,0:T(8,128)(2,1)S(1)}, u32[]{:S(2)}, u32[]{:S(2)}) collective-permute-start(bf16[128,256]{1,0:T(8,128)(2,1)S(1)} %slice_select_fusion), channel_id=1, source_target_pairs={{0,1},{1,0},{2,3},{3,2},{4,5},{5,4},{6,7},{7,6},{8,9},{9,8},{10,11... | collective-permute-start | bytes 196616 | tf_op jit(solution)/shard_map/ppermute | solution.py:315
  42.1 12.4 %collective-permute-start.17 = (bf16[256,256]{1,0:T(8,128)(2,1)S(1)}, bf16[256,256]{1,0:T(8,128)(2,1)S(1)}, u32[]{:S(2)}, u32[]{:S(2)}) collective-permute-start(bf16[256,256]{1,0:T(8,128)(2,1)S(1)} %collective-permute-done.16.refs_0_), channel_id=1, source_target_pairs={{0,1},{1,3},{3,5},{5,7},{7,6},{6,4},{4,2},{2,0},{10,12},{12,14},{1... | collective-permute-start | bytes 393224 | tf_op jit(solution)/shard_map/ppermute | solution.py:315
  42.7 11.8 %collective-permute-start.14 = (bf16[256,256]{1,0:T(8,128)(2,1)S(1)}, bf16[256,256]{1,0:T(8,128)(2,1)S(1)}, u32[]{:S(2)}, u32[]{:S(2)}) collective-permute-start(bf16[256,256]{1,0:T(8,128)(2,1)S(1)} %collective-permute-done.12.refs_1_), channel_id=1, source_target_pairs={{0,2},{1,0},{3,1},{5,3},{7,5},{6,7},{4,6},{2,4},{10,8},{12,10},{14... | collective-permute-start | bytes 393224 | tf_op jit(solution)/shard_map/ppermute | solution.py:315
  44.2 10.3 %collective-permute-start.13 = (bf16[128,256]{1,0:T(8,128)(2,1)S(1)}, bf16[128,256]{1,0:T(8,128)(2,1)S(1)}, u32[]{:S(2)}, u32[]{:S(2)}) collective-permute-start(bf16[128,256]{1,0:T(8,128)(2,1)S(1)} %add_convert_fusion.9), channel_id=1, source_target_pairs={{0,4},{1,5},{2,6},{3,7},{4,0},{5,1},{6,2},{7,3},{8,12},{9,13},{10,... | collective-permute-start | bytes 196616 | tf_op jit(solution)/shard_map/ppermute | solution.py:315
  44.8 12.0 %collective-permute-start.21 = (bf16[256,256]{1,0:T(8,128)(2,1)S(1)}, bf16[256,256]{1,0:T(8,128)(2,1)S(1)}, u32[]{:S(2)}, u32[]{:S(2)}) collective-permute-start(bf16[256,256]{1,0:T(8,128)(2,1)S(1)} %convolution_convert_fusion.1.refs_0_), channel_id=1, source_target_pairs={{0,7},{1,6},{3,4},{5,2},{7,0},{6,1},{4,3},{2,5},{10,13},{12,11},{1... | collective-permute-start | bytes 393224 | tf_op jit(solution)/shard_map/ppermute | solution.py:315
  54.5 5.0 %collective-permute-start.18 = (bf16[256,256]{1,0:T(8,128)(2,1)S(1)}, bf16[256,256]{1,0:T(8,128)(2,1)S(1)}, u32[]{:S(2)}, u32[]{:S(2)}) collective-permute-start(bf16[256,256]{1,0:T(8,128)(2,1)S(1)} %collective-permute-done.17.refs_0_), channel_id=1, source_target_pairs={{0,1},{1,3},{3,5},{5,7},{7,6},{6,4},{4,2},{2,0},{10,12},{12,14},{1... | collective-permute-start | bytes 393224 | tf_op jit(solution)/shard_map/ppermute | solution.py:315
  56.7 5.0 %collective-permute-start.19 = (bf16[256,256]{1,0:T(8,128)(2,1)S(1)}, bf16[256,256]{1,0:T(8,128)(2,1)S(1)}, u32[]{:S(2)}, u32[]{:S(2)}) collective-permute-start(bf16[256,256]{1,0:T(8,128)(2,1)S(1)} %collective-permute-done.14.refs_1_), channel_id=1, source_target_pairs={{0,2},{1,0},{3,1},{5,3},{7,5},{6,7},{4,6},{2,4},{10,8},{12,10},{14... | collective-permute-start | bytes 393224 | tf_op jit(solution)/shard_map/ppermute | solution.py:315
  56.8 7.0 %collective-permute-start.15 = (bf16[128,256]{1,0:T(8,128)(2,1)S(1)}, bf16[128,256]{1,0:T(8,128)(2,1)S(1)}, u32[]{:S(2)}, u32[]{:S(2)}) collective-permute-start(bf16[128,256]{1,0:T(8,128)(2,1)S(1)} %add_convert_fusion.8), channel_id=1, source_target_pairs={{0,2},{1,3},{2,0},{3,1},{4,6},{5,7},{6,4},{7,5},{8,10},{9,11},{10,... | collective-permute-start | bytes 196616 | tf_op jit(solution)/shard_map/ppermute | solution.py:315
  63.7 1.6 %collective-permute-start.22 = (bf16[512,256]{1,0:T(8,128)(2,1)S(1)}, bf16[512,256]{1,0:T(8,128)(2,1)S(1)}, u32[]{:S(2)}, u32[]{:S(2)}) collective-permute-start(bf16[512,256]{1,0:T(8,128)(2,1)S(1)} %get-tuple-element.45), channel_id=1, source_target_pairs={{0,8},{1,9},{2,10},{3,11},{4,12},{5,13},{6,14},{7,15},{8,0},{9,1},... | collective-permute-start | bytes 786440 | tf_op jit(solution)/shard_map/ppermute | solution.py:315
  63.8 4.8 %collective-permute-start.20 = (bf16[128,256]{1,0:T(8,128)(2,1)S(1)}, bf16[128,256]{1,0:T(8,128)(2,1)S(1)}, u32[]{:S(2)}, u32[]{:S(2)}) collective-permute-start(bf16[128,256]{1,0:T(8,128)(2,1)S(1)} %add_convert_fusion.7), channel_id=1, source_target_pairs={{0,16},{1,17},{2,18},{3,19},{4,20},{5,21},{6,22},{7,23},{8,24},{9,... | collective-permute-start | bytes 196616 | tf_op jit(solution)/shard_map/ppermute | solution.py:315
  65.4 5.8 %collective-permute-start.24 = (bf16[256,256]{1,0:T(8,128)(2,1)S(1)}, bf16[256,256]{1,0:T(8,128)(2,1)S(1)}, u32[]{:S(2)}, u32[]{:S(2)}) collective-permute-start(bf16[256,256]{1,0:T(8,128)(2,1)S(1)} %slice.28), channel_id=1, source_target_pairs={{0,16},{1,17},{2,18},{3,19},{4,20},{5,21},{6,22},{7,23},{8,24},{9,... | collective-permute-start | bytes 393224 | tf_op jit(solution)/shard_map/ppermute | solution.py:315
  68.6 1.3 %collective-permute-start.23 = (bf16[128,256]{1,0:T(8,128)(2,1)S(1)}, bf16[128,256]{1,0:T(8,128)(2,1)S(1)}, u32[]{:S(2)}, u32[]{:S(2)}) collective-permute-start(bf16[128,256]{1,0:T(8,128)(2,1)S(1)} %add_convert_fusion.6), channel_id=1, source_target_pairs={{0,8},{1,9},{2,10},{3,11},{4,12},{5,13},{6,14},{7,15},{8,0},{9,1},... | collective-permute-start | bytes 196616 | tf_op jit(solution)/shard_map/ppermute | solution.py:315

commit v4 on v3

--- a/solution.py
+++ b/solution.py
@@ -387,7 +387,7 @@
     half = held.shape[0] // CORES
     chip = (held.astype(F32) + after(got, *gate).astype(F32)).astype(BF16)
     held = jnp.where(grid.core == 0, chip[:half], chip[half:])
-    bits = [(0, 1)] + [(0, 1 << k) for k in range(bits_of(grid.cols) - 1, 0, -1)]
+    bits = [(0, 1 << k) for k in range(bits_of(grid.cols))]
     bits += [(1 << k, 0) for k in range(1, bits_of(grid.rows))]
     for row_bit, col_bit in bits:
         got = move(held, grid.across(row_bit, col_bit))

time: 72.1 us -> 67.5 us (0.936)
  waiting for transfers between devices: 21.3 us -> 18 us
  Pallas kernels: 16.6 us -> 13.4 us
  starting transfers between devices: 26.5 us -> 28.7 us
    ppermute x25, waiting for transfers between devices: 21.3 us -> 18 us  [move(): return lax.ppermute(value, ('row', 'col'), pairs)]
    pallas_call x7, Pallas kernels: 13.2 us -> 9.94 us  [tile_part(): pl.pallas_call(functools.partial(part_kernel, spec), out_shape=out_shape,...]
    ppermute x25, starting transfers between devices: 26.5 us -> 28.7 us  [move(): return lax.ppermute(value, ('row', 'col'), pairs)]
  transfers between devices with their start and end apart: 25 -> 25, of which waited for: 11 -> 10; matrix products, arithmetic and copies ran while one was open for 4% -> 5% of each run, Pallas kernels for 20% -> 18%
where the time goes in v4:
time: 67.5 us; the launch traced here: 67.7 us
  starting transfers between devices  28.7 us (43%)
  waiting for transfers between devices  18 us (27%)
  Pallas kernels  13.4 us (20%)
  matrix products  4.02 us (6%)
  other arithmetic  1.85 us (3%)
  between operations  1.63 us (2%)
    ppermute x25, starting transfers between devices, move(): return lax.ppermute(value, ('row', 'col'), pairs)  28.7 us
    ppermute x25, waiting for transfers between devices, move(): return lax.ppermute(value, ('row', 'col'), pairs)  18 us
    pallas_call x7, Pallas kernels, tile_part(): pl.pallas_call(functools.partial(part_kernel, spec), out_shape=out_shape,...  9.94 us
    pallas_call x1, Pallas kernels, load_tiles(): pl.pallas_call(functools.partial(load_kernel, sizes), out_shape=[jax.Shap...  3.41 us
    dot_general x2, matrix products, restore(): lax.dot_general(moves, values, (((0,), (0,)), ((), ())), preferred_elemen...  1.99 us
    dot_general x2, matrix products, reorder(): return jnp.dot(moves, values, preferred_element_type=F32).astype(BF16)  1.41 us
  transfers between devices with their start and end apart: 25, of which 10 were waited for; matrix products, arithmetic and copies ran while one was open for 5% of the time, Pallas kernels for 18%

profile of v4, /device:TPU:0, one launch (start us, length us, event | category | flops | bytes accessed | tf_op | source)
XLA Modules:
  0.0 67.7 jit_solution(8164671053990720709)
XLA Ops:
  0.7 1.2 %convolution_convert_fusion.4.refs_0_ = bf16[256,256]{1,0:T(8,128)(2,1)S(1)} fusion(bf16[256,256]{1,0:T(8,128)(2,1)} %param.7, s32[256]{0:T(256)S(1)} %iota_add_fusion, s32[256]{0:T(256)} %param.8), kind=kOutput, calls=%fused_computation.9 | convolution fusion | flops 33685504 | bytes 264192 | tf_op jit(solution)/shard_map/dot_general | solution.py:37
  1.9 3.0 %collective-permute-start = (bf16[256,256]{1,0:T(8,128)(2,1)S(1)}, bf16[256,256]{1,0:T(8,128)(2,1)S(1)}, u32[]{:S(2)}, u32[]{:S(2)}) collective-permute-start(bf16[256,256]{1,0:T(8,128)(2,1)S(1)} %convolution_convert_fusion.4.refs_0_), channel_id=1, source_target_pairs={{0,16},{1,17},{2,18},{3,19},{4,20},{5,21},{6,22},{7,23},{8,24},{9,... | collective-permute-start | bytes 393224 | tf_op jit(solution)/shard_map/ppermute | solution.py:315
  5.6 0.1 stack.43.here_ref
  5.6 0.7 %pad_add_fusion.facts_ref = s32[2,256]{1,0:T(2,128)S(1)} fusion(s32[1,1]{1,0:T(1,128)S(6)} %copy.10, s32[1,192]{1,0:T(1,128)} %bitcast.21), kind=kLoop, calls=%fused_computation.44 | loop fusion | flops 512 | bytes 2820 | tf_op jit(solution)/shard_map/concatenate | solution.py:165
  6.3 3.4 %shard_map.94 = (bf16[192,128,128]{2,1,0:T(8,128)(2,1)S(1)}, s32[8,384]{1,0:T(8,128)S(1)}, s32[8,384]{1,0:T(8,128)S(1)}, bf16[256,256]{1,0:T(8,128)(2,1)S(1)}) custom-call(s32[10]{0:T(128)S(1)} %stack.43.here_ref, s32[2,256]{1,0:T(2,128)S(1)} %pad_add_fusion.facts_ref, bf16[192,128,128]{2,1,0:T(8,128)(2,1)} %bitcast.20), custom_call_target="tpu_custom_call" | custom-call | bytes 6291456 | tf_op jit(solution)/shard_map/pallas_call | solution.py:167
  9.8 0.6 collective-permute-start.2
  10.4 1.0 %collective-permute-done.2.refs_3_ = bf16[256,256]{1,0:T(8,128)(2,1)S(1)} collective-permute-done((bf16[256,256]{1,0:T(8,128)(2,1)S(1)}, bf16[256,256]{1,0:T(8,128)(2,1)S(1)}, u32[]{:S(2)}, u32[]{:S(2)}) %collective-permute-start.2) | collective-permute-done | bytes 131104 | tf_op jit(solution)/shard_map/ppermute | solution.py:315
  11.3 1.4 %shard_map.95 = (bf16[256,256]{1,0:T(8,128)(2,1)S(1)}, bf16[256,256]{1,0:T(8,128)(2,1)S(1)}, bf16[256,256]{1,0:T(8,128)(2,1)S(1)}) custom-call(s32[8,384]{1,0:T(8,128)S(1)} %get-tuple-element.29.table_ref, bf16[192,128,128]{2,1,0:T(8,128)(2,1)S(1)} %get-tuple-element.26.tiles_ref, bf16[256,256]{1,0:T(8,128)(2,1)S(1)} %convolution_convert_fusion.4.refs_0_, ...), custom_call_target="tpu_custom_call" | custom-call | flops 603979776 | bytes 2359296 | tf_op jit(solution)/shard_map/pallas_call | solution.py:247
  12.8 2.2 %collective-permute-start.7 = (bf16[256,256]{1,0:T(8,128)(2,1)S(1)}, bf16[256,256]{1,0:T(8,128)(2,1)S(1)}, u32[]{:S(2)}, u32[]{:S(2)}) collective-permute-start(bf16[256,256]{1,0:T(8,128)(2,1)S(1)} %get-tuple-element.34), channel_id=1, source_target_pairs={{0,2},{1,0},{3,1},{5,3},{7,5},{6,7},{4,6},{2,4},{10,8},{12,10},{14... | collective-permute-start | bytes 393224 | tf_op jit(solution)/shard_map/ppermute | solution.py:315
  14.9 4.5 %collective-permute-start.4 = (bf16[256,256]{1,0:T(8,128)(2,1)S(1)}, bf16[256,256]{1,0:T(8,128)(2,1)S(1)}, u32[]{:S(2)}, u32[]{:S(2)}) collective-permute-start(bf16[256,256]{1,0:T(8,128)(2,1)S(1)} %get-tuple-element.31), channel_id=1, source_target_pairs={{0,7},{1,6},{3,4},{5,2},{7,0},{6,1},{4,3},{2,5},{10,13},{12,11},{1... | collective-permute-start | bytes 393224 | tf_op jit(solution)/shard_map/ppermute | solution.py:315
  19.4 1.4 %shard_map.97 = (bf16[256,256]{1,0:T(8,128)(2,1)S(1)}, bf16[256,256]{1,0:T(8,128)(2,1)S(1)}) custom-call(s32[8,384]{1,0:T(8,128)S(1)} %get-tuple-element.29.table_ref, bf16[192,128,128]{2,1,0:T(8,128)(2,1)S(1)} %get-tuple-element.26.tiles_ref, bf16[256,256]{1,0:T(8,128)(2,1)S(1)} %convolution_convert_fusion.4.refs_0_, ...), custom_call_target="tpu_custom_call" | custom-call | flops 402653184 | bytes 1572864 | tf_op jit(solution)/shard_map/pallas_call | solution.py:247
  21.0 2.1 %collective-permute-start.5 = (bf16[256,256]{1,0:T(8,128)(2,1)S(1)}, bf16[256,256]{1,0:T(8,128)(2,1)S(1)}, u32[]{:S(2)}, u32[]{:S(2)}) collective-permute-start(bf16[256,256]{1,0:T(8,128)(2,1)S(1)} %add_convert_fusion.5), channel_id=1, source_target_pairs={{0,1},{1,3},{3,5},{5,7},{7,6},{6,4},{4,2},{2,0},{10,12},{12,14},{1... | collective-permute-start | bytes 393224 | tf_op jit(solution)/shard_map/ppermute | solution.py:315
  23.0 1.4 %shard_map.96 = (bf16[256,256]{1,0:T(8,128)(2,1)S(1)}, bf16[256,256]{1,0:T(8,128)(2,1)S(1)}, bf16[256,256]{1,0:T(8,128)(2,1)S(1)}) custom-call(s32[8,384]{1,0:T(8,128)S(1)} %get-tuple-element.29.table_ref, bf16[192,128,128]{2,1,0:T(8,128)(2,1)S(1)} %get-tuple-element.26.tiles_ref, bf16[256,256]{1,0:T(8,128)(2,1)S(1)} %convolution_convert_fusion.4.refs_0_, ...), custom_call_target="tpu_custom_call" | custom-call | flops 603979776 | bytes 2359296 | tf_op jit(solution)/shard_map/pallas_call | solution.py:247
  24.5 3.3 %collective-permute-done.8 = bf16[256,256]{1,0:T(8,128)(2,1)S(1)} collective-permute-done((bf16[256,256]{1,0:T(8,128)(2,1)S(1)}, bf16[256,256]{1,0:T(8,128)(2,1)S(1)}, u32[]{:S(2)}, u32[]{:S(2)}) %collective-permute-start.8) | collective-permute-done | bytes 131104 | tf_op jit(solution)/shard_map/ppermute | solution.py:315
  27.8 0.5 collective-permute-start.9
  28.4 1.6 %collective-permute-start.6 = (bf16[256,256]{1,0:T(8,128)(2,1)S(1)}, bf16[256,256]{1,0:T(8,128)(2,1)S(1)}, u32[]{:S(2)}, u32[]{:S(2)}) collective-permute-start(bf16[256,256]{1,0:T(8,128)(2,1)S(1)} %add_convert_fusion.4), channel_id=1, source_target_pairs={{0,1},{1,3},{3,5},{5,7},{7,6},{6,4},{4,2},{2,0},{10,12},{12,14},{1... | collective-permute-start | bytes 393224 | tf_op jit(solution)/shard_map/ppermute | solution.py:315
  30.0 3.3 %collective-permute-done.9 = bf16[256,256]{1,0:T(8,128)(2,1)S(1)} collective-permute-done((bf16[256,256]{1,0:T(8,128)(2,1)S(1)}, bf16[256,256]{1,0:T(8,128)(2,1)S(1)}, u32[]{:S(2)}, u32[]{:S(2)}) %collective-permute-start.9) | collective-permute-done | bytes 131104 | tf_op jit(solution)/shard_map/ppermute | solution.py:315
  33.3 0.6 collective-permute-done.6
  33.9 0.1 add_convert_fusion.1
  34.0 0.2 fusion.23
  34.2 0.2 fusion.3
  34.4 0.2 fusion
  34.7 0.1 collective-permute-start.10
  34.7 0.2 convolution_convert_fusion.1.refs_0_
  35.0 2.1 %collective-permute-start.12 = (bf16[256,256]{1,0:T(8,128)(2,1)S(1)}, bf16[256,256]{1,0:T(8,128)(2,1)S(1)}, u32[]{:S(2)}, u32[]{:S(2)}) collective-permute-start(bf16[256,256]{1,0:T(8,128)(2,1)S(1)} %convolution_convert_fusion.1.refs_0_), channel_id=1, source_target_pairs={{0,2},{1,0},{3,1},{5,3},{7,5},{6,7},{4,6},{2,4},{10,8},{12,10},{14... | collective-permute-start | bytes 393224 | tf_op jit(solution)/shard_map/ppermute | solution.py:315
  37.1 1.4 %shard_map.98.refs_2_ = f32[1024,256]{1,0:T(8,128)S(1)} custom-call(s32[8,384]{1,0:T(8,128)S(1)} %get-tuple-element.37.table_ref, bf16[192,128,128]{2,1,0:T(8,128)(2,1)S(1)} %get-tuple-element.26.tiles_ref, bf16[256,256]{1,0:T(8,128)(2,1)S(1)} %convolution_convert_fusion.1.refs_0_), custom_call_target="tpu_custom_call" | custom-call | flops 402653184 | bytes 1572864 | tf_op jit(solution)/shard_map/pallas_call | solution.py:247
  38.6 0.6 collective-permute-start.11
  39.2 2.8 %collective-permute-done.16.refs_0_ = bf16[256,256]{1,0:T(8,128)(2,1)S(1)} collective-permute-done((bf16[256,256]{1,0:T(8,128)(2,1)S(1)}, bf16[256,256]{1,0:T(8,128)(2,1)S(1)}, u32[]{:S(2)}, u32[]{:S(2)}) %collective-permute-start.16) | collective-permute-done | bytes 131104 | tf_op jit(solution)/shard_map/ppermute | solution.py:315
  42.0 2.0 %collective-permute-start.14 = (bf16[256,256]{1,0:T(8,128)(2,1)S(1)}, bf16[256,256]{1,0:T(8,128)(2,1)S(1)}, u32[]{:S(2)}, u32[]{:S(2)}) collective-permute-start(bf16[256,256]{1,0:T(8,128)(2,1)S(1)} %collective-permute-done.12.refs_1_), channel_id=1, source_target_pairs={{0,2},{1,0},{3,1},{5,3},{7,5},{6,7},{4,6},{2,4},{10,8},{12,10},{14... | collective-permute-start | bytes 393224 | tf_op jit(solution)/shard_map/ppermute | solution.py:315
  44.1 1.0 %collective-permute-start.13 = (bf16[128,256]{1,0:T(8,128)(2,1)S(1)}, bf16[128,256]{1,0:T(8,128)(2,1)S(1)}, u32[]{:S(2)}, u32[]{:S(2)}) collective-permute-start(bf16[128,256]{1,0:T(8,128)(2,1)S(1)} %add_convert_fusion.9), channel_id=1, source_target_pairs={{0,2},{1,3},{2,0},{3,1},{4,6},{5,7},{6,4},{7,5},{8,10},{9,11},{10,... | collective-permute-start | bytes 196616 | tf_op jit(solution)/shard_map/ppermute | solution.py:315
  45.1 2.2 %collective-permute-start.21 = (bf16[256,256]{1,0:T(8,128)(2,1)S(1)}, bf16[256,256]{1,0:T(8,128)(2,1)S(1)}, u32[]{:S(2)}, u32[]{:S(2)}) collective-permute-start(bf16[256,256]{1,0:T(8,128)(2,1)S(1)} %convolution_convert_fusion.1.refs_0_), channel_id=1, source_target_pairs={{0,7},{1,6},{3,4},{5,2},{7,0},{6,1},{4,3},{2,5},{10,13},{12,11},{1... | collective-permute-start | bytes 393224 | tf_op jit(solution)/shard_map/ppermute | solution.py:315
  47.3 1.4 %shard_map.99.refs_3_ = f32[1024,256]{1,0:T(8,128)S(1)} custom-call(s32[8,384]{1,0:T(8,128)S(1)} %get-tuple-element.37.table_ref, bf16[192,128,128]{2,1,0:T(8,128)(2,1)S(1)} %get-tuple-element.26.tiles_ref, bf16[256,256]{1,0:T(8,128)(2,1)S(1)} %collective-permute-done.16.refs_0_, bf16[256,256]{1,0:T(8,128)(2,1)S(1)} %collective-permute-done.12.refs_1_, ...), custom_call_target="tpu_custom_call" | custom-call | flops 402653184 | bytes 1572864 | tf_op jit(solution)/shard_map/pallas_call | solution.py:247
  48.8 0.6 collective-permute-done.13
  49.3 0.5 collective-permute-start.18
  49.8 1.6 %collective-permute-start.19 = (bf16[256,256]{1,0:T(8,128)(2,1)S(1)}, bf16[256,256]{1,0:T(8,128)(2,1)S(1)}, u32[]{:S(2)}, u32[]{:S(2)}) collective-permute-start(bf16[256,256]{1,0:T(8,128)(2,1)S(1)} %collective-permute-done.14.refs_1_), channel_id=1, source_target_pairs={{0,2},{1,0},{3,1},{5,3},{7,5},{6,7},{4,6},{2,4},{10,8},{12,10},{14... | collective-permute-start | bytes 393224 | tf_op jit(solution)/shard_map/ppermute | solution.py:315
  51.4 1.9 %collective-permute-start.15 = (bf16[128,256]{1,0:T(8,128)(2,1)S(1)}, bf16[128,256]{1,0:T(8,128)(2,1)S(1)}, u32[]{:S(2)}, u32[]{:S(2)}) collective-permute-start(bf16[128,256]{1,0:T(8,128)(2,1)S(1)} %add_convert_fusion.8), channel_id=1, source_target_pairs={{0,4},{1,5},{2,6},{3,7},{4,0},{5,1},{6,2},{7,3},{8,12},{9,13},{10,... | collective-permute-start | bytes 196616 | tf_op jit(solution)/shard_map/ppermute | solution.py:315
  53.3 1.4 %shard_map.100.refs_2_ = f32[1024,256]{1,0:T(8,128)S(1)} custom-call(s32[8,384]{1,0:T(8,128)S(1)} %get-tuple-element.37.table_ref, bf16[192,128,128]{2,1,0:T(8,128)(2,1)S(1)} %get-tuple-element.26.tiles_ref, bf16[256,256]{1,0:T(8,128)(2,1)S(1)} %collective-permute-done.17.refs_0_, bf16[256,256]{1,0:T(8,128)(2,1)S(1)} %collective-permute-done.14.refs_1_, ...), custom_call_target="tpu_custom_call" | custom-call | flops 402653184 | bytes 1572864 | tf_op jit(solution)/shard_map/pallas_call | solution.py:247
  54.7 1.3 %collective-permute-done.18.refs_0_ = bf16[256,256]{1,0:T(8,128)(2,1)S(1)} collective-permute-done((bf16[256,256]{1,0:T(8,128)(2,1)S(1)}, bf16[256,256]{1,0:T(8,128)(2,1)S(1)}, u32[]{:S(2)}, u32[]{:S(2)}) %collective-permute-start.18) | collective-permute-done | bytes 131104 | tf_op jit(solution)/shard_map/ppermute | solution.py:315
  56.0 1.4 %shard_map.101 = (bf16[512,256]{1,0:T(8,128)(2,1)S(1)}, bf16[512,256]{1,0:T(8,128)(2,1)S(1)}) custom-call(s32[8,384]{1,0:T(8,128)S(1)} %get-tuple-element.37.table_ref, bf16[192,128,128]{2,1,0:T(8,128)(2,1)S(1)} %get-tuple-element.26.tiles_ref, bf16[256,256]{1,0:T(8,128)(2,1)S(1)} %collective-permute-done.18.refs_0_, ...), custom_call_target="tpu_custom_call" | custom-call | flops 402653184 | bytes 1572864 | tf_op jit(solution)/shard_map/pallas_call | solution.py:247
  57.4 0.1 collective-permute-start.22
  57.5 2.0 %collective-permute-done.15 = bf16[128,256]{1,0:T(8,128)(2,1)S(1)} collective-permute-done((bf16[128,256]{1,0:T(8,128)(2,1)S(1)}, bf16[128,256]{1,0:T(8,128)(2,1)S(1)}, u32[]{:S(2)}, u32[]{:S(2)}) %collective-permute-start.15) | collective-permute-done | bytes 65568 | tf_op jit(solution)/shard_map/ppermute | solution.py:315
  59.6 0.3 collective-permute-start.20
  59.9 1.9 %collective-permute-start.24 = (bf16[256,256]{1,0:T(8,128)(2,1)S(1)}, bf16[256,256]{1,0:T(8,128)(2,1)S(1)}, u32[]{:S(2)}, u32[]{:S(2)}) collective-permute-start(bf16[256,256]{1,0:T(8,128)(2,1)S(1)} %slice.28), channel_id=1, source_target_pairs={{0,16},{1,17},{2,18},{3,19},{4,20},{5,21},{6,22},{7,23},{8,24},{9,... | collective-permute-start | bytes 393224 | tf_op jit(solution)/shard_map/ppermute | solution.py:315
  61.8 2.8 %collective-permute-done.20 = bf16[128,256]{1,0:T(8,128)(2,1)S(1)} collective-permute-done((bf16[128,256]{1,0:T(8,128)(2,1)S(1)}, bf16[128,256]{1,0:T(8,128)(2,1)S(1)}, u32[]{:S(2)}, u32[]{:S(2)}) %collective-permute-start.20) | collective-permute-done | bytes 65568 | tf_op jit(solution)/shard_map/ppermute | solution.py:315
  64.7 1.0 %convolution_convert_fusion.3 = bf16[256,256]{1,0:T(8,128)(2,1)} fusion(f32[256,256]{1,0:T(8,128)S(1)} %fusion.23, s32[256]{0:T(256)S(1)} %iota_add_fusion, s32[256]{0:T(256)S(1)} %copy-done.1), kind=kOutput, calls=%fused_computation.8 | convolution fusion | flops 33947648 | bytes 395264 | tf_op jit(solution)/shard_map/dot_general | solution.py:41
  65.7 0.2 collective-permute-done.23
  66.0 0.7 %fusion.12 = f32[256,256]{1,0:T(8,128)} fusion(bf16[128,256]{1,0:T(8,128)(2,1)S(1)} %collective-permute-done.23, bf16[128,256]{1,0:T(8,128)(2,1)S(1)} %add_convert_fusion.6, pred[]{:T(512)S(6)} %eq.67), kind=kLoop, calls=%fused_computation.29 | loop fusion | flops 655360 | bytes 393217 | tf_op jit(solution)/shard_map/convert_element_type | solution.py:399
  66.7 1.0 %convolution_convert_fusion = bf16[256,256]{1,0:T(8,128)(2,1)} fusion(f32[512,256]{1,0:T(8,128)S(1)} %convert_add_fusion, bf16[256,256]{1,0:T(8,128)(2,1)S(1)} %collective-permute-done.24, s32[256]{0:T(256)S(1)} %iota_add_fusion, s32[256]{0:T(256)S(1)} %copy-done.1), kind=kOutput, calls=%fused_computation.2 | convolution fusion | flops 33882112 | bytes 526336 | tf_op jit(solution)/shard_map/dot_general | solution.py:41
  (41 shorter events, 0.6 us)
Async XLA Ops:
  0.6 33.4 %copy-start = (bf16[256,256]{1,0:T(8,128)(2,1)S(1)}, bf16[256,256]{1,0:T(8,128)(2,1)}, u32[]{:S(2)}) copy-start(bf16[256,256]{1,0:T(8,128)(2,1)} %param.12) | copy-start | bytes 393220
  1.9 7.9 %collective-permute-start = (bf16[256,256]{1,0:T(8,128)(2,1)S(1)}, bf16[256,256]{1,0:T(8,128)(2,1)S(1)}, u32[]{:S(2)}, u32[]{:S(2)}) collective-permute-start(bf16[256,256]{1,0:T(8,128)(2,1)S(1)} %convolution_convert_fusion.4.refs_0_), channel_id=1, source_target_pairs={{0,16},{1,17},{2,18},{3,19},{4,20},{5,21},{6,22},{7,23},{8,24},{9,... | collective-permute-start | bytes 393224 | tf_op jit(solution)/shard_map/ppermute | solution.py:315
  4.9 5.5 %collective-permute-start.1 = (bf16[256,256]{1,0:T(8,128)(2,1)S(1)}, bf16[256,256]{1,0:T(8,128)(2,1)S(1)}, u32[]{:S(2)}, u32[]{:S(2)}) collective-permute-start(bf16[256,256]{1,0:T(8,128)(2,1)S(1)} %convolution_convert_fusion.4.refs_0_), channel_id=1, source_target_pairs={{0,8},{1,9},{2,10},{3,11},{4,12},{5,13},{6,14},{7,15},{8,0},{9,1},... | collective-permute-start | bytes 393224 | tf_op jit(solution)/shard_map/ppermute | solution.py:315
  9.8 1.6 %collective-permute-start.2 = (bf16[256,256]{1,0:T(8,128)(2,1)S(1)}, bf16[256,256]{1,0:T(8,128)(2,1)S(1)}, u32[]{:S(2)}, u32[]{:S(2)}) collective-permute-start(bf16[256,256]{1,0:T(8,128)(2,1)S(1)} %compare_select_fusion.2), channel_id=1, source_target_pairs={{0,8},{1,9},{2,10},{3,11},{4,12},{5,13},{6,14},{7,15},{8,0},{9,1},... | collective-permute-start | bytes 393224 | tf_op jit(solution)/shard_map/ppermute | solution.py:315
  12.8 8.1 %collective-permute-start.7 = (bf16[256,256]{1,0:T(8,128)(2,1)S(1)}, bf16[256,256]{1,0:T(8,128)(2,1)S(1)}, u32[]{:S(2)}, u32[]{:S(2)}) collective-permute-start(bf16[256,256]{1,0:T(8,128)(2,1)S(1)} %get-tuple-element.34), channel_id=1, source_target_pairs={{0,2},{1,0},{3,1},{5,3},{7,5},{6,7},{4,6},{2,4},{10,8},{12,10},{14... | collective-permute-start | bytes 393224 | tf_op jit(solution)/shard_map/ppermute | solution.py:315
  14.9 6.0 %collective-permute-start.3 = (bf16[256,256]{1,0:T(8,128)(2,1)S(1)}, bf16[256,256]{1,0:T(8,128)(2,1)S(1)}, u32[]{:S(2)}, u32[]{:S(2)}) collective-permute-start(bf16[256,256]{1,0:T(8,128)(2,1)S(1)} %get-tuple-element.28), channel_id=1, source_target_pairs={{0,1},{1,3},{3,5},{5,7},{7,6},{6,4},{4,2},{2,0},{10,12},{12,14},{1... | collective-permute-start | bytes 393224 | tf_op jit(solution)/shard_map/ppermute | solution.py:315
  14.9 15.1 %collective-permute-start.4 = (bf16[256,256]{1,0:T(8,128)(2,1)S(1)}, bf16[256,256]{1,0:T(8,128)(2,1)S(1)}, u32[]{:S(2)}, u32[]{:S(2)}) collective-permute-start(bf16[256,256]{1,0:T(8,128)(2,1)S(1)} %get-tuple-element.31), channel_id=1, source_target_pairs={{0,7},{1,6},{3,4},{5,2},{7,0},{6,1},{4,3},{2,5},{10,13},{12,11},{1... | collective-permute-start | bytes 393224 | tf_op jit(solution)/shard_map/ppermute | solution.py:315
  20.8 13.4 %copy-start.1 = (s32[256]{0:T(256)S(1)}, s32[256]{0:T(256)}, u32[]{:S(2)}) copy-start(s32[256]{0:T(256)} %param.8) | copy-start | bytes 3076
  20.8 13.4 %copy-start.2 = (bf16[256,256]{1,0:T(8,128)(2,1)S(1)}, bf16[256,256]{1,0:T(8,128)(2,1)}, u32[]{:S(2)}) copy-start(bf16[256,256]{1,0:T(8,128)(2,1)} %param.13) | copy-start | bytes 393220
  20.9 6.9 %collective-permute-start.8 = (bf16[256,256]{1,0:T(8,128)(2,1)S(1)}, bf16[256,256]{1,0:T(8,128)(2,1)S(1)}, u32[]{:S(2)}, u32[]{:S(2)}) collective-permute-start(bf16[256,256]{1,0:T(8,128)(2,1)S(1)} %add_convert_fusion.3), channel_id=1, source_target_pairs={{0,2},{1,0},{3,1},{5,3},{7,5},{6,7},{4,6},{2,4},{10,8},{12,10},{14... | collective-permute-start | bytes 393224 | tf_op jit(solution)/shard_map/ppermute | solution.py:315
  21.0 7.4 %collective-permute-start.5 = (bf16[256,256]{1,0:T(8,128)(2,1)S(1)}, bf16[256,256]{1,0:T(8,128)(2,1)S(1)}, u32[]{:S(2)}, u32[]{:S(2)}) collective-permute-start(bf16[256,256]{1,0:T(8,128)(2,1)S(1)} %add_convert_fusion.5), channel_id=1, source_target_pairs={{0,1},{1,3},{3,5},{5,7},{7,6},{6,4},{4,2},{2,0},{10,12},{12,14},{1... | collective-permute-start | bytes 393224 | tf_op jit(solution)/shard_map/ppermute | solution.py:315
  27.8 5.5 %collective-permute-start.9 = (bf16[256,256]{1,0:T(8,128)(2,1)S(1)}, bf16[256,256]{1,0:T(8,128)(2,1)S(1)}, u32[]{:S(2)}, u32[]{:S(2)}) collective-permute-start(bf16[256,256]{1,0:T(8,128)(2,1)S(1)} %add_convert_fusion.2), channel_id=1, source_target_pairs={{0,2},{1,0},{3,1},{5,3},{7,5},{6,7},{4,6},{2,4},{10,8},{12,10},{14... | collective-permute-start | bytes 393224 | tf_op jit(solution)/shard_map/ppermute | solution.py:315
  28.4 5.5 %collective-permute-start.6 = (bf16[256,256]{1,0:T(8,128)(2,1)S(1)}, bf16[256,256]{1,0:T(8,128)(2,1)S(1)}, u32[]{:S(2)}, u32[]{:S(2)}) collective-permute-start(bf16[256,256]{1,0:T(8,128)(2,1)S(1)} %add_convert_fusion.4), channel_id=1, source_target_pairs={{0,1},{1,3},{3,5},{5,7},{7,6},{6,4},{4,2},{2,0},{10,12},{12,14},{1... | collective-permute-start | bytes 393224 | tf_op jit(solution)/shard_map/ppermute | solution.py:315
  34.7 3.8 %collective-permute-start.10 = (bf16[256,256]{1,0:T(8,128)(2,1)S(1)}, bf16[256,256]{1,0:T(8,128)(2,1)S(1)}, u32[]{:S(2)}, u32[]{:S(2)}) collective-permute-start(bf16[256,256]{1,0:T(8,128)(2,1)S(1)} %fusion), channel_id=1, source_target_pairs={{0,8},{1,9},{2,10},{3,11},{4,12},{5,13},{6,14},{7,15},{8,0},{9,1},... | collective-permute-start | bytes 393224 | tf_op jit(solution)/shard_map/ppermute | solution.py:315
  35.0 7.0 %collective-permute-start.12 = (bf16[256,256]{1,0:T(8,128)(2,1)S(1)}, bf16[256,256]{1,0:T(8,128)(2,1)S(1)}, u32[]{:S(2)}, u32[]{:S(2)}) collective-permute-start(bf16[256,256]{1,0:T(8,128)(2,1)S(1)} %convolution_convert_fusion.1.refs_0_), channel_id=1, source_target_pairs={{0,2},{1,0},{3,1},{5,3},{7,5},{6,7},{4,6},{2,4},{10,8},{12,10},{14... | collective-permute-start | bytes 393224 | tf_op jit(solution)/shard_map/ppermute | solution.py:315
  37.0 5.0 %collective-permute-start.16 = (bf16[256,256]{1,0:T(8,128)(2,1)S(1)}, bf16[256,256]{1,0:T(8,128)(2,1)S(1)}, u32[]{:S(2)}, u32[]{:S(2)}) collective-permute-start(bf16[256,256]{1,0:T(8,128)(2,1)S(1)} %convolution_convert_fusion.1.refs_0_), channel_id=1, source_target_pairs={{0,1},{1,3},{3,5},{5,7},{7,6},{6,4},{4,2},{2,0},{10,12},{12,14},{1... | collective-permute-start | bytes 393224 | tf_op jit(solution)/shard_map/ppermute | solution.py:315
  38.6 5.5 %collective-permute-start.11 = (bf16[128,256]{1,0:T(8,128)(2,1)S(1)}, bf16[128,256]{1,0:T(8,128)(2,1)S(1)}, u32[]{:S(2)}, u32[]{:S(2)}) collective-permute-start(bf16[128,256]{1,0:T(8,128)(2,1)S(1)} %slice_select_fusion), channel_id=1, source_target_pairs={{0,1},{1,0},{2,3},{3,2},{4,5},{5,4},{6,7},{7,6},{8,9},{9,8},{10,11... | collective-permute-start | bytes 196616 | tf_op jit(solution)/shard_map/ppermute | solution.py:315
  42.0 7.3 %collective-permute-start.17 = (bf16[256,256]{1,0:T(8,128)(2,1)S(1)}, bf16[256,256]{1,0:T(8,128)(2,1)S(1)}, u32[]{:S(2)}, u32[]{:S(2)}) collective-permute-start(bf16[256,256]{1,0:T(8,128)(2,1)S(1)} %collective-permute-done.16.refs_0_), channel_id=1, source_target_pairs={{0,1},{1,3},{3,5},{5,7},{7,6},{6,4},{4,2},{2,0},{10,12},{12,14},{1... | collective-permute-start | bytes 393224 | tf_op jit(solution)/shard_map/ppermute | solution.py:315
  42.0 7.3 %collective-permute-start.14 = (bf16[256,256]{1,0:T(8,128)(2,1)S(1)}, bf16[256,256]{1,0:T(8,128)(2,1)S(1)}, u32[]{:S(2)}, u32[]{:S(2)}) collective-permute-start(bf16[256,256]{1,0:T(8,128)(2,1)S(1)} %collective-permute-done.12.refs_1_), channel_id=1, source_target_pairs={{0,2},{1,0},{3,1},{5,3},{7,5},{6,7},{4,6},{2,4},{10,8},{12,10},{14... | collective-permute-start | bytes 393224 | tf_op jit(solution)/shard_map/ppermute | solution.py:315
  44.1 5.2 %collective-permute-start.13 = (bf16[128,256]{1,0:T(8,128)(2,1)S(1)}, bf16[128,256]{1,0:T(8,128)(2,1)S(1)}, u32[]{:S(2)}, u32[]{:S(2)}) collective-permute-start(bf16[128,256]{1,0:T(8,128)(2,1)S(1)} %add_convert_fusion.9), channel_id=1, source_target_pairs={{0,2},{1,3},{2,0},{3,1},{4,6},{5,7},{6,4},{7,5},{8,10},{9,11},{10,... | collective-permute-start | bytes 196616 | tf_op jit(solution)/shard_map/ppermute | solution.py:315
  45.1 8.2 %collective-permute-start.21 = (bf16[256,256]{1,0:T(8,128)(2,1)S(1)}, bf16[256,256]{1,0:T(8,128)(2,1)S(1)}, u32[]{:S(2)}, u32[]{:S(2)}) collective-permute-start(bf16[256,256]{1,0:T(8,128)(2,1)S(1)} %convolution_convert_fusion.1.refs_0_), channel_id=1, source_target_pairs={{0,7},{1,6},{3,4},{5,2},{7,0},{6,1},{4,3},{2,5},{10,13},{12,11},{1... | collective-permute-start | bytes 393224 | tf_op jit(solution)/shard_map/ppermute | solution.py:315
  49.3 6.7 %collective-permute-start.18 = (bf16[256,256]{1,0:T(8,128)(2,1)S(1)}, bf16[256,256]{1,0:T(8,128)(2,1)S(1)}, u32[]{:S(2)}, u32[]{:S(2)}) collective-permute-start(bf16[256,256]{1,0:T(8,128)(2,1)S(1)} %collective-permute-done.17.refs_0_), channel_id=1, source_target_pairs={{0,1},{1,3},{3,5},{5,7},{7,6},{6,4},{4,2},{2,0},{10,12},{12,14},{1... | collective-permute-start | bytes 393224 | tf_op jit(solution)/shard_map/ppermute | solution.py:315
  49.8 6.2 %collective-permute-start.19 = (bf16[256,256]{1,0:T(8,128)(2,1)S(1)}, bf16[256,256]{1,0:T(8,128)(2,1)S(1)}, u32[]{:S(2)}, u32[]{:S(2)}) collective-permute-start(bf16[256,256]{1,0:T(8,128)(2,1)S(1)} %collective-permute-done.14.refs_1_), channel_id=1, source_target_pairs={{0,2},{1,0},{3,1},{5,3},{7,5},{6,7},{4,6},{2,4},{10,8},{12,10},{14... | collective-permute-start | bytes 393224 | tf_op jit(solution)/shard_map/ppermute | solution.py:315
  51.4 8.2 %collective-permute-start.15 = (bf16[128,256]{1,0:T(8,128)(2,1)S(1)}, bf16[128,256]{1,0:T(8,128)(2,1)S(1)}, u32[]{:S(2)}, u32[]{:S(2)}) collective-permute-start(bf16[128,256]{1,0:T(8,128)(2,1)S(1)} %add_convert_fusion.8), channel_id=1, source_target_pairs={{0,4},{1,5},{2,6},{3,7},{4,0},{5,1},{6,2},{7,3},{8,12},{9,13},{10,... | collective-permute-start | bytes 196616 | tf_op jit(solution)/shard_map/ppermute | solution.py:315
  57.4 2.4 %collective-permute-start.22 = (bf16[512,256]{1,0:T(8,128)(2,1)S(1)}, bf16[512,256]{1,0:T(8,128)(2,1)S(1)}, u32[]{:S(2)}, u32[]{:S(2)}) collective-permute-start(bf16[512,256]{1,0:T(8,128)(2,1)S(1)} %get-tuple-element.45), channel_id=1, source_target_pairs={{0,8},{1,9},{2,10},{3,11},{4,12},{5,13},{6,14},{7,15},{8,0},{9,1},... | collective-permute-start | bytes 786440 | tf_op jit(solution)/shard_map/ppermute | solution.py:315
  59.6 5.1 %collective-permute-start.20 = (bf16[128,256]{1,0:T(8,128)(2,1)S(1)}, bf16[128,256]{1,0:T(8,128)(2,1)S(1)}, u32[]{:S(2)}, u32[]{:S(2)}) collective-permute-start(bf16[128,256]{1,0:T(8,128)(2,1)S(1)} %add_convert_fusion.7), channel_id=1, source_target_pairs={{0,16},{1,17},{2,18},{3,19},{4,20},{5,21},{6,22},{7,23},{8,24},{9,... | collective-permute-start | bytes 196616 | tf_op jit(solution)/shard_map/ppermute | solution.py:315
  59.9 6.8 %collective-permute-start.24 = (bf16[256,256]{1,0:T(8,128)(2,1)S(1)}, bf16[256,256]{1,0:T(8,128)(2,1)S(1)}, u32[]{:S(2)}, u32[]{:S(2)}) collective-permute-start(bf16[256,256]{1,0:T(8,128)(2,1)S(1)} %slice.28), channel_id=1, source_target_pairs={{0,16},{1,17},{2,18},{3,19},{4,20},{5,21},{6,22},{7,23},{8,24},{9,... | collective-permute-start | bytes 393224 | tf_op jit(solution)/shard_map/ppermute | solution.py:315
  64.7 1.3 %collective-permute-start.23 = (bf16[128,256]{1,0:T(8,128)(2,1)S(1)}, bf16[128,256]{1,0:T(8,128)(2,1)S(1)}, u32[]{:S(2)}, u32[]{:S(2)}) collective-permute-start(bf16[128,256]{1,0:T(8,128)(2,1)S(1)} %add_convert_fusion.6), channel_id=1, source_target_pairs={{0,8},{1,9},{2,10},{3,11},{4,12},{5,13},{6,14},{7,15},{8,0},{9,1},... | collective-permute-start | bytes 196616 | tf_op jit(solution)/shard_map/ppermute | solution.py:315

commit v5 on v4

--- a/solution.py
+++ b/solution.py
@@ -388,6 +388,7 @@
     chip = (held.astype(F32) + after(got, *gate).astype(F32)).astype(BF16)
     held = jnp.where(grid.core == 0, chip[:half], chip[half:])
     bits = [(0, 1 << k) for k in range(bits_of(grid.cols))]
+    bits[:2] = bits[1::-1]
     bits += [(1 << k, 0) for k in range(1, bits_of(grid.rows))]
     for row_bit, col_bit in bits:
         got = move(held, grid.across(row_bit, col_bit))

time: 67.5 us -> 67.3 us (level)
  waiting for transfers between devices: 18 us -> 16.9 us
    ppermute x25, waiting for transfers between devices: 18 us -> 16.9 us  [move(): return lax.ppermute(value, ('row', 'col'), pairs)]
  transfers between devices with their start and end apart: 25 -> 25, of which waited for: 10 -> 9; matrix products, arithmetic and copies ran while one was open for 5% -> 5% of each run, Pallas kernels for 18% -> 18%
where the time goes in v5:
time: 67.3 us; the launch traced here: 67.1 us
  starting transfers between devices  29.2 us (43%)
  waiting for transfers between devices  16.9 us (25%)
  Pallas kernels  13.4 us (20%)
  matrix products  4.02 us (6%)
  other arithmetic  1.85 us (3%)
  between operations  1.67 us (2%)
    ppermute x25, starting transfers between devices, move(): return lax.ppermute(value, ('row', 'col'), pairs)  29.2 us
    ppermute x25, waiting for transfers between devices, move(): return lax.ppermute(value, ('row', 'col'), pairs)  16.9 us
    pallas_call x7, Pallas kernels, tile_part(): pl.pallas_call(functools.partial(part_kernel, spec), out_shape=out_shape,...  9.94 us
    pallas_call x1, Pallas kernels, load_tiles(): pl.pallas_call(functools.partial(load_kernel, sizes), out_shape=[jax.Shap...  3.41 us
    dot_general x2, matrix products, restore(): lax.dot_general(moves, values, (((0,), (0,)), ((), ())), preferred_elemen...  1.99 us
    dot_general x2, matrix products, reorder(): return jnp.dot(moves, values, preferred_element_type=F32).astype(BF16)  1.41 us
  transfers between devices with their start and end apart: 25, of which 9 were waited for; matrix products, arithmetic and copies ran while one was open for 5% of the time, Pallas kernels for 18%

profile of v5, /device:TPU:0, one launch (start us, length us, event | category | flops | bytes accessed | tf_op | source)
XLA Modules:
  0.0 67.1 jit_solution(8994042331334471425)
XLA Ops:
  0.7 1.2 %convolution_convert_fusion.4.refs_0_ = bf16[256,256]{1,0:T(8,128)(2,1)S(1)} fusion(bf16[256,256]{1,0:T(8,128)(2,1)} %param.7, s32[256]{0:T(256)S(1)} %iota_add_fusion, s32[256]{0:T(256)} %param.8), kind=kOutput, calls=%fused_computation.9 | convolution fusion | flops 33685504 | bytes 264192 | tf_op jit(solution)/shard_map/dot_general | solution.py:37
  1.9 3.0 %collective-permute-start = (bf16[256,256]{1,0:T(8,128)(2,1)S(1)}, bf16[256,256]{1,0:T(8,128)(2,1)S(1)}, u32[]{:S(2)}, u32[]{:S(2)}) collective-permute-start(bf16[256,256]{1,0:T(8,128)(2,1)S(1)} %convolution_convert_fusion.4.refs_0_), channel_id=1, source_target_pairs={{0,16},{1,17},{2,18},{3,19},{4,20},{5,21},{6,22},{7,23},{8,24},{9,... | collective-permute-start | bytes 393224 | tf_op jit(solution)/shard_map/ppermute | solution.py:315
  5.6 0.1 stack.43.here_ref
  5.6 0.7 %pad_add_fusion.facts_ref = s32[2,256]{1,0:T(2,128)S(1)} fusion(s32[1,1]{1,0:T(1,128)S(6)} %copy.10, s32[1,192]{1,0:T(1,128)} %bitcast.21), kind=kLoop, calls=%fused_computation.44 | loop fusion | flops 512 | bytes 2820 | tf_op jit(solution)/shard_map/concatenate | solution.py:165
  6.3 3.4 %shard_map.94 = (bf16[192,128,128]{2,1,0:T(8,128)(2,1)S(1)}, s32[8,384]{1,0:T(8,128)S(1)}, s32[8,384]{1,0:T(8,128)S(1)}, bf16[256,256]{1,0:T(8,128)(2,1)S(1)}) custom-call(s32[10]{0:T(128)S(1)} %stack.43.here_ref, s32[2,256]{1,0:T(2,128)S(1)} %pad_add_fusion.facts_ref, bf16[192,128,128]{2,1,0:T(8,128)(2,1)} %bitcast.20), custom_call_target="tpu_custom_call" | custom-call | bytes 6291456 | tf_op jit(solution)/shard_map/pallas_call | solution.py:167
  9.8 0.6 collective-permute-start.2
  10.4 1.0 %collective-permute-done.2.refs_3_ = bf16[256,256]{1,0:T(8,128)(2,1)S(1)} collective-permute-done((bf16[256,256]{1,0:T(8,128)(2,1)S(1)}, bf16[256,256]{1,0:T(8,128)(2,1)S(1)}, u32[]{:S(2)}, u32[]{:S(2)}) %collective-permute-start.2) | collective-permute-done | bytes 131104 | tf_op jit(solution)/shard_map/ppermute | solution.py:315
  11.3 1.4 %shard_map.95 = (bf16[256,256]{1,0:T(8,128)(2,1)S(1)}, bf16[256,256]{1,0:T(8,128)(2,1)S(1)}, bf16[256,256]{1,0:T(8,128)(2,1)S(1)}) custom-call(s32[8,384]{1,0:T(8,128)S(1)} %get-tuple-element.29.table_ref, bf16[192,128,128]{2,1,0:T(8,128)(2,1)S(1)} %get-tuple-element.26.tiles_ref, bf16[256,256]{1,0:T(8,128)(2,1)S(1)} %convolution_convert_fusion.4.refs_0_, ...), custom_call_target="tpu_custom_call" | custom-call | flops 603979776 | bytes 2359296 | tf_op jit(solution)/shard_map/pallas_call | solution.py:247
  12.8 1.6 %collective-permute-start.7 = (bf16[256,256]{1,0:T(8,128)(2,1)S(1)}, bf16[256,256]{1,0:T(8,128)(2,1)S(1)}, u32[]{:S(2)}, u32[]{:S(2)}) collective-permute-start(bf16[256,256]{1,0:T(8,128)(2,1)S(1)} %get-tuple-element.34), channel_id=1, source_target_pairs={{0,2},{1,0},{3,1},{5,3},{7,5},{6,7},{4,6},{2,4},{10,8},{12,10},{14... | collective-permute-start | bytes 393224 | tf_op jit(solution)/shard_map/ppermute | solution.py:315
  14.4 0.6 collective-permute-start.3
  14.9 4.5 %collective-permute-start.4 = (bf16[256,256]{1,0:T(8,128)(2,1)S(1)}, bf16[256,256]{1,0:T(8,128)(2,1)S(1)}, u32[]{:S(2)}, u32[]{:S(2)}) collective-permute-start(bf16[256,256]{1,0:T(8,128)(2,1)S(1)} %get-tuple-element.31), channel_id=1, source_target_pairs={{0,7},{1,6},{3,4},{5,2},{7,0},{6,1},{4,3},{2,5},{10,13},{12,11},{1... | collective-permute-start | bytes 393224 | tf_op jit(solution)/shard_map/ppermute | solution.py:315
  19.4 1.4 %shard_map.97 = (bf16[256,256]{1,0:T(8,128)(2,1)S(1)}, bf16[256,256]{1,0:T(8,128)(2,1)S(1)}) custom-call(s32[8,384]{1,0:T(8,128)S(1)} %get-tuple-element.29.table_ref, bf16[192,128,128]{2,1,0:T(8,128)(2,1)S(1)} %get-tuple-element.26.tiles_ref, bf16[256,256]{1,0:T(8,128)(2,1)S(1)} %convolution_convert_fusion.4.refs_0_, ...), custom_call_target="tpu_custom_call" | custom-call | flops 402653184 | bytes 1572864 | tf_op jit(solution)/shard_map/pallas_call | solution.py:247
  20.9 0.7 %collective-permute-start.8 = (bf16[256,256]{1,0:T(8,128)(2,1)S(1)}, bf16[256,256]{1,0:T(8,128)(2,1)S(1)}, u32[]{:S(2)}, u32[]{:S(2)}) collective-permute-start(bf16[256,256]{1,0:T(8,128)(2,1)S(1)} %add_convert_fusion.3), channel_id=1, source_target_pairs={{0,2},{1,0},{3,1},{5,3},{7,5},{6,7},{4,6},{2,4},{10,8},{12,10},{14... | collective-permute-start | bytes 393224 | tf_op jit(solution)/shard_map/ppermute | solution.py:315
  21.6 1.4 %collective-permute-start.5 = (bf16[256,256]{1,0:T(8,128)(2,1)S(1)}, bf16[256,256]{1,0:T(8,128)(2,1)S(1)}, u32[]{:S(2)}, u32[]{:S(2)}) collective-permute-start(bf16[256,256]{1,0:T(8,128)(2,1)S(1)} %add_convert_fusion.5), channel_id=1, source_target_pairs={{0,1},{1,3},{3,5},{5,7},{7,6},{6,4},{4,2},{2,0},{10,12},{12,14},{1... | collective-permute-start | bytes 393224 | tf_op jit(solution)/shard_map/ppermute | solution.py:315
  23.0 1.4 %shard_map.96 = (bf16[256,256]{1,0:T(8,128)(2,1)S(1)}, bf16[256,256]{1,0:T(8,128)(2,1)S(1)}, bf16[256,256]{1,0:T(8,128)(2,1)S(1)}) custom-call(s32[8,384]{1,0:T(8,128)S(1)} %get-tuple-element.29.table_ref, bf16[192,128,128]{2,1,0:T(8,128)(2,1)S(1)} %get-tuple-element.26.tiles_ref, bf16[256,256]{1,0:T(8,128)(2,1)S(1)} %convolution_convert_fusion.4.refs_0_, ...), custom_call_target="tpu_custom_call" | custom-call | flops 603979776 | bytes 2359296 | tf_op jit(solution)/shard_map/pallas_call | solution.py:247
  24.5 4.1 %collective-permute-done.8 = bf16[256,256]{1,0:T(8,128)(2,1)S(1)} collective-permute-done((bf16[256,256]{1,0:T(8,128)(2,1)S(1)}, bf16[256,256]{1,0:T(8,128)(2,1)S(1)}, u32[]{:S(2)}, u32[]{:S(2)}) %collective-permute-start.8) | collective-permute-done | bytes 131104 | tf_op jit(solution)/shard_map/ppermute | solution.py:315
  28.7 2.1 %collective-permute-start.6 = (bf16[256,256]{1,0:T(8,128)(2,1)S(1)}, bf16[256,256]{1,0:T(8,128)(2,1)S(1)}, u32[]{:S(2)}, u32[]{:S(2)}) collective-permute-start(bf16[256,256]{1,0:T(8,128)(2,1)S(1)} %add_convert_fusion.4), channel_id=1, source_target_pairs={{0,1},{1,3},{3,5},{5,7},{7,6},{6,4},{4,2},{2,0},{10,12},{12,14},{1... | collective-permute-start | bytes 393224 | tf_op jit(solution)/shard_map/ppermute | solution.py:315
  30.8 3.3 %collective-permute-done.9 = bf16[256,256]{1,0:T(8,128)(2,1)S(1)} collective-permute-done((bf16[256,256]{1,0:T(8,128)(2,1)S(1)}, bf16[256,256]{1,0:T(8,128)(2,1)S(1)}, u32[]{:S(2)}, u32[]{:S(2)}) %collective-permute-start.9) | collective-permute-done | bytes 131104 | tf_op jit(solution)/shard_map/ppermute | solution.py:315
  34.1 0.1 add_convert_fusion.1
  34.2 0.2 fusion.23
  34.4 0.2 fusion.3
  34.6 0.2 fusion
  34.9 0.2 convolution_convert_fusion.1.refs_0_
  35.2 1.5 %collective-permute-start.12 = (bf16[256,256]{1,0:T(8,128)(2,1)S(1)}, bf16[256,256]{1,0:T(8,128)(2,1)S(1)}, u32[]{:S(2)}, u32[]{:S(2)}) collective-permute-start(bf16[256,256]{1,0:T(8,128)(2,1)S(1)} %convolution_convert_fusion.1.refs_0_), channel_id=1, source_target_pairs={{0,2},{1,0},{3,1},{5,3},{7,5},{6,7},{4,6},{2,4},{10,8},{12,10},{14... | collective-permute-start | bytes 393224 | tf_op jit(solution)/shard_map/ppermute | solution.py:315
  36.6 0.6 collective-permute-start.16
  37.2 1.4 %shard_map.98.refs_2_ = f32[1024,256]{1,0:T(8,128)S(1)} custom-call(s32[8,384]{1,0:T(8,128)S(1)} %get-tuple-element.37.table_ref, bf16[192,128,128]{2,1,0:T(8,128)(2,1)S(1)} %get-tuple-element.26.tiles_ref, bf16[256,256]{1,0:T(8,128)(2,1)S(1)} %convolution_convert_fusion.1.refs_0_), custom_call_target="tpu_custom_call" | custom-call | flops 402653184 | bytes 1572864 | tf_op jit(solution)/shard_map/pallas_call | solution.py:247
  38.8 1.5 %collective-permute-start.11 = (bf16[128,256]{1,0:T(8,128)(2,1)S(1)}, bf16[128,256]{1,0:T(8,128)(2,1)S(1)}, u32[]{:S(2)}, u32[]{:S(2)}) collective-permute-start(bf16[128,256]{1,0:T(8,128)(2,1)S(1)} %slice_select_fusion), channel_id=1, source_target_pairs={{0,2},{1,3},{2,0},{3,1},{4,6},{5,7},{6,4},{7,5},{8,10},{9,11},{10,... | collective-permute-start | bytes 196616 | tf_op jit(solution)/shard_map/ppermute | solution.py:315
  40.2 1.6 %collective-permute-done.16.refs_0_ = bf16[256,256]{1,0:T(8,128)(2,1)S(1)} collective-permute-done((bf16[256,256]{1,0:T(8,128)(2,1)S(1)}, bf16[256,256]{1,0:T(8,128)(2,1)S(1)}, u32[]{:S(2)}, u32[]{:S(2)}) %collective-permute-start.16) | collective-permute-done | bytes 131104 | tf_op jit(solution)/shard_map/ppermute | solution.py:315
  41.8 1.0 %collective-permute-start.17 = (bf16[256,256]{1,0:T(8,128)(2,1)S(1)}, bf16[256,256]{1,0:T(8,128)(2,1)S(1)}, u32[]{:S(2)}, u32[]{:S(2)}) collective-permute-start(bf16[256,256]{1,0:T(8,128)(2,1)S(1)} %collective-permute-done.16.refs_0_), channel_id=1, source_target_pairs={{0,1},{1,3},{3,5},{5,7},{7,6},{6,4},{4,2},{2,0},{10,12},{12,14},{1... | collective-permute-start | bytes 393224 | tf_op jit(solution)/shard_map/ppermute | solution.py:315
  42.8 1.0 %collective-permute-start.14 = (bf16[256,256]{1,0:T(8,128)(2,1)S(1)}, bf16[256,256]{1,0:T(8,128)(2,1)S(1)}, u32[]{:S(2)}, u32[]{:S(2)}) collective-permute-start(bf16[256,256]{1,0:T(8,128)(2,1)S(1)} %collective-permute-done.12.refs_1_), channel_id=1, source_target_pairs={{0,2},{1,0},{3,1},{5,3},{7,5},{6,7},{4,6},{2,4},{10,8},{12,10},{14... | collective-permute-start | bytes 393224 | tf_op jit(solution)/shard_map/ppermute | solution.py:315
  43.9 1.0 %collective-permute-start.13 = (bf16[128,256]{1,0:T(8,128)(2,1)S(1)}, bf16[128,256]{1,0:T(8,128)(2,1)S(1)}, u32[]{:S(2)}, u32[]{:S(2)}) collective-permute-start(bf16[128,256]{1,0:T(8,128)(2,1)S(1)} %add_convert_fusion.9), channel_id=1, source_target_pairs={{0,1},{1,0},{2,3},{3,2},{4,5},{5,4},{6,7},{7,6},{8,9},{9,8},{10,11... | collective-permute-start | bytes 196616 | tf_op jit(solution)/shard_map/ppermute | solution.py:315
  44.9 2.7 %collective-permute-start.21 = (bf16[256,256]{1,0:T(8,128)(2,1)S(1)}, bf16[256,256]{1,0:T(8,128)(2,1)S(1)}, u32[]{:S(2)}, u32[]{:S(2)}) collective-permute-start(bf16[256,256]{1,0:T(8,128)(2,1)S(1)} %convolution_convert_fusion.1.refs_0_), channel_id=1, source_target_pairs={{0,7},{1,6},{3,4},{5,2},{7,0},{6,1},{4,3},{2,5},{10,13},{12,11},{1... | collective-permute-start | bytes 393224 | tf_op jit(solution)/shard_map/ppermute | solution.py:315
  47.6 1.4 %shard_map.99.refs_3_ = f32[1024,256]{1,0:T(8,128)S(1)} custom-call(s32[8,384]{1,0:T(8,128)S(1)} %get-tuple-element.37.table_ref, bf16[192,128,128]{2,1,0:T(8,128)(2,1)S(1)} %get-tuple-element.26.tiles_ref, bf16[256,256]{1,0:T(8,128)(2,1)S(1)} %collective-permute-done.16.refs_0_, bf16[256,256]{1,0:T(8,128)(2,1)S(1)} %collective-permute-done.12.refs_1_, ...), custom_call_target="tpu_custom_call" | custom-call | flops 402653184 | bytes 1572864 | tf_op jit(solution)/shard_map/pallas_call | solution.py:247
  49.1 2.0 %collective-permute-start.18 = (bf16[256,256]{1,0:T(8,128)(2,1)S(1)}, bf16[256,256]{1,0:T(8,128)(2,1)S(1)}, u32[]{:S(2)}, u32[]{:S(2)}) collective-permute-start(bf16[256,256]{1,0:T(8,128)(2,1)S(1)} %collective-permute-done.17.refs_0_), channel_id=1, source_target_pairs={{0,1},{1,3},{3,5},{5,7},{7,6},{6,4},{4,2},{2,0},{10,12},{12,14},{1... | collective-permute-start | bytes 393224 | tf_op jit(solution)/shard_map/ppermute | solution.py:315
  51.1 0.1 collective-permute-start.19
  51.2 0.9 %collective-permute-start.15 = (bf16[128,256]{1,0:T(8,128)(2,1)S(1)}, bf16[128,256]{1,0:T(8,128)(2,1)S(1)}, u32[]{:S(2)}, u32[]{:S(2)}) collective-permute-start(bf16[128,256]{1,0:T(8,128)(2,1)S(1)} %add_convert_fusion.8), channel_id=1, source_target_pairs={{0,4},{1,5},{2,6},{3,7},{4,0},{5,1},{6,2},{7,3},{8,12},{9,13},{10,... | collective-permute-start | bytes 196616 | tf_op jit(solution)/shard_map/ppermute | solution.py:315
  52.1 1.9 %collective-permute-done.21.refs_2_ = bf16[256,256]{1,0:T(8,128)(2,1)S(1)} collective-permute-done((bf16[256,256]{1,0:T(8,128)(2,1)S(1)}, bf16[256,256]{1,0:T(8,128)(2,1)S(1)}, u32[]{:S(2)}, u32[]{:S(2)}) %collective-permute-start.21) | collective-permute-done | bytes 131104 | tf_op jit(solution)/shard_map/ppermute | solution.py:315
  54.0 1.4 %shard_map.100.refs_2_ = f32[1024,256]{1,0:T(8,128)S(1)} custom-call(s32[8,384]{1,0:T(8,128)S(1)} %get-tuple-element.37.table_ref, bf16[192,128,128]{2,1,0:T(8,128)(2,1)S(1)} %get-tuple-element.26.tiles_ref, bf16[256,256]{1,0:T(8,128)(2,1)S(1)} %collective-permute-done.17.refs_0_, bf16[256,256]{1,0:T(8,128)(2,1)S(1)} %collective-permute-done.14.refs_1_, ...), custom_call_target="tpu_custom_call" | custom-call | flops 402653184 | bytes 1572864 | tf_op jit(solution)/shard_map/pallas_call | solution.py:247
  55.5 0.6 collective-permute-done.19.refs_1_
  56.1 1.4 %shard_map.101 = (bf16[512,256]{1,0:T(8,128)(2,1)S(1)}, bf16[512,256]{1,0:T(8,128)(2,1)S(1)}) custom-call(s32[8,384]{1,0:T(8,128)S(1)} %get-tuple-element.37.table_ref, bf16[192,128,128]{2,1,0:T(8,128)(2,1)S(1)} %get-tuple-element.26.tiles_ref, bf16[256,256]{1,0:T(8,128)(2,1)S(1)} %collective-permute-done.18.refs_0_, ...), custom_call_target="tpu_custom_call" | custom-call | flops 402653184 | bytes 1572864 | tf_op jit(solution)/shard_map/pallas_call | solution.py:247
  57.6 1.4 %collective-permute-done.15 = bf16[128,256]{1,0:T(8,128)(2,1)S(1)} collective-permute-done((bf16[128,256]{1,0:T(8,128)(2,1)S(1)}, bf16[128,256]{1,0:T(8,128)(2,1)S(1)}, u32[]{:S(2)}, u32[]{:S(2)}) %collective-permute-start.15) | collective-permute-done | bytes 65568 | tf_op jit(solution)/shard_map/ppermute | solution.py:315
  59.0 0.8 %collective-permute-start.20 = (bf16[128,256]{1,0:T(8,128)(2,1)S(1)}, bf16[128,256]{1,0:T(8,128)(2,1)S(1)}, u32[]{:S(2)}, u32[]{:S(2)}) collective-permute-start(bf16[128,256]{1,0:T(8,128)(2,1)S(1)} %add_convert_fusion.7), channel_id=1, source_target_pairs={{0,16},{1,17},{2,18},{3,19},{4,20},{5,21},{6,22},{7,23},{8,24},{9,... | collective-permute-start | bytes 196616 | tf_op jit(solution)/shard_map/ppermute | solution.py:315
  59.9 1.4 %collective-permute-start.24 = (bf16[256,256]{1,0:T(8,128)(2,1)S(1)}, bf16[256,256]{1,0:T(8,128)(2,1)S(1)}, u32[]{:S(2)}, u32[]{:S(2)}) collective-permute-start(bf16[256,256]{1,0:T(8,128)(2,1)S(1)} %slice.28), channel_id=1, source_target_pairs={{0,16},{1,17},{2,18},{3,19},{4,20},{5,21},{6,22},{7,23},{8,24},{9,... | collective-permute-start | bytes 393224 | tf_op jit(solution)/shard_map/ppermute | solution.py:315
  61.3 2.7 %collective-permute-done.20 = bf16[128,256]{1,0:T(8,128)(2,1)S(1)} collective-permute-done((bf16[128,256]{1,0:T(8,128)(2,1)S(1)}, bf16[128,256]{1,0:T(8,128)(2,1)S(1)}, u32[]{:S(2)}, u32[]{:S(2)}) %collective-permute-start.20) | collective-permute-done | bytes 65568 | tf_op jit(solution)/shard_map/ppermute | solution.py:315
  64.1 1.0 %convolution_convert_fusion.3 = bf16[256,256]{1,0:T(8,128)(2,1)} fusion(f32[256,256]{1,0:T(8,128)S(1)} %fusion.23, s32[256]{0:T(256)S(1)} %iota_add_fusion, s32[256]{0:T(256)S(1)} %copy-done.1), kind=kOutput, calls=%fused_computation.8 | convolution fusion | flops 33947648 | bytes 395264 | tf_op jit(solution)/shard_map/dot_general | solution.py:41
  65.1 0.2 collective-permute-done.23
  65.4 0.7 %fusion.12 = f32[256,256]{1,0:T(8,128)} fusion(bf16[128,256]{1,0:T(8,128)(2,1)S(1)} %collective-permute-done.23, bf16[128,256]{1,0:T(8,128)(2,1)S(1)} %add_convert_fusion.6, pred[]{:T(512)S(6)} %eq.67), kind=kLoop, calls=%fused_computation.29 | loop fusion | flops 655360 | bytes 393217 | tf_op jit(solution)/shard_map/convert_element_type | solution.py:400
  66.1 1.0 %convolution_convert_fusion = bf16[256,256]{1,0:T(8,128)(2,1)} fusion(f32[512,256]{1,0:T(8,128)S(1)} %convert_add_fusion, bf16[256,256]{1,0:T(8,128)(2,1)S(1)} %collective-permute-done.24, s32[256]{0:T(256)S(1)} %iota_add_fusion, s32[256]{0:T(256)S(1)} %copy-done.1), kind=kOutput, calls=%fused_computation.2 | convolution fusion | flops 33882112 | bytes 526336 | tf_op jit(solution)/shard_map/dot_general | solution.py:41
  (41 shorter events, 0.7 us)
Async XLA Ops:
  0.6 33.5 %copy-start = (bf16[256,256]{1,0:T(8,128)(2,1)S(1)}, bf16[256,256]{1,0:T(8,128)(2,1)}, u32[]{:S(2)}) copy-start(bf16[256,256]{1,0:T(8,128)(2,1)} %param.12) | copy-start | bytes 393220
  1.9 7.9 %collective-permute-start = (bf16[256,256]{1,0:T(8,128)(2,1)S(1)}, bf16[256,256]{1,0:T(8,128)(2,1)S(1)}, u32[]{:S(2)}, u32[]{:S(2)}) collective-permute-start(bf16[256,256]{1,0:T(8,128)(2,1)S(1)} %convolution_convert_fusion.4.refs_0_), channel_id=1, source_target_pairs={{0,16},{1,17},{2,18},{3,19},{4,20},{5,21},{6,22},{7,23},{8,24},{9,... | collective-permute-start | bytes 393224 | tf_op jit(solution)/shard_map/ppermute | solution.py:315
  4.9 5.5 %collective-permute-start.1 = (bf16[256,256]{1,0:T(8,128)(2,1)S(1)}, bf16[256,256]{1,0:T(8,128)(2,1)S(1)}, u32[]{:S(2)}, u32[]{:S(2)}) collective-permute-start(bf16[256,256]{1,0:T(8,128)(2,1)S(1)} %convolution_convert_fusion.4.refs_0_), channel_id=1, source_target_pairs={{0,8},{1,9},{2,10},{3,11},{4,12},{5,13},{6,14},{7,15},{8,0},{9,1},... | collective-permute-start | bytes 393224 | tf_op jit(solution)/shard_map/ppermute | solution.py:315
  9.8 1.6 %collective-permute-start.2 = (bf16[256,256]{1,0:T(8,128)(2,1)S(1)}, bf16[256,256]{1,0:T(8,128)(2,1)S(1)}, u32[]{:S(2)}, u32[]{:S(2)}) collective-permute-start(bf16[256,256]{1,0:T(8,128)(2,1)S(1)} %compare_select_fusion.2), channel_id=1, source_target_pairs={{0,8},{1,9},{2,10},{3,11},{4,12},{5,13},{6,14},{7,15},{8,0},{9,1},... | collective-permute-start | bytes 393224 | tf_op jit(solution)/shard_map/ppermute | solution.py:315
  12.8 8.1 %collective-permute-start.7 = (bf16[256,256]{1,0:T(8,128)(2,1)S(1)}, bf16[256,256]{1,0:T(8,128)(2,1)S(1)}, u32[]{:S(2)}, u32[]{:S(2)}) collective-permute-start(bf16[256,256]{1,0:T(8,128)(2,1)S(1)} %get-tuple-element.34), channel_id=1, source_target_pairs={{0,2},{1,0},{3,1},{5,3},{7,5},{6,7},{4,6},{2,4},{10,8},{12,10},{14... | collective-permute-start | bytes 393224 | tf_op jit(solution)/shard_map/ppermute | solution.py:315
  14.4 7.2 %collective-permute-start.3 = (bf16[256,256]{1,0:T(8,128)(2,1)S(1)}, bf16[256,256]{1,0:T(8,128)(2,1)S(1)}, u32[]{:S(2)}, u32[]{:S(2)}) collective-permute-start(bf16[256,256]{1,0:T(8,128)(2,1)S(1)} %get-tuple-element.28), channel_id=1, source_target_pairs={{0,1},{1,3},{3,5},{5,7},{7,6},{6,4},{4,2},{2,0},{10,12},{12,14},{1... | collective-permute-start | bytes 393224 | tf_op jit(solution)/shard_map/ppermute | solution.py:315
  14.9 15.8 %collective-permute-start.4 = (bf16[256,256]{1,0:T(8,128)(2,1)S(1)}, bf16[256,256]{1,0:T(8,128)(2,1)S(1)}, u32[]{:S(2)}, u32[]{:S(2)}) collective-permute-start(bf16[256,256]{1,0:T(8,128)(2,1)S(1)} %get-tuple-element.31), channel_id=1, source_target_pairs={{0,7},{1,6},{3,4},{5,2},{7,0},{6,1},{4,3},{2,5},{10,13},{12,11},{1... | collective-permute-start | bytes 393224 | tf_op jit(solution)/shard_map/ppermute | solution.py:315
  20.8 13.6 %copy-start.1 = (s32[256]{0:T(256)S(1)}, s32[256]{0:T(256)}, u32[]{:S(2)}) copy-start(s32[256]{0:T(256)} %param.8) | copy-start | bytes 3076
  20.8 13.6 %copy-start.2 = (bf16[256,256]{1,0:T(8,128)(2,1)S(1)}, bf16[256,256]{1,0:T(8,128)(2,1)}, u32[]{:S(2)}) copy-start(bf16[256,256]{1,0:T(8,128)(2,1)} %param.13) | copy-start | bytes 393220
  20.9 7.7 %collective-permute-start.8 = (bf16[256,256]{1,0:T(8,128)(2,1)S(1)}, bf16[256,256]{1,0:T(8,128)(2,1)S(1)}, u32[]{:S(2)}, u32[]{:S(2)}) collective-permute-start(bf16[256,256]{1,0:T(8,128)(2,1)S(1)} %add_convert_fusion.3), channel_id=1, source_target_pairs={{0,2},{1,0},{3,1},{5,3},{7,5},{6,7},{4,6},{2,4},{10,8},{12,10},{14... | collective-permute-start | bytes 393224 | tf_op jit(solution)/shard_map/ppermute | solution.py:315
  21.6 7.1 %collective-permute-start.5 = (bf16[256,256]{1,0:T(8,128)(2,1)S(1)}, bf16[256,256]{1,0:T(8,128)(2,1)S(1)}, u32[]{:S(2)}, u32[]{:S(2)}) collective-permute-start(bf16[256,256]{1,0:T(8,128)(2,1)S(1)} %add_convert_fusion.5), channel_id=1, source_target_pairs={{0,1},{1,3},{3,5},{5,7},{7,6},{6,4},{4,2},{2,0},{10,12},{12,14},{1... | collective-permute-start | bytes 393224 | tf_op jit(solution)/shard_map/ppermute | solution.py:315
  28.6 5.5 %collective-permute-start.9 = (bf16[256,256]{1,0:T(8,128)(2,1)S(1)}, bf16[256,256]{1,0:T(8,128)(2,1)S(1)}, u32[]{:S(2)}, u32[]{:S(2)}) collective-permute-start(bf16[256,256]{1,0:T(8,128)(2,1)S(1)} %add_convert_fusion.2), channel_id=1, source_target_pairs={{0,2},{1,0},{3,1},{5,3},{7,5},{6,7},{4,6},{2,4},{10,8},{12,10},{14... | collective-permute-start | bytes 393224 | tf_op jit(solution)/shard_map/ppermute | solution.py:315
  28.7 5.3 %collective-permute-start.6 = (bf16[256,256]{1,0:T(8,128)(2,1)S(1)}, bf16[256,256]{1,0:T(8,128)(2,1)S(1)}, u32[]{:S(2)}, u32[]{:S(2)}) collective-permute-start(bf16[256,256]{1,0:T(8,128)(2,1)S(1)} %add_convert_fusion.4), channel_id=1, source_target_pairs={{0,1},{1,3},{3,5},{5,7},{7,6},{6,4},{4,2},{2,0},{10,12},{12,14},{1... | collective-permute-start | bytes 393224 | tf_op jit(solution)/shard_map/ppermute | solution.py:315
  34.8 3.8 %collective-permute-start.10 = (bf16[256,256]{1,0:T(8,128)(2,1)S(1)}, bf16[256,256]{1,0:T(8,128)(2,1)S(1)}, u32[]{:S(2)}, u32[]{:S(2)}) collective-permute-start(bf16[256,256]{1,0:T(8,128)(2,1)S(1)} %fusion), channel_id=1, source_target_pairs={{0,8},{1,9},{2,10},{3,11},{4,12},{5,13},{6,14},{7,15},{8,0},{9,1},... | collective-permute-start | bytes 393224 | tf_op jit(solution)/shard_map/ppermute | solution.py:315
  35.2 7.6 %collective-permute-start.12 = (bf16[256,256]{1,0:T(8,128)(2,1)S(1)}, bf16[256,256]{1,0:T(8,128)(2,1)S(1)}, u32[]{:S(2)}, u32[]{:S(2)}) collective-permute-start(bf16[256,256]{1,0:T(8,128)(2,1)S(1)} %convolution_convert_fusion.1.refs_0_), channel_id=1, source_target_pairs={{0,2},{1,0},{3,1},{5,3},{7,5},{6,7},{4,6},{2,4},{10,8},{12,10},{14... | collective-permute-start | bytes 393224 | tf_op jit(solution)/shard_map/ppermute | solution.py:315
  36.6 5.2 %collective-permute-start.16 = (bf16[256,256]{1,0:T(8,128)(2,1)S(1)}, bf16[256,256]{1,0:T(8,128)(2,1)S(1)}, u32[]{:S(2)}, u32[]{:S(2)}) collective-permute-start(bf16[256,256]{1,0:T(8,128)(2,1)S(1)} %convolution_convert_fusion.1.refs_0_), channel_id=1, source_target_pairs={{0,1},{1,3},{3,5},{5,7},{7,6},{6,4},{4,2},{2,0},{10,12},{12,14},{1... | collective-permute-start | bytes 393224 | tf_op jit(solution)/shard_map/ppermute | solution.py:315
  38.8 5.1 %collective-permute-start.11 = (bf16[128,256]{1,0:T(8,128)(2,1)S(1)}, bf16[128,256]{1,0:T(8,128)(2,1)S(1)}, u32[]{:S(2)}, u32[]{:S(2)}) collective-permute-start(bf16[128,256]{1,0:T(8,128)(2,1)S(1)} %slice_select_fusion), channel_id=1, source_target_pairs={{0,2},{1,3},{2,0},{3,1},{4,6},{5,7},{6,4},{7,5},{8,10},{9,11},{10,... | collective-permute-start | bytes 196616 | tf_op jit(solution)/shard_map/ppermute | solution.py:315
  41.8 7.3 %collective-permute-start.17 = (bf16[256,256]{1,0:T(8,128)(2,1)S(1)}, bf16[256,256]{1,0:T(8,128)(2,1)S(1)}, u32[]{:S(2)}, u32[]{:S(2)}) collective-permute-start(bf16[256,256]{1,0:T(8,128)(2,1)S(1)} %collective-permute-done.16.refs_0_), channel_id=1, source_target_pairs={{0,1},{1,3},{3,5},{5,7},{7,6},{6,4},{4,2},{2,0},{10,12},{12,14},{1... | collective-permute-start | bytes 393224 | tf_op jit(solution)/shard_map/ppermute | solution.py:315
  42.8 6.3 %collective-permute-start.14 = (bf16[256,256]{1,0:T(8,128)(2,1)S(1)}, bf16[256,256]{1,0:T(8,128)(2,1)S(1)}, u32[]{:S(2)}, u32[]{:S(2)}) collective-permute-start(bf16[256,256]{1,0:T(8,128)(2,1)S(1)} %collective-permute-done.12.refs_1_), channel_id=1, source_target_pairs={{0,2},{1,0},{3,1},{5,3},{7,5},{6,7},{4,6},{2,4},{10,8},{12,10},{14... | collective-permute-start | bytes 393224 | tf_op jit(solution)/shard_map/ppermute | solution.py:315
  43.9 5.2 %collective-permute-start.13 = (bf16[128,256]{1,0:T(8,128)(2,1)S(1)}, bf16[128,256]{1,0:T(8,128)(2,1)S(1)}, u32[]{:S(2)}, u32[]{:S(2)}) collective-permute-start(bf16[128,256]{1,0:T(8,128)(2,1)S(1)} %add_convert_fusion.9), channel_id=1, source_target_pairs={{0,1},{1,0},{2,3},{3,2},{4,5},{5,4},{6,7},{7,6},{8,9},{9,8},{10,11... | collective-permute-start | bytes 196616 | tf_op jit(solution)/shard_map/ppermute | solution.py:315
  44.9 9.1 %collective-permute-start.21 = (bf16[256,256]{1,0:T(8,128)(2,1)S(1)}, bf16[256,256]{1,0:T(8,128)(2,1)S(1)}, u32[]{:S(2)}, u32[]{:S(2)}) collective-permute-start(bf16[256,256]{1,0:T(8,128)(2,1)S(1)} %convolution_convert_fusion.1.refs_0_), channel_id=1, source_target_pairs={{0,7},{1,6},{3,4},{5,2},{7,0},{6,1},{4,3},{2,5},{10,13},{12,11},{1... | collective-permute-start | bytes 393224 | tf_op jit(solution)/shard_map/ppermute | solution.py:315
  49.1 6.3 %collective-permute-start.18 = (bf16[256,256]{1,0:T(8,128)(2,1)S(1)}, bf16[256,256]{1,0:T(8,128)(2,1)S(1)}, u32[]{:S(2)}, u32[]{:S(2)}) collective-permute-start(bf16[256,256]{1,0:T(8,128)(2,1)S(1)} %collective-permute-done.17.refs_0_), channel_id=1, source_target_pairs={{0,1},{1,3},{3,5},{5,7},{7,6},{6,4},{4,2},{2,0},{10,12},{12,14},{1... | collective-permute-start | bytes 393224 | tf_op jit(solution)/shard_map/ppermute | solution.py:315
  51.1 5.0 %collective-permute-start.19 = (bf16[256,256]{1,0:T(8,128)(2,1)S(1)}, bf16[256,256]{1,0:T(8,128)(2,1)S(1)}, u32[]{:S(2)}, u32[]{:S(2)}) collective-permute-start(bf16[256,256]{1,0:T(8,128)(2,1)S(1)} %collective-permute-done.14.refs_1_), channel_id=1, source_target_pairs={{0,2},{1,0},{3,1},{5,3},{7,5},{6,7},{4,6},{2,4},{10,8},{12,10},{14... | collective-permute-start | bytes 393224 | tf_op jit(solution)/shard_map/ppermute | solution.py:315
  51.2 7.8 %collective-permute-start.15 = (bf16[128,256]{1,0:T(8,128)(2,1)S(1)}, bf16[128,256]{1,0:T(8,128)(2,1)S(1)}, u32[]{:S(2)}, u32[]{:S(2)}) collective-permute-start(bf16[128,256]{1,0:T(8,128)(2,1)S(1)} %add_convert_fusion.8), channel_id=1, source_target_pairs={{0,4},{1,5},{2,6},{3,7},{4,0},{5,1},{6,2},{7,3},{8,12},{9,13},{10,... | collective-permute-start | bytes 196616 | tf_op jit(solution)/shard_map/ppermute | solution.py:315
  57.5 2.3 %collective-permute-start.22 = (bf16[512,256]{1,0:T(8,128)(2,1)S(1)}, bf16[512,256]{1,0:T(8,128)(2,1)S(1)}, u32[]{:S(2)}, u32[]{:S(2)}) collective-permute-start(bf16[512,256]{1,0:T(8,128)(2,1)S(1)} %get-tuple-element.45), channel_id=1, source_target_pairs={{0,8},{1,9},{2,10},{3,11},{4,12},{5,13},{6,14},{7,15},{8,0},{9,1},... | collective-permute-start | bytes 786440 | tf_op jit(solution)/shard_map/ppermute | solution.py:315
  59.0 5.0 %collective-permute-start.20 = (bf16[128,256]{1,0:T(8,128)(2,1)S(1)}, bf16[128,256]{1,0:T(8,128)(2,1)S(1)}, u32[]{:S(2)}, u32[]{:S(2)}) collective-permute-start(bf16[128,256]{1,0:T(8,128)(2,1)S(1)} %add_convert_fusion.7), channel_id=1, source_target_pairs={{0,16},{1,17},{2,18},{3,19},{4,20},{5,21},{6,22},{7,23},{8,24},{9,... | collective-permute-start | bytes 196616 | tf_op jit(solution)/shard_map/ppermute | solution.py:315
  59.9 6.2 %collective-permute-start.24 = (bf16[256,256]{1,0:T(8,128)(2,1)S(1)}, bf16[256,256]{1,0:T(8,128)(2,1)S(1)}, u32[]{:S(2)}, u32[]{:S(2)}) collective-permute-start(bf16[256,256]{1,0:T(8,128)(2,1)S(1)} %slice.28), channel_id=1, source_target_pairs={{0,16},{1,17},{2,18},{3,19},{4,20},{5,21},{6,22},{7,23},{8,24},{9,... | collective-permute-start | bytes 393224 | tf_op jit(solution)/shard_map/ppermute | solution.py:315
  64.1 1.3 %collective-permute-start.23 = (bf16[128,256]{1,0:T(8,128)(2,1)S(1)}, bf16[128,256]{1,0:T(8,128)(2,1)S(1)}, u32[]{:S(2)}, u32[]{:S(2)}) collective-permute-start(bf16[128,256]{1,0:T(8,128)(2,1)S(1)} %add_convert_fusion.6), channel_id=1, source_target_pairs={{0,8},{1,9},{2,10},{3,11},{4,12},{5,13},{6,14},{7,15},{8,0},{9,1},... | collective-permute-start | bytes 196616 | tf_op jit(solution)/shard_map/ppermute | solution.py:315

commit v6 on v5

--- a/solution.py
+++ b/solution.py
@@ -9,7 +9,7 @@
 
 CORES = 2
 GROUP = 4
-UNROLL = 8
+UNROLL = 4
 LANES = 128
 PACK_BITS = 8
 PACK = 1 << PACK_BITS

time: 67.3 us -> 68 us (1.010)
  Pallas kernels: 13.4 us -> 14.1 us
    pallas_call x7, Pallas kernels: 9.94 us -> 10.7 us  [tile_part(): pl.pallas_call(functools.partial(part_kernel, spec), out_shape=out_shape,...]
  transfers between devices with their start and end apart: 25 -> 25, of which waited for: 9 -> 10; matrix products, arithmetic and copies ran while one was open for 5% -> 5% of each run, Pallas kernels for 18% -> 18%
where the time goes in v6:
time: 68 us; the launch traced here: 68.1 us
  starting transfers between devices  29 us (43%)
  waiting for transfers between devices  17.3 us (25%)
  Pallas kernels  14.1 us (21%)
  matrix products  4.02 us (6%)
  other arithmetic  1.85 us (3%)
  between operations  1.64 us (2%)
    ppermute x25, starting transfers between devices, move(): return lax.ppermute(value, ('row', 'col'), pairs)  29 us
    ppermute x25, waiting for transfers between devices, move(): return lax.ppermute(value, ('row', 'col'), pairs)  17.3 us
    pallas_call x7, Pallas kernels, tile_part(): pl.pallas_call(functools.partial(part_kernel, spec), out_shape=out_shape,...  10.7 us
    pallas_call x1, Pallas kernels, load_tiles(): pl.pallas_call(functools.partial(load_kernel, sizes), out_shape=[jax.Shap...  3.41 us
    dot_general x2, matrix products, restore(): lax.dot_general(moves, values, (((0,), (0,)), ((), ())), preferred_elemen...  1.99 us
    dot_general x2, matrix products, reorder(): return jnp.dot(moves, values, preferred_element_type=F32).astype(BF16)  1.41 us
  transfers between devices with their start and end apart: 25, of which 10 were waited for; matrix products, arithmetic and copies ran while one was open for 5% of the time, Pallas kernels for 18%

profile of v6, /device:TPU:0, one launch (start us, length us, event | category | flops | bytes accessed | tf_op | source)
XLA Modules:
  0.0 68.1 jit_solution(15173920711063047108)
XLA Ops:
  0.7 1.2 %convolution_convert_fusion.4.refs_0_ = bf16[256,256]{1,0:T(8,128)(2,1)S(1)} fusion(bf16[256,256]{1,0:T(8,128)(2,1)} %param.7, s32[256]{0:T(256)S(1)} %iota_add_fusion, s32[256]{0:T(256)} %param.8), kind=kOutput, calls=%fused_computation.9 | convolution fusion | flops 33685504 | bytes 264192 | tf_op jit(solution)/shard_map/dot_general | solution.py:37
  1.9 3.0 %collective-permute-start = (bf16[256,256]{1,0:T(8,128)(2,1)S(1)}, bf16[256,256]{1,0:T(8,128)(2,1)S(1)}, u32[]{:S(2)}, u32[]{:S(2)}) collective-permute-start(bf16[256,256]{1,0:T(8,128)(2,1)S(1)} %convolution_convert_fusion.4.refs_0_), channel_id=1, source_target_pairs={{0,16},{1,17},{2,18},{3,19},{4,20},{5,21},{6,22},{7,23},{8,24},{9,... | collective-permute-start | bytes 393224 | tf_op jit(solution)/shard_map/ppermute | solution.py:315
  5.6 0.1 stack.43.here_ref
  5.6 0.7 %pad_add_fusion.facts_ref = s32[2,256]{1,0:T(2,128)S(1)} fusion(s32[1,1]{1,0:T(1,128)S(6)} %copy.10, s32[1,192]{1,0:T(1,128)} %bitcast.21), kind=kLoop, calls=%fused_computation.44 | loop fusion | flops 512 | bytes 2820 | tf_op jit(solution)/shard_map/concatenate | solution.py:165
  6.3 3.4 %shard_map.94 = (bf16[192,128,128]{2,1,0:T(8,128)(2,1)S(1)}, s32[8,384]{1,0:T(8,128)S(1)}, s32[8,384]{1,0:T(8,128)S(1)}, bf16[256,256]{1,0:T(8,128)(2,1)S(1)}) custom-call(s32[10]{0:T(128)S(1)} %stack.43.here_ref, s32[2,256]{1,0:T(2,128)S(1)} %pad_add_fusion.facts_ref, bf16[192,128,128]{2,1,0:T(8,128)(2,1)} %bitcast.20), custom_call_target="tpu_custom_call" | custom-call | bytes 6291456 | tf_op jit(solution)/shard_map/pallas_call | solution.py:167
  9.8 0.6 collective-permute-start.2
  10.4 1.0 %collective-permute-done.2.refs_3_ = bf16[256,256]{1,0:T(8,128)(2,1)S(1)} collective-permute-done((bf16[256,256]{1,0:T(8,128)(2,1)S(1)}, bf16[256,256]{1,0:T(8,128)(2,1)S(1)}, u32[]{:S(2)}, u32[]{:S(2)}) %collective-permute-start.2) | collective-permute-done | bytes 131104 | tf_op jit(solution)/shard_map/ppermute | solution.py:315
  11.3 1.5 %shard_map.95 = (bf16[256,256]{1,0:T(8,128)(2,1)S(1)}, bf16[256,256]{1,0:T(8,128)(2,1)S(1)}, bf16[256,256]{1,0:T(8,128)(2,1)S(1)}) custom-call(s32[8,384]{1,0:T(8,128)S(1)} %get-tuple-element.29.table_ref, bf16[192,128,128]{2,1,0:T(8,128)(2,1)S(1)} %get-tuple-element.26.tiles_ref, bf16[256,256]{1,0:T(8,128)(2,1)S(1)} %convolution_convert_fusion.4.refs_0_, ...), custom_call_target="tpu_custom_call" | custom-call | flops 603979776 | bytes 2359296 | tf_op jit(solution)/shard_map/pallas_call | solution.py:247
  12.9 2.0 %collective-permute-start.7 = (bf16[256,256]{1,0:T(8,128)(2,1)S(1)}, bf16[256,256]{1,0:T(8,128)(2,1)S(1)}, u32[]{:S(2)}, u32[]{:S(2)}) collective-permute-start(bf16[256,256]{1,0:T(8,128)(2,1)S(1)} %get-tuple-element.34), channel_id=1, source_target_pairs={{0,2},{1,0},{3,1},{5,3},{7,5},{6,7},{4,6},{2,4},{10,8},{12,10},{14... | collective-permute-start | bytes 393224 | tf_op jit(solution)/shard_map/ppermute | solution.py:315
  14.9 0.1 collective-permute-start.3
  15.0 4.2 %collective-permute-start.4 = (bf16[256,256]{1,0:T(8,128)(2,1)S(1)}, bf16[256,256]{1,0:T(8,128)(2,1)S(1)}, u32[]{:S(2)}, u32[]{:S(2)}) collective-permute-start(bf16[256,256]{1,0:T(8,128)(2,1)S(1)} %get-tuple-element.31), channel_id=1, source_target_pairs={{0,7},{1,6},{3,4},{5,2},{7,0},{6,1},{4,3},{2,5},{10,13},{12,11},{1... | collective-permute-start | bytes 393224 | tf_op jit(solution)/shard_map/ppermute | solution.py:315
  19.2 1.2 %shard_map.97 = (bf16[256,256]{1,0:T(8,128)(2,1)S(1)}, bf16[256,256]{1,0:T(8,128)(2,1)S(1)}) custom-call(s32[8,384]{1,0:T(8,128)S(1)} %get-tuple-element.29.table_ref, bf16[192,128,128]{2,1,0:T(8,128)(2,1)S(1)} %get-tuple-element.26.tiles_ref, bf16[256,256]{1,0:T(8,128)(2,1)S(1)} %convolution_convert_fusion.4.refs_0_, ...), custom_call_target="tpu_custom_call" | custom-call | flops 402653184 | bytes 1572864 | tf_op jit(solution)/shard_map/pallas_call | solution.py:247
  20.5 0.3 collective-permute-start.8
  20.8 1.8 %collective-permute-start.5 = (bf16[256,256]{1,0:T(8,128)(2,1)S(1)}, bf16[256,256]{1,0:T(8,128)(2,1)S(1)}, u32[]{:S(2)}, u32[]{:S(2)}) collective-permute-start(bf16[256,256]{1,0:T(8,128)(2,1)S(1)} %add_convert_fusion.5), channel_id=1, source_target_pairs={{0,1},{1,3},{3,5},{5,7},{7,6},{6,4},{4,2},{2,0},{10,12},{12,14},{1... | collective-permute-start | bytes 393224 | tf_op jit(solution)/shard_map/ppermute | solution.py:315
  22.6 1.5 %shard_map.96 = (bf16[256,256]{1,0:T(8,128)(2,1)S(1)}, bf16[256,256]{1,0:T(8,128)(2,1)S(1)}, bf16[256,256]{1,0:T(8,128)(2,1)S(1)}) custom-call(s32[8,384]{1,0:T(8,128)S(1)} %get-tuple-element.29.table_ref, bf16[192,128,128]{2,1,0:T(8,128)(2,1)S(1)} %get-tuple-element.26.tiles_ref, bf16[256,256]{1,0:T(8,128)(2,1)S(1)} %convolution_convert_fusion.4.refs_0_, ...), custom_call_target="tpu_custom_call" | custom-call | flops 603979776 | bytes 2359296 | tf_op jit(solution)/shard_map/pallas_call | solution.py:247
  24.2 3.8 %collective-permute-done.8 = bf16[256,256]{1,0:T(8,128)(2,1)S(1)} collective-permute-done((bf16[256,256]{1,0:T(8,128)(2,1)S(1)}, bf16[256,256]{1,0:T(8,128)(2,1)S(1)}, u32[]{:S(2)}, u32[]{:S(2)}) %collective-permute-start.8) | collective-permute-done | bytes 131104 | tf_op jit(solution)/shard_map/ppermute | solution.py:315
  28.1 0.4 collective-permute-start.9
  28.6 1.7 %collective-permute-start.6 = (bf16[256,256]{1,0:T(8,128)(2,1)S(1)}, bf16[256,256]{1,0:T(8,128)(2,1)S(1)}, u32[]{:S(2)}, u32[]{:S(2)}) collective-permute-start(bf16[256,256]{1,0:T(8,128)(2,1)S(1)} %add_convert_fusion.4), channel_id=1, source_target_pairs={{0,1},{1,3},{3,5},{5,7},{7,6},{6,4},{4,2},{2,0},{10,12},{12,14},{1... | collective-permute-start | bytes 393224 | tf_op jit(solution)/shard_map/ppermute | solution.py:315
  30.2 3.6 %collective-permute-done.9 = bf16[256,256]{1,0:T(8,128)(2,1)S(1)} collective-permute-done((bf16[256,256]{1,0:T(8,128)(2,1)S(1)}, bf16[256,256]{1,0:T(8,128)(2,1)S(1)}, u32[]{:S(2)}, u32[]{:S(2)}) %collective-permute-start.9) | collective-permute-done | bytes 131104 | tf_op jit(solution)/shard_map/ppermute | solution.py:315
  33.8 0.2 collective-permute-done.6
  34.0 0.1 add_convert_fusion.1
  34.1 0.2 fusion.23
  34.3 0.2 fusion.3
  34.6 0.2 fusion
  34.8 0.1 collective-permute-start.10
  34.9 0.2 convolution_convert_fusion.1.refs_0_
  35.1 2.1 %collective-permute-start.12 = (bf16[256,256]{1,0:T(8,128)(2,1)S(1)}, bf16[256,256]{1,0:T(8,128)(2,1)S(1)}, u32[]{:S(2)}, u32[]{:S(2)}) collective-permute-start(bf16[256,256]{1,0:T(8,128)(2,1)S(1)} %convolution_convert_fusion.1.refs_0_), channel_id=1, source_target_pairs={{0,2},{1,0},{3,1},{5,3},{7,5},{6,7},{4,6},{2,4},{10,8},{12,10},{14... | collective-permute-start | bytes 393224 | tf_op jit(solution)/shard_map/ppermute | solution.py:315
  37.2 1.6 %shard_map.98.refs_2_ = f32[1024,256]{1,0:T(8,128)S(1)} custom-call(s32[8,384]{1,0:T(8,128)S(1)} %get-tuple-element.37.table_ref, bf16[192,128,128]{2,1,0:T(8,128)(2,1)S(1)} %get-tuple-element.26.tiles_ref, bf16[256,256]{1,0:T(8,128)(2,1)S(1)} %convolution_convert_fusion.1.refs_0_), custom_call_target="tpu_custom_call" | custom-call | flops 402653184 | bytes 1572864 | tf_op jit(solution)/shard_map/pallas_call | solution.py:247
  38.9 2.1 %collective-permute-start.11 = (bf16[128,256]{1,0:T(8,128)(2,1)S(1)}, bf16[128,256]{1,0:T(8,128)(2,1)S(1)}, u32[]{:S(2)}, u32[]{:S(2)}) collective-permute-start(bf16[128,256]{1,0:T(8,128)(2,1)S(1)} %slice_select_fusion), channel_id=1, source_target_pairs={{0,2},{1,3},{2,0},{3,1},{4,6},{5,7},{6,4},{7,5},{8,10},{9,11},{10,... | collective-permute-start | bytes 196616 | tf_op jit(solution)/shard_map/ppermute | solution.py:315
  41.0 1.6 %collective-permute-done.16.refs_0_ = bf16[256,256]{1,0:T(8,128)(2,1)S(1)} collective-permute-done((bf16[256,256]{1,0:T(8,128)(2,1)S(1)}, bf16[256,256]{1,0:T(8,128)(2,1)S(1)}, u32[]{:S(2)}, u32[]{:S(2)}) %collective-permute-start.16) | collective-permute-done | bytes 131104 | tf_op jit(solution)/shard_map/ppermute | solution.py:315
  42.5 2.0 %collective-permute-start.14 = (bf16[256,256]{1,0:T(8,128)(2,1)S(1)}, bf16[256,256]{1,0:T(8,128)(2,1)S(1)}, u32[]{:S(2)}, u32[]{:S(2)}) collective-permute-start(bf16[256,256]{1,0:T(8,128)(2,1)S(1)} %collective-permute-done.12.refs_1_), channel_id=1, source_target_pairs={{0,2},{1,0},{3,1},{5,3},{7,5},{6,7},{4,6},{2,4},{10,8},{12,10},{14... | collective-permute-start | bytes 393224 | tf_op jit(solution)/shard_map/ppermute | solution.py:315
  44.7 2.4 %collective-permute-start.21 = (bf16[256,256]{1,0:T(8,128)(2,1)S(1)}, bf16[256,256]{1,0:T(8,128)(2,1)S(1)}, u32[]{:S(2)}, u32[]{:S(2)}) collective-permute-start(bf16[256,256]{1,0:T(8,128)(2,1)S(1)} %convolution_convert_fusion.1.refs_0_), channel_id=1, source_target_pairs={{0,7},{1,6},{3,4},{5,2},{7,0},{6,1},{4,3},{2,5},{10,13},{12,11},{1... | collective-permute-start | bytes 393224 | tf_op jit(solution)/shard_map/ppermute | solution.py:315
  47.1 1.6 %shard_map.99.refs_3_ = f32[1024,256]{1,0:T(8,128)S(1)} custom-call(s32[8,384]{1,0:T(8,128)S(1)} %get-tuple-element.37.table_ref, bf16[192,128,128]{2,1,0:T(8,128)(2,1)S(1)} %get-tuple-element.26.tiles_ref, bf16[256,256]{1,0:T(8,128)(2,1)S(1)} %collective-permute-done.16.refs_0_, bf16[256,256]{1,0:T(8,128)(2,1)S(1)} %collective-permute-done.12.refs_1_, ...), custom_call_target="tpu_custom_call" | custom-call | flops 402653184 | bytes 1572864 | tf_op jit(solution)/shard_map/pallas_call | solution.py:247
  48.7 0.2 collective-permute-done.13
  48.9 1.3 %collective-permute-start.18 = (bf16[256,256]{1,0:T(8,128)(2,1)S(1)}, bf16[256,256]{1,0:T(8,128)(2,1)S(1)}, u32[]{:S(2)}, u32[]{:S(2)}) collective-permute-start(bf16[256,256]{1,0:T(8,128)(2,1)S(1)} %collective-permute-done.17.refs_0_), channel_id=1, source_target_pairs={{0,1},{1,3},{3,5},{5,7},{7,6},{6,4},{4,2},{2,0},{10,12},{12,14},{1... | collective-permute-start | bytes 393224 | tf_op jit(solution)/shard_map/ppermute | solution.py:315
  50.2 0.7 %collective-permute-start.19 = (bf16[256,256]{1,0:T(8,128)(2,1)S(1)}, bf16[256,256]{1,0:T(8,128)(2,1)S(1)}, u32[]{:S(2)}, u32[]{:S(2)}) collective-permute-start(bf16[256,256]{1,0:T(8,128)(2,1)S(1)} %collective-permute-done.14.refs_1_), channel_id=1, source_target_pairs={{0,2},{1,0},{3,1},{5,3},{7,5},{6,7},{4,6},{2,4},{10,8},{12,10},{14... | collective-permute-start | bytes 393224 | tf_op jit(solution)/shard_map/ppermute | solution.py:315
  51.0 1.8 %collective-permute-start.15 = (bf16[128,256]{1,0:T(8,128)(2,1)S(1)}, bf16[128,256]{1,0:T(8,128)(2,1)S(1)}, u32[]{:S(2)}, u32[]{:S(2)}) collective-permute-start(bf16[128,256]{1,0:T(8,128)(2,1)S(1)} %add_convert_fusion.8), channel_id=1, source_target_pairs={{0,4},{1,5},{2,6},{3,7},{4,0},{5,1},{6,2},{7,3},{8,12},{9,13},{10,... | collective-permute-start | bytes 196616 | tf_op jit(solution)/shard_map/ppermute | solution.py:315
  52.7 1.6 %shard_map.100.refs_2_ = f32[1024,256]{1,0:T(8,128)S(1)} custom-call(s32[8,384]{1,0:T(8,128)S(1)} %get-tuple-element.37.table_ref, bf16[192,128,128]{2,1,0:T(8,128)(2,1)S(1)} %get-tuple-element.26.tiles_ref, bf16[256,256]{1,0:T(8,128)(2,1)S(1)} %collective-permute-done.17.refs_0_, bf16[256,256]{1,0:T(8,128)(2,1)S(1)} %collective-permute-done.14.refs_1_, ...), custom_call_target="tpu_custom_call" | custom-call | flops 402653184 | bytes 1572864 | tf_op jit(solution)/shard_map/pallas_call | solution.py:247
  54.4 1.4 %collective-permute-done.18.refs_0_ = bf16[256,256]{1,0:T(8,128)(2,1)S(1)} collective-permute-done((bf16[256,256]{1,0:T(8,128)(2,1)S(1)}, bf16[256,256]{1,0:T(8,128)(2,1)S(1)}, u32[]{:S(2)}, u32[]{:S(2)}) %collective-permute-start.18) | collective-permute-done | bytes 131104 | tf_op jit(solution)/shard_map/ppermute | solution.py:315
  55.8 1.6 %shard_map.101 = (bf16[512,256]{1,0:T(8,128)(2,1)S(1)}, bf16[512,256]{1,0:T(8,128)(2,1)S(1)}) custom-call(s32[8,384]{1,0:T(8,128)S(1)} %get-tuple-element.37.table_ref, bf16[192,128,128]{2,1,0:T(8,128)(2,1)S(1)} %get-tuple-element.26.tiles_ref, bf16[256,256]{1,0:T(8,128)(2,1)S(1)} %collective-permute-done.18.refs_0_, ...), custom_call_target="tpu_custom_call" | custom-call | flops 402653184 | bytes 1572864 | tf_op jit(solution)/shard_map/pallas_call | solution.py:247
  57.4 2.5 %collective-permute-done.15 = bf16[128,256]{1,0:T(8,128)(2,1)S(1)} collective-permute-done((bf16[128,256]{1,0:T(8,128)(2,1)S(1)}, bf16[128,256]{1,0:T(8,128)(2,1)S(1)}, u32[]{:S(2)}, u32[]{:S(2)}) %collective-permute-start.15) | collective-permute-done | bytes 65568 | tf_op jit(solution)/shard_map/ppermute | solution.py:315
  60.0 1.5 %collective-permute-start.20 = (bf16[128,256]{1,0:T(8,128)(2,1)S(1)}, bf16[128,256]{1,0:T(8,128)(2,1)S(1)}, u32[]{:S(2)}, u32[]{:S(2)}) collective-permute-start(bf16[128,256]{1,0:T(8,128)(2,1)S(1)} %add_convert_fusion.7), channel_id=1, source_target_pairs={{0,16},{1,17},{2,18},{3,19},{4,20},{5,21},{6,22},{7,23},{8,24},{9,... | collective-permute-start | bytes 196616 | tf_op jit(solution)/shard_map/ppermute | solution.py:315
  61.5 0.7 %collective-permute-start.24 = (bf16[256,256]{1,0:T(8,128)(2,1)S(1)}, bf16[256,256]{1,0:T(8,128)(2,1)S(1)}, u32[]{:S(2)}, u32[]{:S(2)}) collective-permute-start(bf16[256,256]{1,0:T(8,128)(2,1)S(1)} %slice.28), channel_id=1, source_target_pairs={{0,16},{1,17},{2,18},{3,19},{4,20},{5,21},{6,22},{7,23},{8,24},{9,... | collective-permute-start | bytes 393224 | tf_op jit(solution)/shard_map/ppermute | solution.py:315
  62.2 2.8 %collective-permute-done.20 = bf16[128,256]{1,0:T(8,128)(2,1)S(1)} collective-permute-done((bf16[128,256]{1,0:T(8,128)(2,1)S(1)}, bf16[128,256]{1,0:T(8,128)(2,1)S(1)}, u32[]{:S(2)}, u32[]{:S(2)}) %collective-permute-start.20) | collective-permute-done | bytes 65568 | tf_op jit(solution)/shard_map/ppermute | solution.py:315
  65.1 1.0 %convolution_convert_fusion.3 = bf16[256,256]{1,0:T(8,128)(2,1)} fusion(f32[256,256]{1,0:T(8,128)S(1)} %fusion.23, s32[256]{0:T(256)S(1)} %iota_add_fusion, s32[256]{0:T(256)S(1)} %copy-done.1), kind=kOutput, calls=%fused_computation.8 | convolution fusion | flops 33947648 | bytes 395264 | tf_op jit(solution)/shard_map/dot_general | solution.py:41
  66.1 0.2 collective-permute-done.23
  66.3 0.7 %fusion.12 = f32[256,256]{1,0:T(8,128)} fusion(bf16[128,256]{1,0:T(8,128)(2,1)S(1)} %collective-permute-done.23, bf16[128,256]{1,0:T(8,128)(2,1)S(1)} %add_convert_fusion.6, pred[]{:T(512)S(6)} %eq.67), kind=kLoop, calls=%fused_computation.29 | loop fusion | flops 655360 | bytes 393217 | tf_op jit(solution)/shard_map/convert_element_type | solution.py:400
  67.1 1.0 %convolution_convert_fusion = bf16[256,256]{1,0:T(8,128)(2,1)} fusion(f32[512,256]{1,0:T(8,128)S(1)} %convert_add_fusion, bf16[256,256]{1,0:T(8,128)(2,1)S(1)} %collective-permute-done.24, s32[256]{0:T(256)S(1)} %iota_add_fusion, s32[256]{0:T(256)S(1)} %copy-done.1), kind=kOutput, calls=%fused_computation.2 | convolution fusion | flops 33882112 | bytes 526336 | tf_op jit(solution)/shard_map/dot_general | solution.py:41
  (41 shorter events, 0.7 us)
Async XLA Ops:
  0.6 33.5 %copy-start = (bf16[256,256]{1,0:T(8,128)(2,1)S(1)}, bf16[256,256]{1,0:T(8,128)(2,1)}, u32[]{:S(2)}) copy-start(bf16[256,256]{1,0:T(8,128)(2,1)} %param.12) | copy-start | bytes 393220
  1.9 7.9 %collective-permute-start = (bf16[256,256]{1,0:T(8,128)(2,1)S(1)}, bf16[256,256]{1,0:T(8,128)(2,1)S(1)}, u32[]{:S(2)}, u32[]{:S(2)}) collective-permute-start(bf16[256,256]{1,0:T(8,128)(2,1)S(1)} %convolution_convert_fusion.4.refs_0_), channel_id=1, source_target_pairs={{0,16},{1,17},{2,18},{3,19},{4,20},{5,21},{6,22},{7,23},{8,24},{9,... | collective-permute-start | bytes 393224 | tf_op jit(solution)/shard_map/ppermute | solution.py:315
  4.9 5.5 %collective-permute-start.1 = (bf16[256,256]{1,0:T(8,128)(2,1)S(1)}, bf16[256,256]{1,0:T(8,128)(2,1)S(1)}, u32[]{:S(2)}, u32[]{:S(2)}) collective-permute-start(bf16[256,256]{1,0:T(8,128)(2,1)S(1)} %convolution_convert_fusion.4.refs_0_), channel_id=1, source_target_pairs={{0,8},{1,9},{2,10},{3,11},{4,12},{5,13},{6,14},{7,15},{8,0},{9,1},... | collective-permute-start | bytes 393224 | tf_op jit(solution)/shard_map/ppermute | solution.py:315
  9.8 1.6 %collective-permute-start.2 = (bf16[256,256]{1,0:T(8,128)(2,1)S(1)}, bf16[256,256]{1,0:T(8,128)(2,1)S(1)}, u32[]{:S(2)}, u32[]{:S(2)}) collective-permute-start(bf16[256,256]{1,0:T(8,128)(2,1)S(1)} %compare_select_fusion.2), channel_id=1, source_target_pairs={{0,8},{1,9},{2,10},{3,11},{4,12},{5,13},{6,14},{7,15},{8,0},{9,1},... | collective-permute-start | bytes 393224 | tf_op jit(solution)/shard_map/ppermute | solution.py:315
  12.9 7.5 %collective-permute-start.7 = (bf16[256,256]{1,0:T(8,128)(2,1)S(1)}, bf16[256,256]{1,0:T(8,128)(2,1)S(1)}, u32[]{:S(2)}, u32[]{:S(2)}) collective-permute-start(bf16[256,256]{1,0:T(8,128)(2,1)S(1)} %get-tuple-element.34), channel_id=1, source_target_pairs={{0,2},{1,0},{3,1},{5,3},{7,5},{6,7},{4,6},{2,4},{10,8},{12,10},{14... | collective-permute-start | bytes 393224 | tf_op jit(solution)/shard_map/ppermute | solution.py:315
  14.9 5.9 %collective-permute-start.3 = (bf16[256,256]{1,0:T(8,128)(2,1)S(1)}, bf16[256,256]{1,0:T(8,128)(2,1)S(1)}, u32[]{:S(2)}, u32[]{:S(2)}) collective-permute-start(bf16[256,256]{1,0:T(8,128)(2,1)S(1)} %get-tuple-element.28), channel_id=1, source_target_pairs={{0,1},{1,3},{3,5},{5,7},{7,6},{6,4},{4,2},{2,0},{10,12},{12,14},{1... | collective-permute-start | bytes 393224 | tf_op jit(solution)/shard_map/ppermute | solution.py:315
  15.0 15.3 %collective-permute-start.4 = (bf16[256,256]{1,0:T(8,128)(2,1)S(1)}, bf16[256,256]{1,0:T(8,128)(2,1)S(1)}, u32[]{:S(2)}, u32[]{:S(2)}) collective-permute-start(bf16[256,256]{1,0:T(8,128)(2,1)S(1)} %get-tuple-element.31), channel_id=1, source_target_pairs={{0,7},{1,6},{3,4},{5,2},{7,0},{6,1},{4,3},{2,5},{10,13},{12,11},{1... | collective-permute-start | bytes 393224 | tf_op jit(solution)/shard_map/ppermute | solution.py:315
  20.4 13.9 %copy-start.1 = (s32[256]{0:T(256)S(1)}, s32[256]{0:T(256)}, u32[]{:S(2)}) copy-start(s32[256]{0:T(256)} %param.8) | copy-start | bytes 3076
  20.4 13.9 %copy-start.2 = (bf16[256,256]{1,0:T(8,128)(2,1)S(1)}, bf16[256,256]{1,0:T(8,128)(2,1)}, u32[]{:S(2)}) copy-start(bf16[256,256]{1,0:T(8,128)(2,1)} %param.13) | copy-start | bytes 393220
  20.5 7.6 %collective-permute-start.8 = (bf16[256,256]{1,0:T(8,128)(2,1)S(1)}, bf16[256,256]{1,0:T(8,128)(2,1)S(1)}, u32[]{:S(2)}, u32[]{:S(2)}) collective-permute-start(bf16[256,256]{1,0:T(8,128)(2,1)S(1)} %add_convert_fusion.3), channel_id=1, source_target_pairs={{0,2},{1,0},{3,1},{5,3},{7,5},{6,7},{4,6},{2,4},{10,8},{12,10},{14... | collective-permute-start | bytes 393224 | tf_op jit(solution)/shard_map/ppermute | solution.py:315
  20.8 7.7 %collective-permute-start.5 = (bf16[256,256]{1,0:T(8,128)(2,1)S(1)}, bf16[256,256]{1,0:T(8,128)(2,1)S(1)}, u32[]{:S(2)}, u32[]{:S(2)}) collective-permute-start(bf16[256,256]{1,0:T(8,128)(2,1)S(1)} %add_convert_fusion.5), channel_id=1, source_target_pairs={{0,1},{1,3},{3,5},{5,7},{7,6},{6,4},{4,2},{2,0},{10,12},{12,14},{1... | collective-permute-start | bytes 393224 | tf_op jit(solution)/shard_map/ppermute | solution.py:315
  28.1 5.7 %collective-permute-start.9 = (bf16[256,256]{1,0:T(8,128)(2,1)S(1)}, bf16[256,256]{1,0:T(8,128)(2,1)S(1)}, u32[]{:S(2)}, u32[]{:S(2)}) collective-permute-start(bf16[256,256]{1,0:T(8,128)(2,1)S(1)} %add_convert_fusion.2), channel_id=1, source_target_pairs={{0,2},{1,0},{3,1},{5,3},{7,5},{6,7},{4,6},{2,4},{10,8},{12,10},{14... | collective-permute-start | bytes 393224 | tf_op jit(solution)/shard_map/ppermute | solution.py:315
  28.6 5.5 %collective-permute-start.6 = (bf16[256,256]{1,0:T(8,128)(2,1)S(1)}, bf16[256,256]{1,0:T(8,128)(2,1)S(1)}, u32[]{:S(2)}, u32[]{:S(2)}) collective-permute-start(bf16[256,256]{1,0:T(8,128)(2,1)S(1)} %add_convert_fusion.4), channel_id=1, source_target_pairs={{0,1},{1,3},{3,5},{5,7},{7,6},{6,4},{4,2},{2,0},{10,12},{12,14},{1... | collective-permute-start | bytes 393224 | tf_op jit(solution)/shard_map/ppermute | solution.py:315
  34.8 4.0 %collective-permute-start.10 = (bf16[256,256]{1,0:T(8,128)(2,1)S(1)}, bf16[256,256]{1,0:T(8,128)(2,1)S(1)}, u32[]{:S(2)}, u32[]{:S(2)}) collective-permute-start(bf16[256,256]{1,0:T(8,128)(2,1)S(1)} %fusion), channel_id=1, source_target_pairs={{0,8},{1,9},{2,10},{3,11},{4,12},{5,13},{6,14},{7,15},{8,0},{9,1},... | collective-permute-start | bytes 393224 | tf_op jit(solution)/shard_map/ppermute | solution.py:315
  35.1 7.4 %collective-permute-start.12 = (bf16[256,256]{1,0:T(8,128)(2,1)S(1)}, bf16[256,256]{1,0:T(8,128)(2,1)S(1)}, u32[]{:S(2)}, u32[]{:S(2)}) collective-permute-start(bf16[256,256]{1,0:T(8,128)(2,1)S(1)} %convolution_convert_fusion.1.refs_0_), channel_id=1, source_target_pairs={{0,2},{1,0},{3,1},{5,3},{7,5},{6,7},{4,6},{2,4},{10,8},{12,10},{14... | collective-permute-start | bytes 393224 | tf_op jit(solution)/shard_map/ppermute | solution.py:315
  37.2 5.4 %collective-permute-start.16 = (bf16[256,256]{1,0:T(8,128)(2,1)S(1)}, bf16[256,256]{1,0:T(8,128)(2,1)S(1)}, u32[]{:S(2)}, u32[]{:S(2)}) collective-permute-start(bf16[256,256]{1,0:T(8,128)(2,1)S(1)} %convolution_convert_fusion.1.refs_0_), channel_id=1, source_target_pairs={{0,1},{1,3},{3,5},{5,7},{7,6},{6,4},{4,2},{2,0},{10,12},{12,14},{1... | collective-permute-start | bytes 393224 | tf_op jit(solution)/shard_map/ppermute | solution.py:315
  38.9 5.7 %collective-permute-start.11 = (bf16[128,256]{1,0:T(8,128)(2,1)S(1)}, bf16[128,256]{1,0:T(8,128)(2,1)S(1)}, u32[]{:S(2)}, u32[]{:S(2)}) collective-permute-start(bf16[128,256]{1,0:T(8,128)(2,1)S(1)} %slice_select_fusion), channel_id=1, source_target_pairs={{0,2},{1,3},{2,0},{3,1},{4,6},{5,7},{6,4},{7,5},{8,10},{9,11},{10,... | collective-permute-start | bytes 196616 | tf_op jit(solution)/shard_map/ppermute | solution.py:315
  42.5 6.4 %collective-permute-start.17 = (bf16[256,256]{1,0:T(8,128)(2,1)S(1)}, bf16[256,256]{1,0:T(8,128)(2,1)S(1)}, u32[]{:S(2)}, u32[]{:S(2)}) collective-permute-start(bf16[256,256]{1,0:T(8,128)(2,1)S(1)} %collective-permute-done.16.refs_0_), channel_id=1, source_target_pairs={{0,1},{1,3},{3,5},{5,7},{7,6},{6,4},{4,2},{2,0},{10,12},{12,14},{1... | collective-permute-start | bytes 393224 | tf_op jit(solution)/shard_map/ppermute | solution.py:315
  42.5 6.4 %collective-permute-start.14 = (bf16[256,256]{1,0:T(8,128)(2,1)S(1)}, bf16[256,256]{1,0:T(8,128)(2,1)S(1)}, u32[]{:S(2)}, u32[]{:S(2)}) collective-permute-start(bf16[256,256]{1,0:T(8,128)(2,1)S(1)} %collective-permute-done.12.refs_1_), channel_id=1, source_target_pairs={{0,2},{1,0},{3,1},{5,3},{7,5},{6,7},{4,6},{2,4},{10,8},{12,10},{14... | collective-permute-start | bytes 393224 | tf_op jit(solution)/shard_map/ppermute | solution.py:315
  44.6 4.3 %collective-permute-start.13 = (bf16[128,256]{1,0:T(8,128)(2,1)S(1)}, bf16[128,256]{1,0:T(8,128)(2,1)S(1)}, u32[]{:S(2)}, u32[]{:S(2)}) collective-permute-start(bf16[128,256]{1,0:T(8,128)(2,1)S(1)} %add_convert_fusion.9), channel_id=1, source_target_pairs={{0,1},{1,0},{2,3},{3,2},{4,5},{5,4},{6,7},{7,6},{8,9},{9,8},{10,11... | collective-permute-start | bytes 196616 | tf_op jit(solution)/shard_map/ppermute | solution.py:315
  44.7 8.1 %collective-permute-start.21 = (bf16[256,256]{1,0:T(8,128)(2,1)S(1)}, bf16[256,256]{1,0:T(8,128)(2,1)S(1)}, u32[]{:S(2)}, u32[]{:S(2)}) collective-permute-start(bf16[256,256]{1,0:T(8,128)(2,1)S(1)} %convolution_convert_fusion.1.refs_0_), channel_id=1, source_target_pairs={{0,7},{1,6},{3,4},{5,2},{7,0},{6,1},{4,3},{2,5},{10,13},{12,11},{1... | collective-permute-start | bytes 393224 | tf_op jit(solution)/shard_map/ppermute | solution.py:315
  48.9 6.8 %collective-permute-start.18 = (bf16[256,256]{1,0:T(8,128)(2,1)S(1)}, bf16[256,256]{1,0:T(8,128)(2,1)S(1)}, u32[]{:S(2)}, u32[]{:S(2)}) collective-permute-start(bf16[256,256]{1,0:T(8,128)(2,1)S(1)} %collective-permute-done.17.refs_0_), channel_id=1, source_target_pairs={{0,1},{1,3},{3,5},{5,7},{7,6},{6,4},{4,2},{2,0},{10,12},{12,14},{1... | collective-permute-start | bytes 393224 | tf_op jit(solution)/shard_map/ppermute | solution.py:315
  50.2 5.5 %collective-permute-start.19 = (bf16[256,256]{1,0:T(8,128)(2,1)S(1)}, bf16[256,256]{1,0:T(8,128)(2,1)S(1)}, u32[]{:S(2)}, u32[]{:S(2)}) collective-permute-start(bf16[256,256]{1,0:T(8,128)(2,1)S(1)} %collective-permute-done.14.refs_1_), channel_id=1, source_target_pairs={{0,2},{1,0},{3,1},{5,3},{7,5},{6,7},{4,6},{2,4},{10,8},{12,10},{14... | collective-permute-start | bytes 393224 | tf_op jit(solution)/shard_map/ppermute | solution.py:315
  51.0 9.0 %collective-permute-start.15 = (bf16[128,256]{1,0:T(8,128)(2,1)S(1)}, bf16[128,256]{1,0:T(8,128)(2,1)S(1)}, u32[]{:S(2)}, u32[]{:S(2)}) collective-permute-start(bf16[128,256]{1,0:T(8,128)(2,1)S(1)} %add_convert_fusion.8), channel_id=1, source_target_pairs={{0,4},{1,5},{2,6},{3,7},{4,0},{5,1},{6,2},{7,3},{8,12},{9,13},{10,... | collective-permute-start | bytes 196616 | tf_op jit(solution)/shard_map/ppermute | solution.py:315
  57.4 4.1 %collective-permute-start.22 = (bf16[512,256]{1,0:T(8,128)(2,1)S(1)}, bf16[512,256]{1,0:T(8,128)(2,1)S(1)}, u32[]{:S(2)}, u32[]{:S(2)}) collective-permute-start(bf16[512,256]{1,0:T(8,128)(2,1)S(1)} %get-tuple-element.45), channel_id=1, source_target_pairs={{0,8},{1,9},{2,10},{3,11},{4,12},{5,13},{6,14},{7,15},{8,0},{9,1},... | collective-permute-start | bytes 786440 | tf_op jit(solution)/shard_map/ppermute | solution.py:315
  60.0 5.0 %collective-permute-start.20 = (bf16[128,256]{1,0:T(8,128)(2,1)S(1)}, bf16[128,256]{1,0:T(8,128)(2,1)S(1)}, u32[]{:S(2)}, u32[]{:S(2)}) collective-permute-start(bf16[128,256]{1,0:T(8,128)(2,1)S(1)} %add_convert_fusion.7), channel_id=1, source_target_pairs={{0,16},{1,17},{2,18},{3,19},{4,20},{5,21},{6,22},{7,23},{8,24},{9,... | collective-permute-start | bytes 196616 | tf_op jit(solution)/shard_map/ppermute | solution.py:315
  61.5 5.6 %collective-permute-start.24 = (bf16[256,256]{1,0:T(8,128)(2,1)S(1)}, bf16[256,256]{1,0:T(8,128)(2,1)S(1)}, u32[]{:S(2)}, u32[]{:S(2)}) collective-permute-start(bf16[256,256]{1,0:T(8,128)(2,1)S(1)} %slice.28), channel_id=1, source_target_pairs={{0,16},{1,17},{2,18},{3,19},{4,20},{5,21},{6,22},{7,23},{8,24},{9,... | collective-permute-start | bytes 393224 | tf_op jit(solution)/shard_map/ppermute | solution.py:315
  65.0 1.3 %collective-permute-start.23 = (bf16[128,256]{1,0:T(8,128)(2,1)S(1)}, bf16[128,256]{1,0:T(8,128)(2,1)S(1)}, u32[]{:S(2)}, u32[]{:S(2)}) collective-permute-start(bf16[128,256]{1,0:T(8,128)(2,1)S(1)} %add_convert_fusion.6), channel_id=1, source_target_pairs={{0,8},{1,9},{2,10},{3,11},{4,12},{5,13},{6,14},{7,15},{8,0},{9,1},... | collective-permute-start | bytes 196616 | tf_op jit(solution)/shard_map/ppermute | solution.py:315

commit v7 on v5

--- a/solution.py
+++ b/solution.py
@@ -15,7 +15,7 @@
 PACK = 1 << PACK_BITS
 VMEM_BYTES = 16 * 1024 * 1024
 LOAD_BYTES = 45 * 1024 * 1024
-LOADS = 4
+LOADS = 2
 F32 = jnp.float32
 BF16 = jnp.bfloat16
 

time: 67.3 us -> 68 us (1.010)
  transfers between devices with their start and end apart: 25 -> 25, of which waited for: 9 -> 11; matrix products, arithmetic and copies ran while one was open for 5% -> 5% of each run, Pallas kernels for 18% -> 18%
where the time goes in v7:
time: 68 us
  starting transfers between devices  28.9 us (42%)
  waiting for transfers between devices  17.5 us (26%)
  Pallas kernels  13.9 us (20%)
  matrix products  4.02 us (6%)
  other arithmetic  1.85 us (3%)
  between operations  1.65 us (2%)
    ppermute x25, starting transfers between devices, move(): return lax.ppermute(value, ('row', 'col'), pairs)  28.9 us
    ppermute x25, waiting for transfers between devices, move(): return lax.ppermute(value, ('row', 'col'), pairs)  17.5 us
    pallas_call x7, Pallas kernels, tile_part(): pl.pallas_call(functools.partial(part_kernel, spec), out_shape=out_shape,...  10.5 us
    pallas_call x1, Pallas kernels, load_tiles(): pl.pallas_call(functools.partial(load_kernel, sizes), out_shape=[jax.Shap...  3.41 us
    dot_general x2, matrix products, restore(): lax.dot_general(moves, values, (((0,), (0,)), ((), ())), preferred_elemen...  1.99 us
    dot_general x2, matrix products, reorder(): return jnp.dot(moves, values, preferred_element_type=F32).astype(BF16)  1.41 us
  transfers between devices with their start and end apart: 25, of which 11 were waited for; matrix products, arithmetic and copies ran while one was open for 5% of the time, Pallas kernels for 18%

profile of v7, /device:TPU:0, one launch (start us, length us, event | category | flops | bytes accessed | tf_op | source)
XLA Modules:
  0.0 68.0 jit_solution(1955381952882381783)
XLA Ops:
  0.7 1.2 %convolution_convert_fusion.4.refs_0_ = bf16[256,256]{1,0:T(8,128)(2,1)S(1)} fusion(bf16[256,256]{1,0:T(8,128)(2,1)} %param.7, s32[256]{0:T(256)S(1)} %iota_add_fusion, s32[256]{0:T(256)} %param.8), kind=kOutput, calls=%fused_computation.9 | convolution fusion | flops 33685504 | bytes 264192 | tf_op jit(solution)/shard_map/dot_general | solution.py:37
  1.9 3.0 %collective-permute-start = (bf16[256,256]{1,0:T(8,128)(2,1)S(1)}, bf16[256,256]{1,0:T(8,128)(2,1)S(1)}, u32[]{:S(2)}, u32[]{:S(2)}) collective-permute-start(bf16[256,256]{1,0:T(8,128)(2,1)S(1)} %convolution_convert_fusion.4.refs_0_), channel_id=1, source_target_pairs={{0,16},{1,17},{2,18},{3,19},{4,20},{5,21},{6,22},{7,23},{8,24},{9,... | collective-permute-start | bytes 393224 | tf_op jit(solution)/shard_map/ppermute | solution.py:315
  5.6 0.1 stack.43.here_ref
  5.6 0.7 %pad_add_fusion.facts_ref = s32[2,256]{1,0:T(2,128)S(1)} fusion(s32[1,1]{1,0:T(1,128)S(6)} %copy.10, s32[1,192]{1,0:T(1,128)} %bitcast.21), kind=kLoop, calls=%fused_computation.44 | loop fusion | flops 512 | bytes 2820 | tf_op jit(solution)/shard_map/concatenate | solution.py:165
  6.3 3.4 %shard_map.94 = (bf16[192,128,128]{2,1,0:T(8,128)(2,1)S(1)}, s32[8,384]{1,0:T(8,128)S(1)}, s32[8,384]{1,0:T(8,128)S(1)}, bf16[256,256]{1,0:T(8,128)(2,1)S(1)}) custom-call(s32[10]{0:T(128)S(1)} %stack.43.here_ref, s32[2,256]{1,0:T(2,128)S(1)} %pad_add_fusion.facts_ref, bf16[192,128,128]{2,1,0:T(8,128)(2,1)} %bitcast.20), custom_call_target="tpu_custom_call" | custom-call | bytes 6291456 | tf_op jit(solution)/shard_map/pallas_call | solution.py:167
  9.8 0.6 collective-permute-start.2
  10.4 1.0 %collective-permute-done.2.refs_3_ = bf16[256,256]{1,0:T(8,128)(2,1)S(1)} collective-permute-done((bf16[256,256]{1,0:T(8,128)(2,1)S(1)}, bf16[256,256]{1,0:T(8,128)(2,1)S(1)}, u32[]{:S(2)}, u32[]{:S(2)}) %collective-permute-start.2) | collective-permute-done | bytes 131104 | tf_op jit(solution)/shard_map/ppermute | solution.py:315
  11.3 1.4 %shard_map.95 = (bf16[256,256]{1,0:T(8,128)(2,1)S(1)}, bf16[256,256]{1,0:T(8,128)(2,1)S(1)}, bf16[256,256]{1,0:T(8,128)(2,1)S(1)}) custom-call(s32[8,384]{1,0:T(8,128)S(1)} %get-tuple-element.29.table_ref, bf16[192,128,128]{2,1,0:T(8,128)(2,1)S(1)} %get-tuple-element.26.tiles_ref, bf16[256,256]{1,0:T(8,128)(2,1)S(1)} %convolution_convert_fusion.4.refs_0_, ...), custom_call_target="tpu_custom_call" | custom-call | flops 603979776 | bytes 2359296 | tf_op jit(solution)/shard_map/pallas_call | solution.py:247
  12.8 1.6 %collective-permute-start.7 = (bf16[256,256]{1,0:T(8,128)(2,1)S(1)}, bf16[256,256]{1,0:T(8,128)(2,1)S(1)}, u32[]{:S(2)}, u32[]{:S(2)}) collective-permute-start(bf16[256,256]{1,0:T(8,128)(2,1)S(1)} %get-tuple-element.34), channel_id=1, source_target_pairs={{0,2},{1,0},{3,1},{5,3},{7,5},{6,7},{4,6},{2,4},{10,8},{12,10},{14... | collective-permute-start | bytes 393224 | tf_op jit(solution)/shard_map/ppermute | solution.py:315
  14.4 0.4 collective-permute-start.3
  14.8 4.6 %collective-permute-start.4 = (bf16[256,256]{1,0:T(8,128)(2,1)S(1)}, bf16[256,256]{1,0:T(8,128)(2,1)S(1)}, u32[]{:S(2)}, u32[]{:S(2)}) collective-permute-start(bf16[256,256]{1,0:T(8,128)(2,1)S(1)} %get-tuple-element.31), channel_id=1, source_target_pairs={{0,7},{1,6},{3,4},{5,2},{7,0},{6,1},{4,3},{2,5},{10,13},{12,11},{1... | collective-permute-start | bytes 393224 | tf_op jit(solution)/shard_map/ppermute | solution.py:315
  19.4 1.4 %shard_map.97 = (bf16[256,256]{1,0:T(8,128)(2,1)S(1)}, bf16[256,256]{1,0:T(8,128)(2,1)S(1)}) custom-call(s32[8,384]{1,0:T(8,128)S(1)} %get-tuple-element.29.table_ref, bf16[192,128,128]{2,1,0:T(8,128)(2,1)S(1)} %get-tuple-element.26.tiles_ref, bf16[256,256]{1,0:T(8,128)(2,1)S(1)} %convolution_convert_fusion.4.refs_0_, ...), custom_call_target="tpu_custom_call" | custom-call | flops 402653184 | bytes 1572864 | tf_op jit(solution)/shard_map/pallas_call | solution.py:247
  21.0 2.1 %collective-permute-start.5 = (bf16[256,256]{1,0:T(8,128)(2,1)S(1)}, bf16[256,256]{1,0:T(8,128)(2,1)S(1)}, u32[]{:S(2)}, u32[]{:S(2)}) collective-permute-start(bf16[256,256]{1,0:T(8,128)(2,1)S(1)} %add_convert_fusion.5), channel_id=1, source_target_pairs={{0,1},{1,3},{3,5},{5,7},{7,6},{6,4},{4,2},{2,0},{10,12},{12,14},{1... | collective-permute-start | bytes 393224 | tf_op jit(solution)/shard_map/ppermute | solution.py:315
  23.0 1.4 %shard_map.96 = (bf16[256,256]{1,0:T(8,128)(2,1)S(1)}, bf16[256,256]{1,0:T(8,128)(2,1)S(1)}, bf16[256,256]{1,0:T(8,128)(2,1)S(1)}) custom-call(s32[8,384]{1,0:T(8,128)S(1)} %get-tuple-element.29.table_ref, bf16[192,128,128]{2,1,0:T(8,128)(2,1)S(1)} %get-tuple-element.26.tiles_ref, bf16[256,256]{1,0:T(8,128)(2,1)S(1)} %convolution_convert_fusion.4.refs_0_, ...), custom_call_target="tpu_custom_call" | custom-call | flops 603979776 | bytes 2359296 | tf_op jit(solution)/shard_map/pallas_call | solution.py:247
  24.5 3.4 %collective-permute-done.8 = bf16[256,256]{1,0:T(8,128)(2,1)S(1)} collective-permute-done((bf16[256,256]{1,0:T(8,128)(2,1)S(1)}, bf16[256,256]{1,0:T(8,128)(2,1)S(1)}, u32[]{:S(2)}, u32[]{:S(2)}) %collective-permute-start.8) | collective-permute-done | bytes 131104 | tf_op jit(solution)/shard_map/ppermute | solution.py:315
  27.9 0.5 collective-permute-start.9
  28.4 1.7 %collective-permute-start.6 = (bf16[256,256]{1,0:T(8,128)(2,1)S(1)}, bf16[256,256]{1,0:T(8,128)(2,1)S(1)}, u32[]{:S(2)}, u32[]{:S(2)}) collective-permute-start(bf16[256,256]{1,0:T(8,128)(2,1)S(1)} %add_convert_fusion.4), channel_id=1, source_target_pairs={{0,1},{1,3},{3,5},{5,7},{7,6},{6,4},{4,2},{2,0},{10,12},{12,14},{1... | collective-permute-start | bytes 393224 | tf_op jit(solution)/shard_map/ppermute | solution.py:315
  30.1 3.3 %collective-permute-done.9 = bf16[256,256]{1,0:T(8,128)(2,1)S(1)} collective-permute-done((bf16[256,256]{1,0:T(8,128)(2,1)S(1)}, bf16[256,256]{1,0:T(8,128)(2,1)S(1)}, u32[]{:S(2)}, u32[]{:S(2)}) %collective-permute-start.9) | collective-permute-done | bytes 131104 | tf_op jit(solution)/shard_map/ppermute | solution.py:315
  33.4 0.5 collective-permute-done.6
  33.9 0.1 add_convert_fusion.1
  34.0 0.2 fusion.23
  34.2 0.2 fusion.3
  34.4 0.2 fusion
  34.7 0.1 collective-permute-start.10
  34.7 0.2 convolution_convert_fusion.1.refs_0_
  35.0 2.1 %collective-permute-start.12 = (bf16[256,256]{1,0:T(8,128)(2,1)S(1)}, bf16[256,256]{1,0:T(8,128)(2,1)S(1)}, u32[]{:S(2)}, u32[]{:S(2)}) collective-permute-start(bf16[256,256]{1,0:T(8,128)(2,1)S(1)} %convolution_convert_fusion.1.refs_0_), channel_id=1, source_target_pairs={{0,2},{1,0},{3,1},{5,3},{7,5},{6,7},{4,6},{2,4},{10,8},{12,10},{14... | collective-permute-start | bytes 393224 | tf_op jit(solution)/shard_map/ppermute | solution.py:315
  37.0 1.4 %shard_map.98.refs_2_ = f32[1024,256]{1,0:T(8,128)S(1)} custom-call(s32[8,384]{1,0:T(8,128)S(1)} %get-tuple-element.37.table_ref, bf16[192,128,128]{2,1,0:T(8,128)(2,1)S(1)} %get-tuple-element.26.tiles_ref, bf16[256,256]{1,0:T(8,128)(2,1)S(1)} %convolution_convert_fusion.1.refs_0_), custom_call_target="tpu_custom_call" | custom-call | flops 402653184 | bytes 1572864 | tf_op jit(solution)/shard_map/pallas_call | solution.py:247
  38.6 2.1 %collective-permute-start.11 = (bf16[128,256]{1,0:T(8,128)(2,1)S(1)}, bf16[128,256]{1,0:T(8,128)(2,1)S(1)}, u32[]{:S(2)}, u32[]{:S(2)}) collective-permute-start(bf16[128,256]{1,0:T(8,128)(2,1)S(1)} %slice_select_fusion), channel_id=1, source_target_pairs={{0,2},{1,3},{2,0},{3,1},{4,6},{5,7},{6,4},{7,5},{8,10},{9,11},{10,... | collective-permute-start | bytes 196616 | tf_op jit(solution)/shard_map/ppermute | solution.py:315
  40.7 1.9 %collective-permute-done.16.refs_0_ = bf16[256,256]{1,0:T(8,128)(2,1)S(1)} collective-permute-done((bf16[256,256]{1,0:T(8,128)(2,1)S(1)}, bf16[256,256]{1,0:T(8,128)(2,1)S(1)}, u32[]{:S(2)}, u32[]{:S(2)}) %collective-permute-start.16) | collective-permute-done | bytes 131104 | tf_op jit(solution)/shard_map/ppermute | solution.py:315
  42.5 2.0 %collective-permute-start.14 = (bf16[256,256]{1,0:T(8,128)(2,1)S(1)}, bf16[256,256]{1,0:T(8,128)(2,1)S(1)}, u32[]{:S(2)}, u32[]{:S(2)}) collective-permute-start(bf16[256,256]{1,0:T(8,128)(2,1)S(1)} %collective-permute-done.12.refs_1_), channel_id=1, source_target_pairs={{0,2},{1,0},{3,1},{5,3},{7,5},{6,7},{4,6},{2,4},{10,8},{12,10},{14... | collective-permute-start | bytes 393224 | tf_op jit(solution)/shard_map/ppermute | solution.py:315
  44.7 1.9 %collective-permute-start.21 = (bf16[256,256]{1,0:T(8,128)(2,1)S(1)}, bf16[256,256]{1,0:T(8,128)(2,1)S(1)}, u32[]{:S(2)}, u32[]{:S(2)}) collective-permute-start(bf16[256,256]{1,0:T(8,128)(2,1)S(1)} %convolution_convert_fusion.1.refs_0_), channel_id=1, source_target_pairs={{0,7},{1,6},{3,4},{5,2},{7,0},{6,1},{4,3},{2,5},{10,13},{12,11},{1... | collective-permute-start | bytes 393224 | tf_op jit(solution)/shard_map/ppermute | solution.py:315
  46.5 1.4 %shard_map.99.refs_3_ = f32[1024,256]{1,0:T(8,128)S(1)} custom-call(s32[8,384]{1,0:T(8,128)S(1)} %get-tuple-element.37.table_ref, bf16[192,128,128]{2,1,0:T(8,128)(2,1)S(1)} %get-tuple-element.26.tiles_ref, bf16[256,256]{1,0:T(8,128)(2,1)S(1)} %collective-permute-done.16.refs_0_, bf16[256,256]{1,0:T(8,128)(2,1)S(1)} %collective-permute-done.12.refs_1_, ...), custom_call_target="tpu_custom_call" | custom-call | flops 402653184 | bytes 1572864 | tf_op jit(solution)/shard_map/pallas_call | solution.py:247
  48.0 0.9 %collective-permute-done.13 = bf16[128,256]{1,0:T(8,128)(2,1)S(1)} collective-permute-done((bf16[128,256]{1,0:T(8,128)(2,1)S(1)}, bf16[128,256]{1,0:T(8,128)(2,1)S(1)}, u32[]{:S(2)}, u32[]{:S(2)}) %collective-permute-start.13) | collective-permute-done | bytes 65568 | tf_op jit(solution)/shard_map/ppermute | solution.py:315
  48.9 1.1 %collective-permute-start.18 = (bf16[256,256]{1,0:T(8,128)(2,1)S(1)}, bf16[256,256]{1,0:T(8,128)(2,1)S(1)}, u32[]{:S(2)}, u32[]{:S(2)}) collective-permute-start(bf16[256,256]{1,0:T(8,128)(2,1)S(1)} %collective-permute-done.17.refs_0_), channel_id=1, source_target_pairs={{0,1},{1,3},{3,5},{5,7},{7,6},{6,4},{4,2},{2,0},{10,12},{12,14},{1... | collective-permute-start | bytes 393224 | tf_op jit(solution)/shard_map/ppermute | solution.py:315
  50.1 0.9 %collective-permute-start.19 = (bf16[256,256]{1,0:T(8,128)(2,1)S(1)}, bf16[256,256]{1,0:T(8,128)(2,1)S(1)}, u32[]{:S(2)}, u32[]{:S(2)}) collective-permute-start(bf16[256,256]{1,0:T(8,128)(2,1)S(1)} %collective-permute-done.14.refs_1_), channel_id=1, source_target_pairs={{0,2},{1,0},{3,1},{5,3},{7,5},{6,7},{4,6},{2,4},{10,8},{12,10},{14... | collective-permute-start | bytes 393224 | tf_op jit(solution)/shard_map/ppermute | solution.py:315
  51.0 1.5 %collective-permute-start.15 = (bf16[128,256]{1,0:T(8,128)(2,1)S(1)}, bf16[128,256]{1,0:T(8,128)(2,1)S(1)}, u32[]{:S(2)}, u32[]{:S(2)}) collective-permute-start(bf16[128,256]{1,0:T(8,128)(2,1)S(1)} %add_convert_fusion.8), channel_id=1, source_target_pairs={{0,4},{1,5},{2,6},{3,7},{4,0},{5,1},{6,2},{7,3},{8,12},{9,13},{10,... | collective-permute-start | bytes 196616 | tf_op jit(solution)/shard_map/ppermute | solution.py:315
  52.5 0.5 collective-permute-done.21.refs_2_
  53.0 2.0 %shard_map.100.refs_2_ = f32[1024,256]{1,0:T(8,128)S(1)} custom-call(s32[8,384]{1,0:T(8,128)S(1)} %get-tuple-element.37.table_ref, bf16[192,128,128]{2,1,0:T(8,128)(2,1)S(1)} %get-tuple-element.26.tiles_ref, bf16[256,256]{1,0:T(8,128)(2,1)S(1)} %collective-permute-done.17.refs_0_, bf16[256,256]{1,0:T(8,128)(2,1)S(1)} %collective-permute-done.14.refs_1_, ...), custom_call_target="tpu_custom_call" | custom-call | flops 402653184 | bytes 1572864 | tf_op jit(solution)/shard_map/pallas_call | solution.py:247
  55.0 0.8 %collective-permute-done.18.refs_0_ = bf16[256,256]{1,0:T(8,128)(2,1)S(1)} collective-permute-done((bf16[256,256]{1,0:T(8,128)(2,1)S(1)}, bf16[256,256]{1,0:T(8,128)(2,1)S(1)}, u32[]{:S(2)}, u32[]{:S(2)}) %collective-permute-start.18) | collective-permute-done | bytes 131104 | tf_op jit(solution)/shard_map/ppermute | solution.py:315
  55.8 1.4 %shard_map.101 = (bf16[512,256]{1,0:T(8,128)(2,1)S(1)}, bf16[512,256]{1,0:T(8,128)(2,1)S(1)}) custom-call(s32[8,384]{1,0:T(8,128)S(1)} %get-tuple-element.37.table_ref, bf16[192,128,128]{2,1,0:T(8,128)(2,1)S(1)} %get-tuple-element.26.tiles_ref, bf16[256,256]{1,0:T(8,128)(2,1)S(1)} %collective-permute-done.18.refs_0_, ...), custom_call_target="tpu_custom_call" | custom-call | flops 402653184 | bytes 1572864 | tf_op jit(solution)/shard_map/pallas_call | solution.py:247
  57.2 0.6 collective-permute-start.22
  57.7 2.1 %collective-permute-done.15 = bf16[128,256]{1,0:T(8,128)(2,1)S(1)} collective-permute-done((bf16[128,256]{1,0:T(8,128)(2,1)S(1)}, bf16[128,256]{1,0:T(8,128)(2,1)S(1)}, u32[]{:S(2)}, u32[]{:S(2)}) %collective-permute-start.15) | collective-permute-done | bytes 65568 | tf_op jit(solution)/shard_map/ppermute | solution.py:315
  60.1 2.1 %collective-permute-start.24 = (bf16[256,256]{1,0:T(8,128)(2,1)S(1)}, bf16[256,256]{1,0:T(8,128)(2,1)S(1)}, u32[]{:S(2)}, u32[]{:S(2)}) collective-permute-start(bf16[256,256]{1,0:T(8,128)(2,1)S(1)} %slice.28), channel_id=1, source_target_pairs={{0,16},{1,17},{2,18},{3,19},{4,20},{5,21},{6,22},{7,23},{8,24},{9,... | collective-permute-start | bytes 393224 | tf_op jit(solution)/shard_map/ppermute | solution.py:315
  62.2 2.8 %collective-permute-done.20 = bf16[128,256]{1,0:T(8,128)(2,1)S(1)} collective-permute-done((bf16[128,256]{1,0:T(8,128)(2,1)S(1)}, bf16[128,256]{1,0:T(8,128)(2,1)S(1)}, u32[]{:S(2)}, u32[]{:S(2)}) %collective-permute-start.20) | collective-permute-done | bytes 65568 | tf_op jit(solution)/shard_map/ppermute | solution.py:315
  65.0 1.0 %convolution_convert_fusion.3 = bf16[256,256]{1,0:T(8,128)(2,1)} fusion(f32[256,256]{1,0:T(8,128)S(1)} %fusion.23, s32[256]{0:T(256)S(1)} %iota_add_fusion, s32[256]{0:T(256)S(1)} %copy-done.1), kind=kOutput, calls=%fused_computation.8 | convolution fusion | flops 33947648 | bytes 395264 | tf_op jit(solution)/shard_map/dot_general | solution.py:41
  66.0 0.2 collective-permute-done.23
  66.3 0.7 %fusion.12 = f32[256,256]{1,0:T(8,128)} fusion(bf16[128,256]{1,0:T(8,128)(2,1)S(1)} %collective-permute-done.23, bf16[128,256]{1,0:T(8,128)(2,1)S(1)} %add_convert_fusion.6, pred[]{:T(512)S(6)} %eq.67), kind=kLoop, calls=%fused_computation.29 | loop fusion | flops 655360 | bytes 393217 | tf_op jit(solution)/shard_map/convert_element_type | solution.py:400
  67.0 1.0 %convolution_convert_fusion = bf16[256,256]{1,0:T(8,128)(2,1)} fusion(f32[512,256]{1,0:T(8,128)S(1)} %convert_add_fusion, bf16[256,256]{1,0:T(8,128)(2,1)S(1)} %collective-permute-done.24, s32[256]{0:T(256)S(1)} %iota_add_fusion, s32[256]{0:T(256)S(1)} %copy-done.1), kind=kOutput, calls=%fused_computation.2 | convolution fusion | flops 33882112 | bytes 526336 | tf_op jit(solution)/shard_map/dot_general | solution.py:41
  (41 shorter events, 0.7 us)
Async XLA Ops:
  0.6 33.3 %copy-start = (bf16[256,256]{1,0:T(8,128)(2,1)S(1)}, bf16[256,256]{1,0:T(8,128)(2,1)}, u32[]{:S(2)}) copy-start(bf16[256,256]{1,0:T(8,128)(2,1)} %param.12) | copy-start | bytes 393220
  1.9 7.9 %collective-permute-start = (bf16[256,256]{1,0:T(8,128)(2,1)S(1)}, bf16[256,256]{1,0:T(8,128)(2,1)S(1)}, u32[]{:S(2)}, u32[]{:S(2)}) collective-permute-start(bf16[256,256]{1,0:T(8,128)(2,1)S(1)} %convolution_convert_fusion.4.refs_0_), channel_id=1, source_target_pairs={{0,16},{1,17},{2,18},{3,19},{4,20},{5,21},{6,22},{7,23},{8,24},{9,... | collective-permute-start | bytes 393224 | tf_op jit(solution)/shard_map/ppermute | solution.py:315
  4.9 5.5 %collective-permute-start.1 = (bf16[256,256]{1,0:T(8,128)(2,1)S(1)}, bf16[256,256]{1,0:T(8,128)(2,1)S(1)}, u32[]{:S(2)}, u32[]{:S(2)}) collective-permute-start(bf16[256,256]{1,0:T(8,128)(2,1)S(1)} %convolution_convert_fusion.4.refs_0_), channel_id=1, source_target_pairs={{0,8},{1,9},{2,10},{3,11},{4,12},{5,13},{6,14},{7,15},{8,0},{9,1},... | collective-permute-start | bytes 393224 | tf_op jit(solution)/shard_map/ppermute | solution.py:315
  9.8 1.6 %collective-permute-start.2 = (bf16[256,256]{1,0:T(8,128)(2,1)S(1)}, bf16[256,256]{1,0:T(8,128)(2,1)S(1)}, u32[]{:S(2)}, u32[]{:S(2)}) collective-permute-start(bf16[256,256]{1,0:T(8,128)(2,1)S(1)} %compare_select_fusion.2), channel_id=1, source_target_pairs={{0,8},{1,9},{2,10},{3,11},{4,12},{5,13},{6,14},{7,15},{8,0},{9,1},... | collective-permute-start | bytes 393224 | tf_op jit(solution)/shard_map/ppermute | solution.py:315
  12.8 8.1 %collective-permute-start.7 = (bf16[256,256]{1,0:T(8,128)(2,1)S(1)}, bf16[256,256]{1,0:T(8,128)(2,1)S(1)}, u32[]{:S(2)}, u32[]{:S(2)}) collective-permute-start(bf16[256,256]{1,0:T(8,128)(2,1)S(1)} %get-tuple-element.34), channel_id=1, source_target_pairs={{0,2},{1,0},{3,1},{5,3},{7,5},{6,7},{4,6},{2,4},{10,8},{12,10},{14... | collective-permute-start | bytes 393224 | tf_op jit(solution)/shard_map/ppermute | solution.py:315
  14.4 6.5 %collective-permute-start.3 = (bf16[256,256]{1,0:T(8,128)(2,1)S(1)}, bf16[256,256]{1,0:T(8,128)(2,1)S(1)}, u32[]{:S(2)}, u32[]{:S(2)}) collective-permute-start(bf16[256,256]{1,0:T(8,128)(2,1)S(1)} %get-tuple-element.28), channel_id=1, source_target_pairs={{0,1},{1,3},{3,5},{5,7},{7,6},{6,4},{4,2},{2,0},{10,12},{12,14},{1... | collective-permute-start | bytes 393224 | tf_op jit(solution)/shard_map/ppermute | solution.py:315
  14.8 15.3 %collective-permute-start.4 = (bf16[256,256]{1,0:T(8,128)(2,1)S(1)}, bf16[256,256]{1,0:T(8,128)(2,1)S(1)}, u32[]{:S(2)}, u32[]{:S(2)}) collective-permute-start(bf16[256,256]{1,0:T(8,128)(2,1)S(1)} %get-tuple-element.31), channel_id=1, source_target_pairs={{0,7},{1,6},{3,4},{5,2},{7,0},{6,1},{4,3},{2,5},{10,13},{12,11},{1... | collective-permute-start | bytes 393224 | tf_op jit(solution)/shard_map/ppermute | solution.py:315
  20.8 13.4 %copy-start.1 = (s32[256]{0:T(256)S(1)}, s32[256]{0:T(256)}, u32[]{:S(2)}) copy-start(s32[256]{0:T(256)} %param.8) | copy-start | bytes 3076
  20.8 13.4 %copy-start.2 = (bf16[256,256]{1,0:T(8,128)(2,1)S(1)}, bf16[256,256]{1,0:T(8,128)(2,1)}, u32[]{:S(2)}) copy-start(bf16[256,256]{1,0:T(8,128)(2,1)} %param.13) | copy-start | bytes 393220
  20.9 7.0 %collective-permute-start.8 = (bf16[256,256]{1,0:T(8,128)(2,1)S(1)}, bf16[256,256]{1,0:T(8,128)(2,1)S(1)}, u32[]{:S(2)}, u32[]{:S(2)}) collective-permute-start(bf16[256,256]{1,0:T(8,128)(2,1)S(1)} %add_convert_fusion.3), channel_id=1, source_target_pairs={{0,2},{1,0},{3,1},{5,3},{7,5},{6,7},{4,6},{2,4},{10,8},{12,10},{14... | collective-permute-start | bytes 393224 | tf_op jit(solution)/shard_map/ppermute | solution.py:315
  21.0 7.4 %collective-permute-start.5 = (bf16[256,256]{1,0:T(8,128)(2,1)S(1)}, bf16[256,256]{1,0:T(8,128)(2,1)S(1)}, u32[]{:S(2)}, u32[]{:S(2)}) collective-permute-start(bf16[256,256]{1,0:T(8,128)(2,1)S(1)} %add_convert_fusion.5), channel_id=1, source_target_pairs={{0,1},{1,3},{3,5},{5,7},{7,6},{6,4},{4,2},{2,0},{10,12},{12,14},{1... | collective-permute-start | bytes 393224 | tf_op jit(solution)/shard_map/ppermute | solution.py:315
  27.9 5.5 %collective-permute-start.9 = (bf16[256,256]{1,0:T(8,128)(2,1)S(1)}, bf16[256,256]{1,0:T(8,128)(2,1)S(1)}, u32[]{:S(2)}, u32[]{:S(2)}) collective-permute-start(bf16[256,256]{1,0:T(8,128)(2,1)S(1)} %add_convert_fusion.2), channel_id=1, source_target_pairs={{0,2},{1,0},{3,1},{5,3},{7,5},{6,7},{4,6},{2,4},{10,8},{12,10},{14... | collective-permute-start | bytes 393224 | tf_op jit(solution)/shard_map/ppermute | solution.py:315
  28.4 5.5 %collective-permute-start.6 = (bf16[256,256]{1,0:T(8,128)(2,1)S(1)}, bf16[256,256]{1,0:T(8,128)(2,1)S(1)}, u32[]{:S(2)}, u32[]{:S(2)}) collective-permute-start(bf16[256,256]{1,0:T(8,128)(2,1)S(1)} %add_convert_fusion.4), channel_id=1, source_target_pairs={{0,1},{1,3},{3,5},{5,7},{7,6},{6,4},{4,2},{2,0},{10,12},{12,14},{1... | collective-permute-start | bytes 393224 | tf_op jit(solution)/shard_map/ppermute | solution.py:315
  34.7 3.8 %collective-permute-start.10 = (bf16[256,256]{1,0:T(8,128)(2,1)S(1)}, bf16[256,256]{1,0:T(8,128)(2,1)S(1)}, u32[]{:S(2)}, u32[]{:S(2)}) collective-permute-start(bf16[256,256]{1,0:T(8,128)(2,1)S(1)} %fusion), channel_id=1, source_target_pairs={{0,8},{1,9},{2,10},{3,11},{4,12},{5,13},{6,14},{7,15},{8,0},{9,1},... | collective-permute-start | bytes 393224 | tf_op jit(solution)/shard_map/ppermute | solution.py:315
  35.0 7.6 %collective-permute-start.12 = (bf16[256,256]{1,0:T(8,128)(2,1)S(1)}, bf16[256,256]{1,0:T(8,128)(2,1)S(1)}, u32[]{:S(2)}, u32[]{:S(2)}) collective-permute-start(bf16[256,256]{1,0:T(8,128)(2,1)S(1)} %convolution_convert_fusion.1.refs_0_), channel_id=1, source_target_pairs={{0,2},{1,0},{3,1},{5,3},{7,5},{6,7},{4,6},{2,4},{10,8},{12,10},{14... | collective-permute-start | bytes 393224 | tf_op jit(solution)/shard_map/ppermute | solution.py:315
  37.0 5.5 %collective-permute-start.16 = (bf16[256,256]{1,0:T(8,128)(2,1)S(1)}, bf16[256,256]{1,0:T(8,128)(2,1)S(1)}, u32[]{:S(2)}, u32[]{:S(2)}) collective-permute-start(bf16[256,256]{1,0:T(8,128)(2,1)S(1)} %convolution_convert_fusion.1.refs_0_), channel_id=1, source_target_pairs={{0,1},{1,3},{3,5},{5,7},{7,6},{6,4},{4,2},{2,0},{10,12},{12,14},{1... | collective-permute-start | bytes 393224 | tf_op jit(solution)/shard_map/ppermute | solution.py:315
  38.6 6.0 %collective-permute-start.11 = (bf16[128,256]{1,0:T(8,128)(2,1)S(1)}, bf16[128,256]{1,0:T(8,128)(2,1)S(1)}, u32[]{:S(2)}, u32[]{:S(2)}) collective-permute-start(bf16[128,256]{1,0:T(8,128)(2,1)S(1)} %slice_select_fusion), channel_id=1, source_target_pairs={{0,2},{1,3},{2,0},{3,1},{4,6},{5,7},{6,4},{7,5},{8,10},{9,11},{10,... | collective-permute-start | bytes 196616 | tf_op jit(solution)/shard_map/ppermute | solution.py:315
  42.5 6.4 %collective-permute-start.17 = (bf16[256,256]{1,0:T(8,128)(2,1)S(1)}, bf16[256,256]{1,0:T(8,128)(2,1)S(1)}, u32[]{:S(2)}, u32[]{:S(2)}) collective-permute-start(bf16[256,256]{1,0:T(8,128)(2,1)S(1)} %collective-permute-done.16.refs_0_), channel_id=1, source_target_pairs={{0,1},{1,3},{3,5},{5,7},{7,6},{6,4},{4,2},{2,0},{10,12},{12,14},{1... | collective-permute-start | bytes 393224 | tf_op jit(solution)/shard_map/ppermute | solution.py:315
  42.5 6.4 %collective-permute-start.14 = (bf16[256,256]{1,0:T(8,128)(2,1)S(1)}, bf16[256,256]{1,0:T(8,128)(2,1)S(1)}, u32[]{:S(2)}, u32[]{:S(2)}) collective-permute-start(bf16[256,256]{1,0:T(8,128)(2,1)S(1)} %collective-permute-done.12.refs_1_), channel_id=1, source_target_pairs={{0,2},{1,0},{3,1},{5,3},{7,5},{6,7},{4,6},{2,4},{10,8},{12,10},{14... | collective-permute-start | bytes 393224 | tf_op jit(solution)/shard_map/ppermute | solution.py:315
  44.6 4.3 %collective-permute-start.13 = (bf16[128,256]{1,0:T(8,128)(2,1)S(1)}, bf16[128,256]{1,0:T(8,128)(2,1)S(1)}, u32[]{:S(2)}, u32[]{:S(2)}) collective-permute-start(bf16[128,256]{1,0:T(8,128)(2,1)S(1)} %add_convert_fusion.9), channel_id=1, source_target_pairs={{0,1},{1,0},{2,3},{3,2},{4,5},{5,4},{6,7},{7,6},{8,9},{9,8},{10,11... | collective-permute-start | bytes 196616 | tf_op jit(solution)/shard_map/ppermute | solution.py:315
  44.7 8.3 %collective-permute-start.21 = (bf16[256,256]{1,0:T(8,128)(2,1)S(1)}, bf16[256,256]{1,0:T(8,128)(2,1)S(1)}, u32[]{:S(2)}, u32[]{:S(2)}) collective-permute-start(bf16[256,256]{1,0:T(8,128)(2,1)S(1)} %convolution_convert_fusion.1.refs_0_), channel_id=1, source_target_pairs={{0,7},{1,6},{3,4},{5,2},{7,0},{6,1},{4,3},{2,5},{10,13},{12,11},{1... | collective-permute-start | bytes 393224 | tf_op jit(solution)/shard_map/ppermute | solution.py:315
  48.9 6.8 %collective-permute-start.18 = (bf16[256,256]{1,0:T(8,128)(2,1)S(1)}, bf16[256,256]{1,0:T(8,128)(2,1)S(1)}, u32[]{:S(2)}, u32[]{:S(2)}) collective-permute-start(bf16[256,256]{1,0:T(8,128)(2,1)S(1)} %collective-permute-done.17.refs_0_), channel_id=1, source_target_pairs={{0,1},{1,3},{3,5},{5,7},{7,6},{6,4},{4,2},{2,0},{10,12},{12,14},{1... | collective-permute-start | bytes 393224 | tf_op jit(solution)/shard_map/ppermute | solution.py:315
  50.1 5.7 %collective-permute-start.19 = (bf16[256,256]{1,0:T(8,128)(2,1)S(1)}, bf16[256,256]{1,0:T(8,128)(2,1)S(1)}, u32[]{:S(2)}, u32[]{:S(2)}) collective-permute-start(bf16[256,256]{1,0:T(8,128)(2,1)S(1)} %collective-permute-done.14.refs_1_), channel_id=1, source_target_pairs={{0,2},{1,0},{3,1},{5,3},{7,5},{6,7},{4,6},{2,4},{10,8},{12,10},{14... | collective-permute-start | bytes 393224 | tf_op jit(solution)/shard_map/ppermute | solution.py:315
  51.0 8.9 %collective-permute-start.15 = (bf16[128,256]{1,0:T(8,128)(2,1)S(1)}, bf16[128,256]{1,0:T(8,128)(2,1)S(1)}, u32[]{:S(2)}, u32[]{:S(2)}) collective-permute-start(bf16[128,256]{1,0:T(8,128)(2,1)S(1)} %add_convert_fusion.8), channel_id=1, source_target_pairs={{0,4},{1,5},{2,6},{3,7},{4,0},{5,1},{6,2},{7,3},{8,12},{9,13},{10,... | collective-permute-start | bytes 196616 | tf_op jit(solution)/shard_map/ppermute | solution.py:315
  57.2 2.8 %collective-permute-start.22 = (bf16[512,256]{1,0:T(8,128)(2,1)S(1)}, bf16[512,256]{1,0:T(8,128)(2,1)S(1)}, u32[]{:S(2)}, u32[]{:S(2)}) collective-permute-start(bf16[512,256]{1,0:T(8,128)(2,1)S(1)} %get-tuple-element.45), channel_id=1, source_target_pairs={{0,8},{1,9},{2,10},{3,11},{4,12},{5,13},{6,14},{7,15},{8,0},{9,1},... | collective-permute-start | bytes 786440 | tf_op jit(solution)/shard_map/ppermute | solution.py:315
  59.9 5.0 %collective-permute-start.20 = (bf16[128,256]{1,0:T(8,128)(2,1)S(1)}, bf16[128,256]{1,0:T(8,128)(2,1)S(1)}, u32[]{:S(2)}, u32[]{:S(2)}) collective-permute-start(bf16[128,256]{1,0:T(8,128)(2,1)S(1)} %add_convert_fusion.7), channel_id=1, source_target_pairs={{0,16},{1,17},{2,18},{3,19},{4,20},{5,21},{6,22},{7,23},{8,24},{9,... | collective-permute-start | bytes 196616 | tf_op jit(solution)/shard_map/ppermute | solution.py:315
  60.1 6.9 %collective-permute-start.24 = (bf16[256,256]{1,0:T(8,128)(2,1)S(1)}, bf16[256,256]{1,0:T(8,128)(2,1)S(1)}, u32[]{:S(2)}, u32[]{:S(2)}) collective-permute-start(bf16[256,256]{1,0:T(8,128)(2,1)S(1)} %slice.28), channel_id=1, source_target_pairs={{0,16},{1,17},{2,18},{3,19},{4,20},{5,21},{6,22},{7,23},{8,24},{9,... | collective-permute-start | bytes 393224 | tf_op jit(solution)/shard_map/ppermute | solution.py:315
  65.0 1.3 %collective-permute-start.23 = (bf16[128,256]{1,0:T(8,128)(2,1)S(1)}, bf16[128,256]{1,0:T(8,128)(2,1)S(1)}, u32[]{:S(2)}, u32[]{:S(2)}) collective-permute-start(bf16[128,256]{1,0:T(8,128)(2,1)S(1)} %add_convert_fusion.6), channel_id=1, source_target_pairs={{0,8},{1,9},{2,10},{3,11},{4,12},{5,13},{6,14},{7,15},{8,0},{9,1},... | collective-permute-start | bytes 196616 | tf_op jit(solution)/shard_map/ppermute | solution.py:315
